TPU v7x, 512 devices: a whole 4x8x8 slice. The times are simulated.
512 devices in a mesh: ctx: 256 (over z, x, y), mp: 2 (over core).
Axes of the slice: x: 4, y: 8, z: 8, core: 2. Of those that a mesh axis runs over, the one named last changes fastest.
Arguments:
- queries: bfloat16 [32768, 2048], P('ctx', 'mp'), may hold values from -4.5 to 4.5
- keys: bfloat16 [32768, 512], P('ctx', 'mp'), may hold values from -6 to 6
- values: bfloat16 [32768, 512], P('ctx', 'mp'), may hold values from -6 to 6
- lengths: int32 [256], P('ctx'), may hold values from 16 to 128, as said below
- fire_w1: float32 [32], replicated, may hold values from -8 to 8
- fire_b1: float32 [32], replicated, may hold values from -1 to 1
- fire_w2: float32 [32, 16], replicated, may hold values from -1 to 1
- grad_out: bfloat16 [32768, 2048], P('ctx', 'mp'), may hold values from -6 to 6
Outputs:
- attended: bfloat16 [32768, 2048], P('ctx', 'mp')
- grad_q: bfloat16 [32768, 2048], P('ctx', 'mp')
- grad_k: bfloat16 [32768, 512], P('ctx', 'mp')
- grad_v: bfloat16 [32768, 512], P('ctx', 'mp')
- grad_w1: float32 [32], replicated
- grad_b1: float32 [32], replicated
- grad_w2: float32 [32, 16], replicated
Inputs may be any that keep to these rules, and one draw needn't show every extreme that they name: Tokens at offsets lengths[b] and beyond in block b are padding; some block is full.
All inputs are finite; a program needn't handle non-finite values.
Results may differ from a plain program's by a relative error of at most 0.014.
Values sent between devices are 32-bit elements; how exact they have to be, the bound alone decides.
No kernel may reach another device: no remote copies, remote signals or barrier semaphores. Data moves between devices by JAX's collectives and lax.ppermute only.
A program may use at most 64 MiB of HBM per device.

v0:
```python
import jax
import jax.numpy as jnp
from jax import lax
from jax.sharding import PartitionSpec as P

HEAD_SIZE = 128
COARSE = 32


def swapped(value, axis, stride):
    mask = 2**stride
    pairs = [(source, source ^ mask) for source in range(lax.axis_size(axis))]
    return lax.ppermute(value, axis, pairs)


def merge_pair(own_part, got_part, upper_half):
    first = jnp.where(upper_half, got_part, own_part)
    second = jnp.where(upper_half, own_part, got_part)
    joined = jnp.concatenate([first, second], 0)
    return joined.reshape((COARSE, 2) + own_part.shape[1:]).sum(1)


def shards(queries, keys, values, lengths, fire_w1, fire_b1, fire_w2, grad_out):
    tok_rows = queries.shape[0]
    kv_width = keys.shape[1]
    q_heads = queries.shape[1] // HEAD_SIZE
    kv_heads = kv_width // HEAD_SIZE
    group_size = q_heads // kv_heads
    score_scale = HEAD_SIZE ** (-0.5)
    ctx_count = lax.axis_size("ctx")
    level_count = ctx_count.bit_length() - 1
    ctx_index = lax.axis_index("ctx")
    mp_index = lax.axis_index("mp")
    run_length = tok_rows // COARSE
    token_live = (jnp.arange(tok_rows) < lengths[0]).astype(jnp.float32)
    key_f = keys.astype(jnp.float32) * token_live[:, None]
    value_f = values.astype(jnp.float32) * token_live[:, None]
    own_keys = key_f.reshape(COARSE, run_length, kv_width).sum(1)
    own_values = value_f.reshape(COARSE, run_length, kv_width).sum(1)
    own_counts = token_live.reshape(COARSE, run_length).sum(1)
    sib_keys, sib_values, sib_counts = ([], [], [])
    for height in range(level_count):
        got_keys, got_values, got_counts = swapped(
            (own_keys, own_values, own_counts), "ctx", height
        )
        sib_keys.append(got_keys)
        sib_values.append(got_values)
        sib_counts.append(got_counts)
        if height + 1 < level_count:
            upper_half = ctx_index >> height & 1 == 1
            own_keys = merge_pair(own_keys, got_keys, upper_half)
            own_values = merge_pair(own_values, got_values, upper_half)
            own_counts = merge_pair(own_counts, got_counts, upper_half)
    sib_pos = []
    for height in range(level_count):
        level_run = 2**height * tok_rows // COARSE
        start = ((ctx_index >> height ^ 1) * 2**height * tok_rows).astype(jnp.float32)
        inside = (jnp.arange(COARSE) * level_run).astype(jnp.float32) + (level_run - 1) / 2.0
        sib_pos.append(start + inside)
    coarse_sum_k = jnp.concatenate(sib_keys, 0)
    coarse_sum_v = jnp.concatenate(sib_values, 0)
    coarse_count = jnp.concatenate(sib_counts, 0)
    safe_count = jnp.maximum(coarse_count, 1.0)
    mean_keys = (coarse_sum_k / safe_count[:, None]).astype(jnp.bfloat16)
    mean_values = (coarse_sum_v / safe_count[:, None]).astype(jnp.bfloat16)
    keys_all = jnp.concatenate([keys, mean_keys], 0).reshape(-1, kv_heads, HEAD_SIZE)
    values_all = jnp.concatenate([values, mean_values], 0).reshape(-1, kv_heads, HEAD_SIZE)
    key_live = jnp.concatenate([token_live > 0, coarse_count > 0])
    query_pos = (ctx_index * tok_rows + jnp.arange(tok_rows)).astype(jnp.float32)
    key_pos = jnp.concatenate([query_pos] + sib_pos)
    seq_total = jnp.asarray(ctx_count * tok_rows, dtype=jnp.float32)
    phase = jnp.log1p(jnp.abs(query_pos[:, None] - key_pos[None, :])) / jnp.log1p(seq_total)
    hidden = jax.nn.relu(phase[:, :, None] * fire_w1 + fire_b1)
    w2_local = lax.dynamic_slice_in_dim(fire_w2, mp_index * q_heads, q_heads, 1)
    fire_bias = jnp.einsum("tkm,mh->htk", hidden, w2_local, precision=lax.Precision.HIGHEST)
    query_grid = queries.reshape(tok_rows, kv_heads, group_size, HEAD_SIZE)
    raw_scores = jnp.einsum(
        "tjgd,kjd->jgtk", query_grid, keys_all, preferred_element_type=jnp.float32
    )
    scores = raw_scores.reshape(q_heads, tok_rows, -1) * score_scale + fire_bias
    scores = jnp.where(key_live[None, None, :], scores, -jnp.inf)
    top_score = jnp.max(scores, axis=-1, keepdims=True)
    weights = jnp.exp(scores - top_score)
    probs = weights / jnp.sum(weights, axis=-1, keepdims=True)
    probs_b = probs.astype(jnp.bfloat16).reshape(kv_heads, group_size, tok_rows, -1)
    output = jnp.einsum(
        "jgtk,kjd->tjgd", probs_b, values_all, preferred_element_type=jnp.float32
    ).reshape(tok_rows, -1)
    attended = (output * token_live[:, None]).astype(jnp.bfloat16)
    masked_grad = jnp.where(token_live[:, None] > 0, grad_out, jnp.zeros_like(grad_out))
    grad_grid = masked_grad.reshape(tok_rows, kv_heads, group_size, HEAD_SIZE)
    dprobs = jnp.einsum(
        "tjgd,kjd->jgtk", grad_grid, values_all, preferred_element_type=jnp.float32
    ).reshape(q_heads, tok_rows, -1)
    dscores = probs * (dprobs - jnp.sum(probs * dprobs, axis=-1, keepdims=True))
    dscores_b = dscores.astype(jnp.bfloat16).reshape(kv_heads, group_size, tok_rows, -1)
    grad_query = score_scale * jnp.einsum(
        "jgtk,kjd->tjgd", dscores_b, keys_all, preferred_element_type=jnp.float32
    )
    grad_q = grad_query.reshape(tok_rows, -1).astype(jnp.bfloat16)
    key_grads = score_scale * jnp.einsum(
        "jgtk,tjgd->kjd", dscores_b, query_grid, preferred_element_type=jnp.float32
    )
    key_grads = key_grads.reshape(-1, kv_width)
    value_grads = jnp.einsum(
        "jgtk,tjgd->kjd", probs_b, grad_grid, preferred_element_type=jnp.float32
    ).reshape(-1, kv_width)
    coarse_gk = key_grads[tok_rows:] / safe_count[:, None]
    coarse_gv = value_grads[tok_rows:] / safe_count[:, None]
    token_gk = key_grads[:tok_rows]
    token_gv = value_grads[:tok_rows]
    back_keys = jnp.zeros((COARSE, kv_width), jnp.float32)
    back_values = jnp.zeros((COARSE, kv_width), jnp.float32)
    for height in reversed(range(level_count)):
        send_keys = coarse_gk[height * COARSE : (height + 1) * COARSE]
        send_values = coarse_gv[height * COARSE : (height + 1) * COARSE]
        keep_keys = jnp.zeros((COARSE, kv_width), jnp.float32)
        keep_values = jnp.zeros((COARSE, kv_width), jnp.float32)
        if height + 1 < level_count:
            upper_half = ctx_index >> height & 1 == 1
            lower_keys = jnp.repeat(back_keys[: COARSE // 2], 2, axis=0)
            higher_keys = jnp.repeat(back_keys[COARSE // 2 :], 2, axis=0)
            lower_values = jnp.repeat(back_values[: COARSE // 2], 2, axis=0)
            higher_values = jnp.repeat(back_values[COARSE // 2 :], 2, axis=0)
            keep_keys = jnp.where(upper_half, higher_keys, lower_keys)
            keep_values = jnp.where(upper_half, higher_values, lower_values)
            send_keys = send_keys + jnp.where(upper_half, lower_keys, higher_keys)
            send_values = send_values + jnp.where(upper_half, lower_values, higher_values)
        came_keys, came_values = swapped((send_keys, send_values), "ctx", height)
        back_keys = keep_keys + came_keys
        back_values = keep_values + came_values
    token_gk = token_gk + jnp.repeat(back_keys, run_length, axis=0)
    token_gv = token_gv + jnp.repeat(back_values, run_length, axis=0)
    grad_k = (token_gk * token_live[:, None]).astype(jnp.bfloat16)
    grad_v = (token_gv * token_live[:, None]).astype(jnp.bfloat16)
    w2_term = jnp.einsum("htk,tkm->mh", dscores, hidden, precision=lax.Precision.HIGHEST)
    active = (hidden > 0).astype(jnp.float32)
    plain_sum = jnp.einsum("htk,tkm->hm", dscores, active, precision=lax.Precision.HIGHEST)
    phase_sum = jnp.einsum(
        "htk,tkm->hm", dscores * phase[None], active, precision=lax.Precision.HIGHEST
    )
    b1_term = jnp.sum(w2_local * plain_sum.T, axis=1)
    w1_term = jnp.sum(w2_local * phase_sum.T, axis=1)
    w2_full = lax.dynamic_update_slice_in_dim(
        jnp.zeros(fire_w2.shape, jnp.float32), w2_term, mp_index * q_heads, 1
    )
    grad_w1, grad_b1, grad_w2 = lax.psum((w1_term, b1_term, w2_full), ("ctx", "mp"))
    return (attended, grad_q, grad_k, grad_v, grad_w1, grad_b1, grad_w2)


def solution(mesh):
    placed = (
        P("ctx", "mp"),
        P("ctx", "mp"),
        P("ctx", "mp"),
        P("ctx"),
        P(),
        P(),
        P(),
        P("ctx", "mp"),
    )
    return jax.shard_map(
        shards,
        mesh=mesh,
        in_specs=placed,
        out_specs=(P("ctx", "mp"), P("ctx", "mp"), P("ctx", "mp"), P("ctx", "mp"), P(), P(), P()),
        check_vma=False,
    )
```

profile of v0, /device:TPU:1, one launch (start us, length us, event | category | flops | bytes accessed | tf_op | source)
XLA Modules:
  0.0 355.3 jit_solution(8799155123252933738)
XLA Ops:
  2.4 4.0 %collective-permute-start = (f32[32,256]{1,0:T(8,128)S(1)}, f32[32,256]{1,0:T(8,128)S(1)}, u32[]{:S(2)}, u32[]{:S(2)}) collective-permute-start(f32[32,256]{1,0:T(8,128)S(1)} %reduce_sum.252), channel_id=1, source_target_pairs={{0,2},{2,0},{4,6},{6,4},{8,10},{10,8},{12,14},{14,12},{16,18},{18,... | collective-permute-start | bytes 98312 | tf_op jit(solution)/shard_map/ppermute | solution.py:13
  8.5 3.4 collective-permute-start.16
  12.5 3.7 %fusion.2 = f32[128,384,32]{0,2,1:T(8,128)} fusion(f32[32]{0:T(128)S(1)} %copy-done.19, f32[32]{0:T(128)S(1)} %copy-done.21, f32[128,384]{0,1:T(8,128)S(1)} %copy.192), kind=kLoop, calls=%fused_computation.3 | loop fusion | flops 4718592 | bytes 6488320 | tf_op jit(solution)/shard_map/jit(relu)/max | solution.py:73
  16.2 6.7 %copy.193 = f32[128,384,32]{1,2,0:T(8,128)} copy(f32[128,384,32]{0,2,1:T(8,128)} %fusion.2) | data formatting | bytes 12582912 | tf_op jit(solution)/shard_map/jit(relu)/max | solution.py:73
  23.1 5.1 %fusion.47 = f32[8,128,384]{2,0,1:T(8,128)S(1)} fusion(f32[128,384,32]{1,2,0:T(8,128)} %copy.193, f32[32,16]{0,1:T(8,128)S(1)} %copy-done.17, s32[]{:T(128)S(6)} %select_n.506), kind=kOutput, calls=%fused_computation.151 | convolution fusion | flops 150994944 | bytes 7868420 | tf_op jit(solution)/shard_map/tkm,mh->htk/dot_general | solution.py:75
  28.7 4.2 %collective-permute-start.9 = (f32[32]{0:T(128)S(1)}, f32[32]{0:T(128)S(1)}, u32[]{:S(2)}, u32[]{:S(2)}) collective-permute-start(f32[32]{0:T(128)S(1)} %maximum_reduce_fusion), channel_id=1, source_target_pairs={{0,4},{2,6},{4,0},{6,2},{8,12},{10,14},{12,8},{14,10},{16,20},{18,... | collective-permute-start | bytes 392 | tf_op jit(solution)/shard_map/ppermute | solution.py:13
  34.3 6.6 %collective-permute-start.10 = (f32[32]{0:T(128)S(1)}, f32[32]{0:T(128)S(1)}, u32[]{:S(2)}, u32[]{:S(2)}) collective-permute-start(f32[32]{0:T(128)S(1)} %maximum_reduce_fusion.1), channel_id=1, source_target_pairs={{0,8},{2,10},{4,12},{6,14},{8,0},{10,2},{12,4},{14,6},{16,24},{18,... | collective-permute-start | bytes 392 | tf_op jit(solution)/shard_map/ppermute | solution.py:13
  42.9 3.1 collective-permute-start.11
  47.7 4.7 %collective-permute-start.12 = (f32[32]{0:T(128)S(1)}, f32[32]{0:T(128)S(1)}, u32[]{:S(2)}, u32[]{:S(2)}) collective-permute-start(f32[32]{0:T(128)S(1)} %maximum_reduce_fusion.3), channel_id=1, source_target_pairs={{0,32},{2,34},{4,36},{6,38},{8,40},{10,42},{12,44},{14,46},{16,48}... | collective-permute-start | bytes 392 | tf_op jit(solution)/shard_map/ppermute | solution.py:13
  53.9 4.0 %collective-permute-start.13 = (f32[32]{0:T(128)S(1)}, f32[32]{0:T(128)S(1)}, u32[]{:S(2)}, u32[]{:S(2)}) collective-permute-start(f32[32]{0:T(128)S(1)} %maximum_reduce_fusion.4), channel_id=1, source_target_pairs={{0,64},{2,66},{4,68},{6,70},{8,72},{10,74},{12,76},{14,78},{16,80}... | collective-permute-start | bytes 392 | tf_op jit(solution)/shard_map/ppermute | solution.py:13
  59.2 5.8 %collective-permute-start.14 = (f32[32]{0:T(128)S(1)}, f32[32]{0:T(128)S(1)}, u32[]{:S(2)}, u32[]{:S(2)}) collective-permute-start(f32[32]{0:T(128)S(1)} %maximum_reduce_fusion.5), channel_id=1, source_target_pairs={{0,128},{2,130},{4,132},{6,134},{8,136},{10,138},{12,140},{14,142}... | collective-permute-start | bytes 392 | tf_op jit(solution)/shard_map/ppermute | solution.py:13
  66.4 8.5 %collective-permute-start.15 = (f32[32]{0:T(128)S(1)}, f32[32]{0:T(128)S(1)}, u32[]{:S(2)}, u32[]{:S(2)}) collective-permute-start(f32[32]{0:T(128)S(1)} %maximum_reduce_fusion.6), channel_id=1, source_target_pairs={{0,256},{2,258},{4,260},{6,262},{8,264},{10,266},{12,268},{14,270}... | collective-permute-start | bytes 392 | tf_op jit(solution)/shard_map/ppermute | solution.py:13
  76.7 4.2 %collective-permute-start.1 = (f32[32,256]{1,0:T(8,128)S(1)}, f32[32,256]{1,0:T(8,128)S(1)}, u32[]{:S(2)}, u32[]{:S(2)}) collective-permute-start(f32[32,256]{1,0:T(8,128)S(1)} %reduce_sum.253), channel_id=1, source_target_pairs={{0,4},{2,6},{4,0},{6,2},{8,12},{10,14},{12,8},{14,10},{16,20},{18,... | collective-permute-start | bytes 98312 | tf_op jit(solution)/shard_map/ppermute | solution.py:13
  81.1 2.0 collective-permute-start.17
  83.2 6.6 %collective-permute-start.2 = (f32[32,256]{1,0:T(8,128)S(1)}, f32[32,256]{1,0:T(8,128)S(1)}, u32[]{:S(2)}, u32[]{:S(2)}) collective-permute-start(f32[32,256]{1,0:T(8,128)S(1)} %reduce_sum.254), channel_id=1, source_target_pairs={{0,8},{2,10},{4,12},{6,14},{8,0},{10,2},{12,4},{14,6},{16,24},{18,... | collective-permute-start | bytes 98312 | tf_op jit(solution)/shard_map/ppermute | solution.py:13
  90.0 2.6 collective-permute-start.18
  92.8 3.1 collective-permute-start.3
  95.9 2.6 collective-permute-done.18
  98.7 3.1 collective-permute-start.19
  102.0 4.4 %collective-permute-start.4 = (f32[32,256]{1,0:T(8,128)S(1)}, f32[32,256]{1,0:T(8,128)S(1)}, u32[]{:S(2)}, u32[]{:S(2)}) collective-permute-start(f32[32,256]{1,0:T(8,128)S(1)} %reduce_sum.256), channel_id=1, source_target_pairs={{0,32},{2,34},{4,36},{6,38},{8,40},{10,42},{12,44},{14,46},{16,48}... | collective-permute-start | bytes 98312 | tf_op jit(solution)/shard_map/ppermute | solution.py:13
  106.6 2.4 collective-permute-start.20
  109.2 3.1 collective-permute-start.5
  112.9 3.1 collective-permute-start.21
  116.2 4.0 %collective-permute-start.6 = (f32[32,256]{1,0:T(8,128)S(1)}, f32[32,256]{1,0:T(8,128)S(1)}, u32[]{:S(2)}, u32[]{:S(2)}) collective-permute-start(f32[32,256]{1,0:T(8,128)S(1)} %reduce_sum.258), channel_id=1, source_target_pairs={{0,128},{2,130},{4,132},{6,134},{8,136},{10,138},{12,140},{14,142}... | collective-permute-start | bytes 98312 | tf_op jit(solution)/shard_map/ppermute | solution.py:13
  120.4 2.2 collective-permute-start.22
  122.7 7.1 %collective-permute-start.7 = (f32[32,256]{1,0:T(8,128)S(1)}, f32[32,256]{1,0:T(8,128)S(1)}, u32[]{:S(2)}, u32[]{:S(2)}) collective-permute-start(f32[32,256]{1,0:T(8,128)S(1)} %reduce_sum.259), channel_id=1, source_target_pairs={{0,256},{2,258},{4,260},{6,262},{8,264},{10,266},{12,268},{14,270}... | collective-permute-start | bytes 98312 | tf_op jit(solution)/shard_map/ppermute | solution.py:13
  130.0 3.7 %collective-permute-start.23 = (f32[32,256]{1,0:T(8,128)S(1)}, f32[32,256]{1,0:T(8,128)S(1)}, u32[]{:S(2)}, u32[]{:S(2)}) collective-permute-start(f32[32,256]{1,0:T(8,128)S(1)} %reduce_sum.275), channel_id=1, source_target_pairs={{0,256},{2,258},{4,260},{6,262},{8,264},{10,266},{12,268},{14,270}... | collective-permute-start | bytes 98312 | tf_op jit(solution)/shard_map/ppermute | solution.py:13
  133.8 5.2 %collective-permute-done.23 = f32[32,256]{1,0:T(8,128)S(1)} collective-permute-done((f32[32,256]{1,0:T(8,128)S(1)}, f32[32,256]{1,0:T(8,128)S(1)}, u32[]{:S(2)}, u32[]{:S(2)}) %collective-permute-start.23) | collective-permute-done | bytes 32800 | tf_op jit(solution)/shard_map/ppermute | solution.py:13
  145.6 2.0 copy.223
  155.4 3.4 fusion.43
  158.8 5.4 %fusion.25 = f32[32,16]{0,1:T(8,128)S(1)} fusion(f32[32,16]{0,1:T(8,128)S(1)} %broadcast_in_dim.170, s32[]{:T(128)S(6)} %select_n.506, f32[8,128,384]{1,0,2:T(8,128)S(1)} %copy-done.8, f32[32]{0:T(128)S(1)} %copy-done.20, f32[32]{0:T(128)S(1)} %copy-done.22, f32[128,384]{0,1:T(8,128)S(1)} %copy-done.13), kind=kOutput, calls=%fused_computation.28 | convolution fusion | flops 155713536 | bytes 1774596 | tf_op jit(solution)/shard_map/htk,tkm->mh/dot_general | solution.py:136
  166.0 5.0 %fusion.40 = f32[32]{0:T(128)S(1)} fusion(f32[8,128,384]{1,0,2:T(8,128)} %copy.209, f32[32]{0:T(128)S(1)} %copy-done.20, f32[32]{0:T(128)S(1)} %copy-done.22, f32[128,384]{0,1:T(8,128)S(1)} %copy-done.13, f32[32,16]{0,1:T(8,128)S(1)} %copy-done.17, s32[]{:T(128)S(6)} %select_n.506), kind=kOutput, calls=%fused_computation.33 | convolution fusion | flops 155714016 | bytes 1770884 | tf_op jit(solution)/shard_map/htk,tkm->hm/dot_general | solution.py:139
  176.2 3.3 collective-permute-start.24
  179.9 6.0 %collective-permute-start.32 = (f32[32,256]{1,0:T(8,128)S(1)}, f32[32,256]{1,0:T(8,128)S(1)}, u32[]{:S(2)}, u32[]{:S(2)}) collective-permute-start(f32[32,256]{1,0:T(8,128)S(1)} %slice.234), channel_id=1, source_target_pairs={{0,256},{2,258},{4,260},{6,262},{8,264},{10,266},{12,268},{14,270}... | collective-permute-start | bytes 98312 | tf_op jit(solution)/shard_map/ppermute | solution.py:13
  186.8 4.0 %collective-permute-start.25 = (f32[32,256]{1,0:T(8,128)S(1)}, f32[32,256]{1,0:T(8,128)S(1)}, u32[]{:S(2)}, u32[]{:S(2)}) collective-permute-start(f32[32,256]{1,0:T(8,128)S(1)} %slice_add_fusion.13), channel_id=1, source_target_pairs={{0,128},{2,130},{4,132},{6,134},{8,136},{10,138},{12,140},{14,142}... | collective-permute-start | bytes 98312 | tf_op jit(solution)/shard_map/ppermute | solution.py:13
  190.9 2.2 collective-permute-start.33
  194.0 1.9 collective-permute-start.26
  196.7 2.7 collective-permute-start.34
  199.6 3.0 collective-permute-start.27
  202.8 3.8 %collective-permute-start.35 = (f32[32,256]{1,0:T(8,128)S(1)}, f32[32,256]{1,0:T(8,128)S(1)}, u32[]{:S(2)}, u32[]{:S(2)}) collective-permute-start(f32[32,256]{1,0:T(8,128)S(1)} %slice_add_fusion.4), channel_id=1, source_target_pairs={{0,32},{2,34},{4,36},{6,38},{8,40},{10,42},{12,44},{14,46},{16,48}... | collective-permute-start | bytes 98312 | tf_op jit(solution)/shard_map/ppermute | solution.py:13
  209.1 3.1 collective-permute-start.36
  212.4 3.3 collective-permute-start.29
  215.8 5.9 %collective-permute-start.37 = (f32[32,256]{1,0:T(8,128)S(1)}, f32[32,256]{1,0:T(8,128)S(1)}, u32[]{:S(2)}, u32[]{:S(2)}) collective-permute-start(f32[32,256]{1,0:T(8,128)S(1)} %slice_add_fusion.2), channel_id=1, source_target_pairs={{0,8},{2,10},{4,12},{6,14},{8,0},{10,2},{12,4},{14,6},{16,24},{18,... | collective-permute-start | bytes 98312 | tf_op jit(solution)/shard_map/ppermute | solution.py:13
  221.9 2.6 collective-permute-start.30
  224.7 4.2 %collective-permute-start.38 = (f32[32,256]{1,0:T(8,128)S(1)}, f32[32,256]{1,0:T(8,128)S(1)}, u32[]{:S(2)}, u32[]{:S(2)}) collective-permute-start(f32[32,256]{1,0:T(8,128)S(1)} %slice_add_fusion.1), channel_id=1, source_target_pairs={{0,4},{2,6},{4,0},{6,2},{8,12},{10,14},{12,8},{14,10},{16,20},{18,... | collective-permute-start | bytes 98312 | tf_op jit(solution)/shard_map/ppermute | solution.py:13
  230.3 3.1 collective-permute-start.31
  233.5 2.2 collective-permute-start.39
  236.5 116.7 %all-reduce = (f32[32]{0:T(128)}, f32[32]{0:T(128)}, f32[32,16]{0,1:T(8,128)}) all-reduce(f32[32]{0:T(128)S(1)} %fusion.40, f32[32]{0:T(128)S(1)} %fusion.43, f32[32,16]{0,1:T(8,128)S(1)} %fusion.25), channel_id=1, replica_groups=mesh['ctx'=256,'mp'=2] {'ctx','mp'}, use_global_device_ids=true, to_apply=%region_28.29 | all-reduce | flops 576 | bytes 4608 | tf_op jit(solution)/shard_map/psum | solution.py:147
  (350 shorter events, 48.7 us)
Async XLA Ops:
  0.6 11.8 %copy-start.21 = (f32[32]{0:T(128)S(1)}, f32[32]{0:T(128)}, u32[]{:S(2)}) copy-start(f32[32]{0:T(128)} %param.12) | copy-start | bytes 388
  0.6 11.8 %copy-start.19 = (f32[32]{0:T(128)S(1)}, f32[32]{0:T(128)}, u32[]{:S(2)}) copy-start(f32[32]{0:T(128)} %param.13) | copy-start | bytes 388
  2.4 74.1 %collective-permute-start = (f32[32,256]{1,0:T(8,128)S(1)}, f32[32,256]{1,0:T(8,128)S(1)}, u32[]{:S(2)}, u32[]{:S(2)}) collective-permute-start(f32[32,256]{1,0:T(8,128)S(1)} %reduce_sum.252), channel_id=1, source_target_pairs={{0,2},{2,0},{4,6},{6,4},{8,10},{10,8},{12,14},{14,12},{16,18},{18,... | collective-permute-start | bytes 98312 | tf_op jit(solution)/shard_map/ppermute | solution.py:13
  6.5 21.7 %collective-permute-start.8 = (f32[32]{0:T(128)S(1)}, f32[32]{0:T(128)S(1)}, u32[]{:S(2)}, u32[]{:S(2)}) collective-permute-start(f32[32]{0:T(128)S(1)} %convert_reduce_fusion), channel_id=1, source_target_pairs={{0,2},{2,0},{4,6},{6,4},{8,10},{10,8},{12,14},{14,12},{16,18},{18,... | collective-permute-start | bytes 392 | tf_op jit(solution)/shard_map/ppermute | solution.py:13
  8.5 72.4 %collective-permute-start.16 = (f32[32,256]{1,0:T(8,128)S(1)}, f32[32,256]{1,0:T(8,128)S(1)}, u32[]{:S(2)}, u32[]{:S(2)}) collective-permute-start(f32[32,256]{1,0:T(8,128)S(1)} %reduce_sum.268), channel_id=1, source_target_pairs={{0,2},{2,0},{4,6},{6,4},{8,10},{10,8},{12,14},{14,12},{16,18},{18,... | collective-permute-start | bytes 98312 | tf_op jit(solution)/shard_map/ppermute | solution.py:13
  16.2 6.8 %copy-start.14 = (bf16[128,1024]{1,0:T(8,128)(2,1)S(1)}, bf16[128,1024]{1,0:T(8,128)(2,1)}, u32[]{:S(2)}) copy-start(bf16[128,1024]{1,0:T(8,128)(2,1)} %param.15) | copy-start | bytes 786436
  16.2 6.9 %copy-start.17 = (f32[32,16]{0,1:T(8,128)S(1)}, f32[32,16]{0,1:T(8,128)}, u32[]{:S(2)}) copy-start(f32[32,16]{0,1:T(8,128)} %param.14) | copy-start | bytes 6148
  23.0 51.8 %copy-start.15 = (bf16[128,1024]{1,0:T(8,128)(2,1)S(1)}, bf16[128,1024]{1,0:T(8,128)(2,1)}, u32[]{:S(2)}) copy-start(bf16[128,1024]{1,0:T(8,128)(2,1)} %param.8) | copy-start | bytes 786436
  28.7 5.2 %collective-permute-start.9 = (f32[32]{0:T(128)S(1)}, f32[32]{0:T(128)S(1)}, u32[]{:S(2)}, u32[]{:S(2)}) collective-permute-start(f32[32]{0:T(128)S(1)} %maximum_reduce_fusion), channel_id=1, source_target_pairs={{0,4},{2,6},{4,0},{6,2},{8,12},{10,14},{12,8},{14,10},{16,20},{18,... | collective-permute-start | bytes 392 | tf_op jit(solution)/shard_map/ppermute | solution.py:13
  34.3 8.2 %collective-permute-start.10 = (f32[32]{0:T(128)S(1)}, f32[32]{0:T(128)S(1)}, u32[]{:S(2)}, u32[]{:S(2)}) collective-permute-start(f32[32]{0:T(128)S(1)} %maximum_reduce_fusion.1), channel_id=1, source_target_pairs={{0,8},{2,10},{4,12},{6,14},{8,0},{10,2},{12,4},{14,6},{16,24},{18,... | collective-permute-start | bytes 392 | tf_op jit(solution)/shard_map/ppermute | solution.py:13
  42.9 4.3 %collective-permute-start.11 = (f32[32]{0:T(128)S(1)}, f32[32]{0:T(128)S(1)}, u32[]{:S(2)}, u32[]{:S(2)}) collective-permute-start(f32[32]{0:T(128)S(1)} %maximum_reduce_fusion.2), channel_id=1, source_target_pairs={{0,16},{2,18},{4,20},{6,22},{8,24},{10,26},{12,28},{14,30},{16,0},... | collective-permute-start | bytes 392 | tf_op jit(solution)/shard_map/ppermute | solution.py:13
  47.7 5.8 %collective-permute-start.12 = (f32[32]{0:T(128)S(1)}, f32[32]{0:T(128)S(1)}, u32[]{:S(2)}, u32[]{:S(2)}) collective-permute-start(f32[32]{0:T(128)S(1)} %maximum_reduce_fusion.3), channel_id=1, source_target_pairs={{0,32},{2,34},{4,36},{6,38},{8,40},{10,42},{12,44},{14,46},{16,48}... | collective-permute-start | bytes 392 | tf_op jit(solution)/shard_map/ppermute | solution.py:13
  53.9 4.9 %collective-permute-start.13 = (f32[32]{0:T(128)S(1)}, f32[32]{0:T(128)S(1)}, u32[]{:S(2)}, u32[]{:S(2)}) collective-permute-start(f32[32]{0:T(128)S(1)} %maximum_reduce_fusion.4), channel_id=1, source_target_pairs={{0,64},{2,66},{4,68},{6,70},{8,72},{10,74},{12,76},{14,78},{16,80}... | collective-permute-start | bytes 392 | tf_op jit(solution)/shard_map/ppermute | solution.py:13
  59.2 6.7 %collective-permute-start.14 = (f32[32]{0:T(128)S(1)}, f32[32]{0:T(128)S(1)}, u32[]{:S(2)}, u32[]{:S(2)}) collective-permute-start(f32[32]{0:T(128)S(1)} %maximum_reduce_fusion.5), channel_id=1, source_target_pairs={{0,128},{2,130},{4,132},{6,134},{8,136},{10,138},{12,140},{14,142}... | collective-permute-start | bytes 392 | tf_op jit(solution)/shard_map/ppermute | solution.py:13
  66.4 9.5 %collective-permute-start.15 = (f32[32]{0:T(128)S(1)}, f32[32]{0:T(128)S(1)}, u32[]{:S(2)}, u32[]{:S(2)}) collective-permute-start(f32[32]{0:T(128)S(1)} %maximum_reduce_fusion.6), channel_id=1, source_target_pairs={{0,256},{2,258},{4,260},{6,262},{8,264},{10,266},{12,268},{14,270}... | collective-permute-start | bytes 392 | tf_op jit(solution)/shard_map/ppermute | solution.py:13
  76.7 6.4 %collective-permute-start.1 = (f32[32,256]{1,0:T(8,128)S(1)}, f32[32,256]{1,0:T(8,128)S(1)}, u32[]{:S(2)}, u32[]{:S(2)}) collective-permute-start(f32[32,256]{1,0:T(8,128)S(1)} %reduce_sum.253), channel_id=1, source_target_pairs={{0,4},{2,6},{4,0},{6,2},{8,12},{10,14},{12,8},{14,10},{16,20},{18,... | collective-permute-start | bytes 98312 | tf_op jit(solution)/shard_map/ppermute | solution.py:13
  81.1 8.7 %collective-permute-start.17 = (f32[32,256]{1,0:T(8,128)S(1)}, f32[32,256]{1,0:T(8,128)S(1)}, u32[]{:S(2)}, u32[]{:S(2)}) collective-permute-start(f32[32,256]{1,0:T(8,128)S(1)} %reduce_sum.269), channel_id=1, source_target_pairs={{0,4},{2,6},{4,0},{6,2},{8,12},{10,14},{12,8},{14,10},{16,20},{18,... | collective-permute-start | bytes 98312 | tf_op jit(solution)/shard_map/ppermute | solution.py:13
  83.2 9.4 %collective-permute-start.2 = (f32[32,256]{1,0:T(8,128)S(1)}, f32[32,256]{1,0:T(8,128)S(1)}, u32[]{:S(2)}, u32[]{:S(2)}) collective-permute-start(f32[32,256]{1,0:T(8,128)S(1)} %reduce_sum.254), channel_id=1, source_target_pairs={{0,8},{2,10},{4,12},{6,14},{8,0},{10,2},{12,4},{14,6},{16,24},{18,... | collective-permute-start | bytes 98312 | tf_op jit(solution)/shard_map/ppermute | solution.py:13
  90.0 8.6 %collective-permute-start.18 = (f32[32,256]{1,0:T(8,128)S(1)}, f32[32,256]{1,0:T(8,128)S(1)}, u32[]{:S(2)}, u32[]{:S(2)}) collective-permute-start(f32[32,256]{1,0:T(8,128)S(1)} %reduce_sum.270), channel_id=1, source_target_pairs={{0,8},{2,10},{4,12},{6,14},{8,0},{10,2},{12,4},{14,6},{16,24},{18,... | collective-permute-start | bytes 98312 | tf_op jit(solution)/shard_map/ppermute | solution.py:13
  92.8 9.1 %collective-permute-start.3 = (f32[32,256]{1,0:T(8,128)S(1)}, f32[32,256]{1,0:T(8,128)S(1)}, u32[]{:S(2)}, u32[]{:S(2)}) collective-permute-start(f32[32,256]{1,0:T(8,128)S(1)} %reduce_sum.255), channel_id=1, source_target_pairs={{0,16},{2,18},{4,20},{6,22},{8,24},{10,26},{12,28},{14,30},{16,0},... | collective-permute-start | bytes 98312 | tf_op jit(solution)/shard_map/ppermute | solution.py:13
  98.7 7.7 %collective-permute-start.19 = (f32[32,256]{1,0:T(8,128)S(1)}, f32[32,256]{1,0:T(8,128)S(1)}, u32[]{:S(2)}, u32[]{:S(2)}) collective-permute-start(f32[32,256]{1,0:T(8,128)S(1)} %reduce_sum.271), channel_id=1, source_target_pairs={{0,16},{2,18},{4,20},{6,22},{8,24},{10,26},{12,28},{14,30},{16,0},... | collective-permute-start | bytes 98312 | tf_op jit(solution)/shard_map/ppermute | solution.py:13
  102.0 7.0 %collective-permute-start.4 = (f32[32,256]{1,0:T(8,128)S(1)}, f32[32,256]{1,0:T(8,128)S(1)}, u32[]{:S(2)}, u32[]{:S(2)}) collective-permute-start(f32[32,256]{1,0:T(8,128)S(1)} %reduce_sum.256), channel_id=1, source_target_pairs={{0,32},{2,34},{4,36},{6,38},{8,40},{10,42},{12,44},{14,46},{16,48}... | collective-permute-start | bytes 98312 | tf_op jit(solution)/shard_map/ppermute | solution.py:13
  106.6 6.2 %collective-permute-start.20 = (f32[32,256]{1,0:T(8,128)S(1)}, f32[32,256]{1,0:T(8,128)S(1)}, u32[]{:S(2)}, u32[]{:S(2)}) collective-permute-start(f32[32,256]{1,0:T(8,128)S(1)} %reduce_sum.272), channel_id=1, source_target_pairs={{0,32},{2,34},{4,36},{6,38},{8,40},{10,42},{12,44},{14,46},{16,48}... | collective-permute-start | bytes 98312 | tf_op jit(solution)/shard_map/ppermute | solution.py:13
  109.2 6.8 %collective-permute-start.5 = (f32[32,256]{1,0:T(8,128)S(1)}, f32[32,256]{1,0:T(8,128)S(1)}, u32[]{:S(2)}, u32[]{:S(2)}) collective-permute-start(f32[32,256]{1,0:T(8,128)S(1)} %reduce_sum.257), channel_id=1, source_target_pairs={{0,64},{2,66},{4,68},{6,70},{8,72},{10,74},{12,76},{14,78},{16,80}... | collective-permute-start | bytes 98312 | tf_op jit(solution)/shard_map/ppermute | solution.py:13
  112.8 26.3 %copy-start.16 = (bf16[128,256]{1,0:T(8,128)(2,1)S(1)}, bf16[128,256]{1,0:T(8,128)(2,1)}, u32[]{:S(2)}) copy-start(bf16[128,256]{1,0:T(8,128)(2,1)} %param.9) | copy-start | bytes 196612
  112.9 7.3 %collective-permute-start.21 = (f32[32,256]{1,0:T(8,128)S(1)}, f32[32,256]{1,0:T(8,128)S(1)}, u32[]{:S(2)}, u32[]{:S(2)}) collective-permute-start(f32[32,256]{1,0:T(8,128)S(1)} %reduce_sum.273), channel_id=1, source_target_pairs={{0,64},{2,66},{4,68},{6,70},{8,72},{10,74},{12,76},{14,78},{16,80}... | collective-permute-start | bytes 98312 | tf_op jit(solution)/shard_map/ppermute | solution.py:13
  116.2 6.4 %collective-permute-start.6 = (f32[32,256]{1,0:T(8,128)S(1)}, f32[32,256]{1,0:T(8,128)S(1)}, u32[]{:S(2)}, u32[]{:S(2)}) collective-permute-start(f32[32,256]{1,0:T(8,128)S(1)} %reduce_sum.258), channel_id=1, source_target_pairs={{0,128},{2,130},{4,132},{6,134},{8,136},{10,138},{12,140},{14,142}... | collective-permute-start | bytes 98312 | tf_op jit(solution)/shard_map/ppermute | solution.py:13
  120.4 9.5 %collective-permute-start.22 = (f32[32,256]{1,0:T(8,128)S(1)}, f32[32,256]{1,0:T(8,128)S(1)}, u32[]{:S(2)}, u32[]{:S(2)}) collective-permute-start(f32[32,256]{1,0:T(8,128)S(1)} %reduce_sum.274), channel_id=1, source_target_pairs={{0,128},{2,130},{4,132},{6,134},{8,136},{10,138},{12,140},{14,142}... | collective-permute-start | bytes 98312 | tf_op jit(solution)/shard_map/ppermute | solution.py:13
  122.7 11.0 %collective-permute-start.7 = (f32[32,256]{1,0:T(8,128)S(1)}, f32[32,256]{1,0:T(8,128)S(1)}, u32[]{:S(2)}, u32[]{:S(2)}) collective-permute-start(f32[32,256]{1,0:T(8,128)S(1)} %reduce_sum.259), channel_id=1, source_target_pairs={{0,256},{2,258},{4,260},{6,262},{8,264},{10,266},{12,268},{14,270}... | collective-permute-start | bytes 98312 | tf_op jit(solution)/shard_map/ppermute | solution.py:13
  130.0 8.9 %collective-permute-start.23 = (f32[32,256]{1,0:T(8,128)S(1)}, f32[32,256]{1,0:T(8,128)S(1)}, u32[]{:S(2)}, u32[]{:S(2)}) collective-permute-start(f32[32,256]{1,0:T(8,128)S(1)} %reduce_sum.275), channel_id=1, source_target_pairs={{0,256},{2,258},{4,260},{6,262},{8,264},{10,266},{12,268},{14,270}... | collective-permute-start | bytes 98312 | tf_op jit(solution)/shard_map/ppermute | solution.py:13
  176.2 9.7 %collective-permute-start.24 = (f32[32,256]{1,0:T(8,128)S(1)}, f32[32,256]{1,0:T(8,128)S(1)}, u32[]{:S(2)}, u32[]{:S(2)}) collective-permute-start(f32[32,256]{1,0:T(8,128)S(1)} %slice.210), channel_id=1, source_target_pairs={{0,256},{2,258},{4,260},{6,262},{8,264},{10,266},{12,268},{14,270}... | collective-permute-start | bytes 98312 | tf_op jit(solution)/shard_map/ppermute | solution.py:13
  179.9 19.7 %copy-start.10 = (f32[256,256]{1,0:T(8,128)S(1)}, f32[256,256]{1,0:T(8,128)}, u32[]{:S(2)}) copy-start(f32[256,256]{1,0:T(8,128)} %copy-done.9) | copy-start | bytes 786436
  179.9 10.9 %collective-permute-start.32 = (f32[32,256]{1,0:T(8,128)S(1)}, f32[32,256]{1,0:T(8,128)S(1)}, u32[]{:S(2)}, u32[]{:S(2)}) collective-permute-start(f32[32,256]{1,0:T(8,128)S(1)} %slice.234), channel_id=1, source_target_pairs={{0,256},{2,258},{4,260},{6,262},{8,264},{10,266},{12,268},{14,270}... | collective-permute-start | bytes 98312 | tf_op jit(solution)/shard_map/ppermute | solution.py:13
  186.8 6.4 %collective-permute-start.25 = (f32[32,256]{1,0:T(8,128)S(1)}, f32[32,256]{1,0:T(8,128)S(1)}, u32[]{:S(2)}, u32[]{:S(2)}) collective-permute-start(f32[32,256]{1,0:T(8,128)S(1)} %slice_add_fusion.13), channel_id=1, source_target_pairs={{0,128},{2,130},{4,132},{6,134},{8,136},{10,138},{12,140},{14,142}... | collective-permute-start | bytes 98312 | tf_op jit(solution)/shard_map/ppermute | solution.py:13
  190.9 5.7 %collective-permute-start.33 = (f32[32,256]{1,0:T(8,128)S(1)}, f32[32,256]{1,0:T(8,128)S(1)}, u32[]{:S(2)}, u32[]{:S(2)}) collective-permute-start(f32[32,256]{1,0:T(8,128)S(1)} %slice_add_fusion.6), channel_id=1, source_target_pairs={{0,128},{2,130},{4,132},{6,134},{8,136},{10,138},{12,140},{14,142}... | collective-permute-start | bytes 98312 | tf_op jit(solution)/shard_map/ppermute | solution.py:13
  194.0 5.5 %collective-permute-start.26 = (f32[32,256]{1,0:T(8,128)S(1)}, f32[32,256]{1,0:T(8,128)S(1)}, u32[]{:S(2)}, u32[]{:S(2)}) collective-permute-start(f32[32,256]{1,0:T(8,128)S(1)} %slice_add_fusion.12), channel_id=1, source_target_pairs={{0,64},{2,66},{4,68},{6,70},{8,72},{10,74},{12,76},{14,78},{16,80}... | collective-permute-start | bytes 98312 | tf_op jit(solution)/shard_map/ppermute | solution.py:13
  196.7 5.9 %collective-permute-start.34 = (f32[32,256]{1,0:T(8,128)S(1)}, f32[32,256]{1,0:T(8,128)S(1)}, u32[]{:S(2)}, u32[]{:S(2)}) collective-permute-start(f32[32,256]{1,0:T(8,128)S(1)} %slice_add_fusion.5), channel_id=1, source_target_pairs={{0,64},{2,66},{4,68},{6,70},{8,72},{10,74},{12,76},{14,78},{16,80}... | collective-permute-start | bytes 98312 | tf_op jit(solution)/shard_map/ppermute | solution.py:13
  199.6 7.0 %collective-permute-start.27 = (f32[32,256]{1,0:T(8,128)S(1)}, f32[32,256]{1,0:T(8,128)S(1)}, u32[]{:S(2)}, u32[]{:S(2)}) collective-permute-start(f32[32,256]{1,0:T(8,128)S(1)} %slice_add_fusion.11), channel_id=1, source_target_pairs={{0,32},{2,34},{4,36},{6,38},{8,40},{10,42},{12,44},{14,46},{16,48}... | collective-permute-start | bytes 98312 | tf_op jit(solution)/shard_map/ppermute | solution.py:13
  202.7 26.1 %copy-start.5 = (bf16[384,256]{0,1:T(8,128)(2,1)S(1)}, bf16[384,256]{0,1:T(8,128)(2,1)}, u32[]{:S(2)}) copy-start(bf16[384,256]{0,1:T(8,128)(2,1)} %copy.189) | copy-start | bytes 589828
  202.8 6.2 %collective-permute-start.35 = (f32[32,256]{1,0:T(8,128)S(1)}, f32[32,256]{1,0:T(8,128)S(1)}, u32[]{:S(2)}, u32[]{:S(2)}) collective-permute-start(f32[32,256]{1,0:T(8,128)S(1)} %slice_add_fusion.4), channel_id=1, source_target_pairs={{0,32},{2,34},{4,36},{6,38},{8,40},{10,42},{12,44},{14,46},{16,48}... | collective-permute-start | bytes 98312 | tf_op jit(solution)/shard_map/ppermute | solution.py:13
  206.8 5.5 %collective-permute-start.28 = (f32[32,256]{1,0:T(8,128)S(1)}, f32[32,256]{1,0:T(8,128)S(1)}, u32[]{:S(2)}, u32[]{:S(2)}) collective-permute-start(f32[32,256]{1,0:T(8,128)S(1)} %slice_add_fusion.10), channel_id=1, source_target_pairs={{0,16},{2,18},{4,20},{6,22},{8,24},{10,26},{12,28},{14,30},{16,0},... | collective-permute-start | bytes 98312 | tf_op jit(solution)/shard_map/ppermute | solution.py:13
  209.1 6.5 %collective-permute-start.36 = (f32[32,256]{1,0:T(8,128)S(1)}, f32[32,256]{1,0:T(8,128)S(1)}, u32[]{:S(2)}, u32[]{:S(2)}) collective-permute-start(f32[32,256]{1,0:T(8,128)S(1)} %slice_add_fusion.3), channel_id=1, source_target_pairs={{0,16},{2,18},{4,20},{6,22},{8,24},{10,26},{12,28},{14,30},{16,0},... | collective-permute-start | bytes 98312 | tf_op jit(solution)/shard_map/ppermute | solution.py:13
  212.4 9.4 %collective-permute-start.29 = (f32[32,256]{1,0:T(8,128)S(1)}, f32[32,256]{1,0:T(8,128)S(1)}, u32[]{:S(2)}, u32[]{:S(2)}) collective-permute-start(f32[32,256]{1,0:T(8,128)S(1)} %slice_add_fusion.9), channel_id=1, source_target_pairs={{0,8},{2,10},{4,12},{6,14},{8,0},{10,2},{12,4},{14,6},{16,24},{18,... | collective-permute-start | bytes 98312 | tf_op jit(solution)/shard_map/ppermute | solution.py:13
  215.8 8.7 %collective-permute-start.37 = (f32[32,256]{1,0:T(8,128)S(1)}, f32[32,256]{1,0:T(8,128)S(1)}, u32[]{:S(2)}, u32[]{:S(2)}) collective-permute-start(f32[32,256]{1,0:T(8,128)S(1)} %slice_add_fusion.2), channel_id=1, source_target_pairs={{0,8},{2,10},{4,12},{6,14},{8,0},{10,2},{12,4},{14,6},{16,24},{18,... | collective-permute-start | bytes 98312 | tf_op jit(solution)/shard_map/ppermute | solution.py:13
  221.9 7.6 %collective-permute-start.30 = (f32[32,256]{1,0:T(8,128)S(1)}, f32[32,256]{1,0:T(8,128)S(1)}, u32[]{:S(2)}, u32[]{:S(2)}) collective-permute-start(f32[32,256]{1,0:T(8,128)S(1)} %slice_add_fusion.8), channel_id=1, source_target_pairs={{0,4},{2,6},{4,0},{6,2},{8,12},{10,14},{12,8},{14,10},{16,20},{18,... | collective-permute-start | bytes 98312 | tf_op jit(solution)/shard_map/ppermute | solution.py:13
  224.7 5.6 %collective-permute-start.38 = (f32[32,256]{1,0:T(8,128)S(1)}, f32[32,256]{1,0:T(8,128)S(1)}, u32[]{:S(2)}, u32[]{:S(2)}) collective-permute-start(f32[32,256]{1,0:T(8,128)S(1)} %slice_add_fusion.1), channel_id=1, source_target_pairs={{0,4},{2,6},{4,0},{6,2},{8,12},{10,14},{12,8},{14,10},{16,20},{18,... | collective-permute-start | bytes 98312 | tf_op jit(solution)/shard_map/ppermute | solution.py:13
  230.3 124.1 %collective-permute-start.31 = (f32[32,256]{1,0:T(8,128)S(1)}, f32[32,256]{1,0:T(8,128)S(1)}, u32[]{:S(2)}, u32[]{:S(2)}) collective-permute-start(f32[32,256]{1,0:T(8,128)S(1)} %slice_add_fusion.7), channel_id=1, source_target_pairs={{0,2},{2,0},{4,6},{6,4},{8,10},{10,8},{12,14},{14,12},{16,18},{18,... | collective-permute-start | bytes 98312 | tf_op jit(solution)/shard_map/ppermute | solution.py:13
  233.5 121.0 %collective-permute-start.39 = (f32[32,256]{1,0:T(8,128)S(1)}, f32[32,256]{1,0:T(8,128)S(1)}, u32[]{:S(2)}, u32[]{:S(2)}) collective-permute-start(f32[32,256]{1,0:T(8,128)S(1)} %slice_add_fusion), channel_id=1, source_target_pairs={{0,2},{2,0},{4,6},{6,4},{8,10},{10,8},{12,14},{14,12},{16,18},{18,... | collective-permute-start | bytes 98312 | tf_op jit(solution)/shard_map/ppermute | solution.py:13
  (15 other events, 34.2 us)
where the time goes:
time: 357 us; the launch traced here: 355 us
  starting transfers between devices  151 us (42%)
  blocking collectives  117 us (33%)
  local copies, waits for them, and re-layouts  27 us (8%)
  matrix products  23.3 us (7%)
  other arithmetic  17.2 us (5%)
  waiting for transfers between devices  16.6 us (5%)
  between operations  3.65 us (1%)
    ppermute x40, starting transfers between devices, swapped(): return lax.ppermute(value, axis, pairs)  151 us
    psum x1, blocking collectives, shards(): lax.psum((w1_term, b1_term, w2_full), ('ctx', 'mp'))  117 us
    ppermute x40, waiting for transfers between devices, swapped(): return lax.ppermute(value, axis, pairs)  16.6 us
  transfers between devices with their start and end apart: 40, of which 12 were waited for; matrix products, arithmetic and copies ran while one was open for 8% of the time, Pallas kernels for 0%

commit v1 on v0

v1 whole, which is shorter than its diff:
```python
import functools

import jax
import jax.numpy as jnp
from jax import lax
from jax.experimental import pallas as pl
from jax.experimental.pallas import tpu as pltpu
from jax.sharding import PartitionSpec as P

D = 128
COARSE = 32
T = 128
LEVELS = 8
KEYS = T + LEVELS * COARSE
HIDDEN = 32
HEADS = 8
KV = 2
GROUP = HEADS // KV
SUB = 8
SCALE = D ** (-0.5)
MASKS = (1, 2, 6, 8, 24, 32, 64, 192)
NT = (((1,), (1,)), ((), ()))
TN = (((0,), (0,)), ((), ()))
VMEM = pl.BlockSpec(memory_space=pltpu.VMEM)
SMEM = pl.BlockSpec(memory_space=pltpu.SMEM)


def dot(a, b, dims=(((1,), (0,)), ((), ()))):
    return lax.dot_general(a, b, dims, preferred_element_type=jnp.float32)


def exchange(value, level):
    pairs = [(i, i ^ MASKS[level]) for i in range(lax.axis_size("ctx"))]
    return lax.ppermute(value, "ctx", pairs)


def leaf_kernel(len_ref, k_ref, v_ref, out_ref):
    run = T // COARSE
    row = lax.broadcasted_iota(jnp.int32, (COARSE, T), 0)
    tok = lax.broadcasted_iota(jnp.int32, (COARSE, T), 1)
    member = jnp.where((tok // run == row) & (tok < len_ref[0]), 1.0, 0.0)
    member_b = member.astype(jnp.bfloat16)
    out_ref[:, : KV * D] = dot(member_b, k_ref[...])
    out_ref[:, KV * D : 2 * KV * D] = dot(member_b, v_ref[...])
    count = jnp.sum(member, axis=1, keepdims=True)
    out_ref[:, 2 * KV * D :] = jnp.broadcast_to(count, (COARSE, D))


def bias_kernel(ctx_ref, w1_ref, b1_ref, w2_ref, bias_ref, phase_ref):
    ctx = ctx_ref[0]
    col = lax.broadcasted_iota(jnp.int32, (1, KEYS), 1)
    level = (col - T) // COARSE
    pos = col.astype(jnp.float32)
    for k in range(LEVELS):
        run = 2**k * T // COARSE
        start = ((ctx >> k) ^ 1) * 2**k * T - ctx * T
        inside = (col - T - k * COARSE) * run
        here = (start + inside).astype(jnp.float32) + (run - 1) / 2.0
        pos = jnp.where((col >= T) & (level == k), here, pos)
    top = jnp.log1p(jnp.full((1, KEYS), 1.0, jnp.float32) * (LEVEL_TOKENS))

    def body(i, carry):
        row = i * SUB + lax.broadcasted_iota(jnp.int32, (SUB, KEYS), 0)
        phase = jnp.log1p(jnp.abs(row.astype(jnp.float32) - pos)) / top
        phase_ref[pl.ds(i * SUB, SUB), :] = phase
        sums = [jnp.zeros((SUB, KEYS), jnp.float32) for _ in range(HEADS)]
        for m in range(HIDDEN):
            hidden = jnp.maximum(phase * w1_ref[m] + b1_ref[m], 0.0)
            for h in range(HEADS):
                sums[h] = sums[h] + hidden * w2_ref[m, h]
        for h in range(HEADS):
            bias_ref[h, pl.ds(i * SUB, SUB), :] = sums[h]
        return carry

    lax.fori_loop(0, T // SUB, body, 0)


LEVEL_TOKENS = float(T * 2**LEVELS)


def main_kernel(
    len_ref, w1_ref, b1_ref, coef_ref, q_ref, k_ref, v_ref, g_ref, sib_ref, bias_ref, phase_ref,
    out_ref, gq_ref, gk_ref, gv_ref, ck_ref, cv_ref, w_ref, ds_ref, acc_ref,
):
    length = len_ref[0]
    count = sib_ref[:, 2 * KV * D :]
    safe = jnp.maximum(count, 1.0)
    count_t = jnp.concatenate([count[:T].T[:1], count[T:].T[:1]], axis=1)
    token_live = lax.broadcasted_iota(jnp.int32, (1, T), 1) < length
    live = jnp.concatenate([token_live.astype(jnp.float32), count_t], axis=1) > 0.0
    row_live = lax.broadcasted_iota(jnp.int32, (T, 1), 0) < length
    row_live_f = row_live.astype(jnp.float32)
    for j in range(KV):
        cols = slice(j * D, (j + 1) * D)
        vcols = slice((KV + j) * D, (KV + j + 1) * D)
        keys = jnp.concatenate([k_ref[:, cols], (sib_ref[:, cols] / safe).astype(jnp.bfloat16)], axis=0)
        values = jnp.concatenate([v_ref[:, cols], (sib_ref[:, vcols] / safe).astype(jnp.bfloat16)], axis=0)
        key_grads = jnp.zeros((KEYS, D), jnp.float32)
        value_grads = jnp.zeros((KEYS, D), jnp.float32)
        for g in range(GROUP):
            h = j * GROUP + g
            hcols = slice(h * D, (h + 1) * D)
            query = q_ref[:, hcols]
            scores = dot(query, keys, NT) * SCALE + bias_ref[h]
            scores = jnp.where(live, scores, -jnp.inf)
            top = jnp.max(scores, axis=1, keepdims=True)
            weights = jnp.exp(scores - top)
            probs = weights / jnp.sum(weights, axis=1, keepdims=True)
            probs_b = probs.astype(jnp.bfloat16)
            out_ref[:, hcols] = (dot(probs_b, values) * row_live_f).astype(jnp.bfloat16)
            grad = g_ref[:, hcols]
            grad = jnp.where(row_live, grad, jnp.zeros_like(grad))
            dprobs = dot(grad, values, NT)
            dscores = probs * (dprobs - jnp.sum(probs * dprobs, axis=1, keepdims=True))
            ds_ref[h] = dscores
            dscores_b = dscores.astype(jnp.bfloat16)
            gq_ref[:, hcols] = (SCALE * dot(dscores_b, keys)).astype(jnp.bfloat16)
            key_grads = key_grads + dot(dscores_b, query, TN)
            value_grads = value_grads + dot(probs_b, grad, TN)
        key_grads = key_grads * SCALE
        gk_ref[:, cols] = key_grads[:T]
        gv_ref[:, cols] = value_grads[:T]
        ck_ref[:, cols] = key_grads[T:] / safe
        cv_ref[:, cols] = value_grads[T:] / safe
    acc_ref[...] = jnp.zeros_like(acc_ref)

    def body(i, carry):
        rows = pl.ds(i * SUB, SUB)
        phase = phase_ref[rows, :]
        parts = [ds_ref[h, rows, :] for h in range(HEADS)]
        parts = jnp.concatenate(parts + [p * phase for p in parts], axis=0)
        high = parts.astype(jnp.bfloat16)
        low = (parts - high.astype(jnp.float32)).astype(jnp.bfloat16)
        both = jnp.concatenate([high, low], axis=0)
        active = [
            jnp.where(phase * w1_ref[m] + b1_ref[m] > 0.0, 1.0, 0.0) for m in range(HIDDEN)
        ]
        active = jnp.concatenate(active, axis=0).astype(jnp.bfloat16)
        acc_ref[...] += dot(both, active, NT)
        return carry

    lax.fori_loop(0, T // SUB, body, 0)
    acc = acc_ref[...]
    rows = 2 * HEADS * SUB
    acc = acc[:rows] + acc[rows:]
    sub_row = lax.broadcasted_iota(jnp.int32, acc.shape, 0) % SUB
    sub_col = lax.broadcasted_iota(jnp.int32, acc.shape, 1) % SUB
    acc = jnp.where(sub_row == sub_col, acc, 0.0)
    acc = acc.reshape(2 * HEADS, SUB, HIDDEN * SUB).sum(axis=1)
    unit = lax.broadcasted_iota(jnp.int32, (HIDDEN * SUB, D), 0) // SUB
    lane = lax.broadcasted_iota(jnp.int32, (HIDDEN * SUB, D), 1) % HIDDEN
    gather = jnp.where(unit == lane, 1.0, 0.0)
    sums = lax.dot_general(
        acc, gather, (((1,), (0,)), ((), ())),
        precision=lax.Precision.HIGHEST, preferred_element_type=jnp.float32,
    )
    w_ref[...] = coef_ref[0] * sums[:HEADS] + coef_ref[1] * sums[HEADS:]


def shards(queries, keys, values, lengths, fire_w1, fire_b1, fire_w2, grad_out):
    f32, bf16 = jnp.float32, jnp.bfloat16
    shape = jax.ShapeDtypeStruct
    ctx = lax.axis_index("ctx")
    mp = lax.axis_index("mp")
    w2 = lax.dynamic_slice_in_dim(fire_w2, mp * HEADS, HEADS, 1)
    w2_t = w2.T
    spread = lambda row: jnp.broadcast_to(row[None], (HEADS, HIDDEN))
    zero = jnp.zeros((HEADS, HIDDEN), f32)
    coef = jnp.stack([
        jnp.concatenate([spread(fire_b1), zero, w2_t, zero], axis=1),
        jnp.concatenate([spread(fire_w1), w2_t, zero, zero], axis=1),
    ])
    own = pl.pallas_call(
        leaf_kernel,
        out_shape=shape((COARSE, (2 * KV + 1) * D), f32),
        in_specs=[SMEM, VMEM, VMEM],
        out_specs=VMEM,
        name="leaf",
    )(lengths, keys, values)
    bias, phase = pl.pallas_call(
        bias_kernel,
        out_shape=(shape((HEADS, T, KEYS), f32), shape((T, KEYS), f32)),
        in_specs=[SMEM] * 4,
        out_specs=(VMEM, VMEM),
        cost_estimate=pl.CostEstimate(flops=60_000_000, bytes_accessed=2_000_000, transcendentals=50_000),
        name="bias",
    )(ctx.reshape(1), fire_w1, fire_b1, w2)
    siblings = []
    for level in range(LEVELS):
        got = exchange(own, level)
        siblings.append(got)
        if level + 1 < LEVELS:
            upper = (ctx >> level) & 1 == 1
            first = jnp.where(upper, got, own)
            second = jnp.where(upper, own, got)
            own = jnp.concatenate([first, second], 0).reshape(COARSE, 2, -1).sum(1)
    siblings = jnp.concatenate(siblings, 0)
    width = KV * D
    attended, grad_q, own_gk, own_gv, coarse_gk, coarse_gv, w_part = pl.pallas_call(
        main_kernel,
        out_shape=(
            shape((T, HEADS * D), bf16),
            shape((T, HEADS * D), bf16),
            shape((T, width), f32),
            shape((T, width), f32),
            shape((LEVELS * COARSE, width), f32),
            shape((LEVELS * COARSE, width), f32),
            shape((HEADS, D), f32),
        ),
        in_specs=[SMEM, SMEM, SMEM] + [VMEM] * 8,
        out_specs=(VMEM,) * 7,
        scratch_shapes=[
            pltpu.VMEM((HEADS, T, KEYS), f32),
            pltpu.VMEM((4 * HEADS * SUB, HIDDEN * SUB), f32),
        ],
        compiler_params=pltpu.CompilerParams(vmem_limit_bytes=32 * 2**20),
        name="attention",
    )(lengths, fire_w1, fire_b1, coef, queries, keys, values, grad_out, siblings, bias, phase)
    coarse = jnp.concatenate([coarse_gk, coarse_gv], 1)
    w_sum = w_part.reshape(2, -1)
    back = jnp.zeros((COARSE, 2 * width), f32)
    half = COARSE // 2
    for level in reversed(range(LEVELS)):
        send = coarse[level * COARSE : (level + 1) * COARSE]
        keep = 0.0
        if level + 1 < LEVELS:
            upper = (ctx >> level) & 1 == 1
            lower_part = jnp.repeat(back[:half], 2, axis=0)
            upper_part = jnp.repeat(back[half:], 2, axis=0)
            keep = jnp.where(upper, upper_part, lower_part)
            send = send + jnp.where(upper, lower_part, upper_part)
        came = exchange(jnp.concatenate([send, w_sum], 0), level)
        back = keep + came[:COARSE]
        w_sum = w_sum + came[COARSE:]
    token_live = (jnp.arange(T) < lengths[0]).astype(f32)[:, None]
    back = jnp.repeat(back, T // COARSE, axis=0)
    grad_k = ((own_gk + back[:, :width]) * token_live).astype(bf16)
    grad_v = ((own_gv + back[:, width:]) * token_live).astype(bf16)
    w_mine = w_sum.reshape(HEADS, D)
    placed = lax.dynamic_update_slice_in_dim(jnp.zeros((2 * HEADS, D), f32), w_mine, mp * HEADS, 0)
    w_all = lax.psum(placed, "mp")
    grad_w2 = w_all[:, :HIDDEN].T
    grad_w1 = w_all[:, HIDDEN : 2 * HIDDEN].sum(0)
    grad_b1 = w_all[:, 2 * HIDDEN : 3 * HIDDEN].sum(0)
    return (attended, grad_q, grad_k, grad_v, grad_w1, grad_b1, grad_w2)


def solution(mesh):
    split = P("ctx", "mp")
    return jax.shard_map(
        shards,
        mesh=mesh,
        in_specs=(split, split, split, P("ctx"), P(), P(), P(), split),
        out_specs=(split, split, split, split, P(), P(), P()),
        check_vma=False,
    )
```

time: 357 us -> 154 us (0.43)
  blocking collectives: 117 us -> 19.9 us
  starting transfers between devices: 151 us -> 68.8 us
  matrix products: 23.3 us -> 0 us
  local copies, waits for them, and re-layouts: 27 us -> 4.11 us
  Pallas kernels: 0 us -> 19.6 us
  waiting for transfers between devices: 16.6 us -> 33.2 us
  other arithmetic: 17.2 us -> 4.74 us
    psum x1, blocking collectives: 117 us -> 19.9 us  [shards(): w_all = lax.psum(placed, 'mp')]
    ppermute x40 -> x16, starting transfers between devices: 151 us -> 68.8 us  [exchange(): return lax.ppermute(value, 'ctx', pairs)]
    dot_general x10 -> x0, matrix products: 23.3 us -> none  [the longest x1 5.4 us: shards(): jnp.einsum('htk,tkm->mh', dscores, hidden, precision=lax.Precision.HIGHEST)]
    pallas_call x0 -> x3, Pallas kernels: none -> 19.6 us  [the longest x1 10.8 us: shards(): pl.pallas_call(main_kernel, out_shape=(shape((T, HEADS * D), bf16), shape...]
    ppermute x40 -> x16, waiting for transfers between devices: 16.6 us -> 33.2 us  [exchange(): return lax.ppermute(value, 'ctx', pairs)]
    max x1 -> x0, local copies, waits for them, and re-layouts: 6.75 us -> none  [shards(): hidden = jax.nn.relu(phase[:, :, None] * fire_w1 + fire_b1)]
    mul x3 -> x0, local copies, waits for them, and re-layouts: 5.15 us -> none  [the longest x1 1.76 us: shards(): dscores * phase[None]]
    max x2 -> x0, other arithmetic: 3.68 us -> none  [the longest x1 3.68 us: shards(): hidden = jax.nn.relu(phase[:, :, None] * fire_w1 + fire_b1)]
  transfers between devices with their start and end apart: 40 -> 16, of which waited for: 12 -> 15; matrix products, arithmetic and copies ran while one was open for 8% -> 1% of each run, Pallas kernels for 0% -> 5%
where the time goes in v1:
time: 154 us; the launch traced here: 153 us
  starting transfers between devices  68.8 us (45%)
  waiting for transfers between devices  33.2 us (22%)
  blocking collectives  19.9 us (13%)
  Pallas kernels  19.6 us (13%)
  other arithmetic  4.74 us (3%)
  local copies, waits for them, and re-layouts  4.11 us (3%)
  between operations  2.36 us (2%)
    ppermute x16, starting transfers between devices, exchange(): return lax.ppermute(value, 'ctx', pairs)  68.8 us
    ppermute x16, waiting for transfers between devices, exchange(): return lax.ppermute(value, 'ctx', pairs)  33.2 us
    psum x1, blocking collectives, shards(): w_all = lax.psum(placed, 'mp')  19.9 us
    pallas_call x1, Pallas kernels, shards(): pl.pallas_call(main_kernel, out_shape=(shape((T, HEADS * D), bf16), shape...  10.8 us
    pallas_call x1, Pallas kernels, shards(): pl.pallas_call(bias_kernel, out_shape=(shape((HEADS, T, KEYS), f32), shap...  7.21 us
  transfers between devices with their start and end apart: 16, of which 15 were waited for; matrix products, arithmetic and copies ran while one was open for 1% of the time, Pallas kernels for 5%

profile of v1, /device:TPU:1, one launch (start us, length us, event | category | flops | bytes accessed | tf_op | source)
XLA Modules:
  0.0 152.8 jit_solution(14067402793696859609)
XLA Ops:
  1.3 1.6 %leaf.1 = f32[32,640]{1,0:T(8,128)} custom-call(s32[1]{0:T(128)} %copy.25.len_ref, bf16[128,256]{1,0:T(8,128)(2,1)} %k_ref.3, bf16[128,256]{1,0:T(8,128)(2,1)} %v_ref.3), custom_call_target="tpu_custom_call" | custom-call | tf_op jit(solution)/shard_map/leaf/pallas_call | solution.py:173
  3.0 4.0 %collective-permute-start = (f32[32,640]{1,0:T(8,128)}, f32[32,640]{1,0:T(8,128)S(1)}, u32[]{:S(2)}, u32[]{:S(2)}) collective-permute-start(f32[32,640]{1,0:T(8,128)} %leaf.1), channel_id=1, source_target_pairs={{0,2},{2,0},{4,6},{6,4},{8,10},{10,8},{12,14},{14,12},{16,18},{18,... | collective-permute-start | bytes 245768 | tf_op jit(solution)/shard_map/ppermute | solution.py:34
  7.0 2.0 %collective-permute-done = f32[32,640]{1,0:T(8,128)S(1)} collective-permute-done((f32[32,640]{1,0:T(8,128)}, f32[32,640]{1,0:T(8,128)S(1)}, u32[]{:S(2)}, u32[]{:S(2)}) %collective-permute-start) | collective-permute-done | bytes 81952 | tf_op jit(solution)/shard_map/ppermute | solution.py:34
  9.0 0.9 broadcast_select_fusion.13
  10.1 0.2 reduce_sum.81
  10.3 4.4 %collective-permute-start.1 = (f32[32,640]{1,0:T(8,128)S(1)}, f32[32,640]{1,0:T(8,128)S(1)}, u32[]{:S(2)}, u32[]{:S(2)}) collective-permute-start(f32[32,640]{1,0:T(8,128)S(1)} %reduce_sum.81), channel_id=1, source_target_pairs={{0,4},{2,6},{4,0},{6,2},{8,12},{10,14},{12,8},{14,10},{16,20},{18,... | collective-permute-start | bytes 245768 | tf_op jit(solution)/shard_map/ppermute | solution.py:34
  14.6 1.9 %collective-permute-done.1 = f32[32,640]{1,0:T(8,128)S(1)} collective-permute-done((f32[32,640]{1,0:T(8,128)S(1)}, f32[32,640]{1,0:T(8,128)S(1)}, u32[]{:S(2)}, u32[]{:S(2)}) %collective-permute-start.1) | collective-permute-done | bytes 81952 | tf_op jit(solution)/shard_map/ppermute | solution.py:34
  16.7 0.2 reduce_sum.82
  16.9 5.9 %collective-permute-start.2 = (f32[32,640]{1,0:T(8,128)S(1)}, f32[32,640]{1,0:T(8,128)S(1)}, u32[]{:S(2)}, u32[]{:S(2)}) collective-permute-start(f32[32,640]{1,0:T(8,128)S(1)} %reduce_sum.82), channel_id=1, source_target_pairs={{0,12},{2,14},{4,8},{6,10},{8,4},{10,6},{12,0},{14,2},{16,28},{18,... | collective-permute-start | bytes 245768 | tf_op jit(solution)/shard_map/ppermute | solution.py:34
  22.8 2.2 %collective-permute-done.2 = f32[32,640]{1,0:T(8,128)S(1)} collective-permute-done((f32[32,640]{1,0:T(8,128)S(1)}, f32[32,640]{1,0:T(8,128)S(1)}, u32[]{:S(2)}, u32[]{:S(2)}) %collective-permute-start.2) | collective-permute-done | bytes 81952 | tf_op jit(solution)/shard_map/ppermute | solution.py:34
  25.2 0.2 reduce_sum.83
  25.4 3.1 %collective-permute-start.3 = (f32[32,640]{1,0:T(8,128)S(1)}, f32[32,640]{1,0:T(8,128)S(1)}, u32[]{:S(2)}, u32[]{:S(2)}) collective-permute-start(f32[32,640]{1,0:T(8,128)S(1)} %reduce_sum.83), channel_id=1, source_target_pairs={{0,16},{2,18},{4,20},{6,22},{8,24},{10,26},{12,28},{14,30},{16,0},... | collective-permute-start | bytes 245768 | tf_op jit(solution)/shard_map/ppermute | solution.py:34
  28.7 1.9 %collective-permute-done.3 = f32[32,640]{1,0:T(8,128)S(1)} collective-permute-done((f32[32,640]{1,0:T(8,128)S(1)}, f32[32,640]{1,0:T(8,128)S(1)}, u32[]{:S(2)}, u32[]{:S(2)}) %collective-permute-start.3) | collective-permute-done | bytes 81952 | tf_op jit(solution)/shard_map/ppermute | solution.py:34
  30.7 0.2 reduce_sum.84
  30.9 4.4 %collective-permute-start.4 = (f32[32,640]{1,0:T(8,128)S(1)}, f32[32,640]{1,0:T(8,128)S(1)}, u32[]{:S(2)}, u32[]{:S(2)}) collective-permute-start(f32[32,640]{1,0:T(8,128)S(1)} %reduce_sum.84), channel_id=1, source_target_pairs={{0,48},{2,50},{4,52},{6,54},{8,56},{10,58},{12,60},{14,62},{16,32}... | collective-permute-start | bytes 245768 | tf_op jit(solution)/shard_map/ppermute | solution.py:34
  35.4 2.0 %collective-permute-done.4 = f32[32,640]{1,0:T(8,128)S(1)} collective-permute-done((f32[32,640]{1,0:T(8,128)S(1)}, f32[32,640]{1,0:T(8,128)S(1)}, u32[]{:S(2)}, u32[]{:S(2)}) %collective-permute-start.4) | collective-permute-done | bytes 81952 | tf_op jit(solution)/shard_map/ppermute | solution.py:34
  37.5 0.2 reduce_sum.85
  37.8 4.1 %collective-permute-start.5 = (f32[32,640]{1,0:T(8,128)S(1)}, f32[32,640]{1,0:T(8,128)S(1)}, u32[]{:S(2)}, u32[]{:S(2)}) collective-permute-start(f32[32,640]{1,0:T(8,128)S(1)} %reduce_sum.85), channel_id=1, source_target_pairs={{0,64},{2,66},{4,68},{6,70},{8,72},{10,74},{12,76},{14,78},{16,80}... | collective-permute-start | bytes 245768 | tf_op jit(solution)/shard_map/ppermute | solution.py:34
  42.0 1.7 %collective-permute-done.5 = f32[32,640]{1,0:T(8,128)S(1)} collective-permute-done((f32[32,640]{1,0:T(8,128)S(1)}, f32[32,640]{1,0:T(8,128)S(1)}, u32[]{:S(2)}, u32[]{:S(2)}) %collective-permute-start.5) | collective-permute-done | bytes 81952 | tf_op jit(solution)/shard_map/ppermute | solution.py:34
  43.8 0.2 reduce_sum.86
  44.1 5.8 %collective-permute-start.6 = (f32[32,640]{1,0:T(8,128)S(1)}, f32[32,640]{1,0:T(8,128)S(1)}, u32[]{:S(2)}, u32[]{:S(2)}) collective-permute-start(f32[32,640]{1,0:T(8,128)S(1)} %reduce_sum.86), channel_id=1, source_target_pairs={{0,128},{2,130},{4,132},{6,134},{8,136},{10,138},{12,140},{14,142}... | collective-permute-start | bytes 245768 | tf_op jit(solution)/shard_map/ppermute | solution.py:34
  49.9 0.7 copy.15.w2_ref
  50.6 7.2 %bias.1 = (f32[8,128,384]{2,1,0:T(8,128)}, f32[128,384]{1,0:T(8,128)}) custom-call(s32[1]{0:T(128)} %bitcast.3.ctx_ref, f32[32]{0:T(128)} %w1_ref.3, f32[32]{0:T(128)} %b1_ref.3, f32[32,8]{1,0:T(8,128)} %copy.15.w2_ref), custom_call_target="tpu_custom_call" | custom-call | flops 60000000 | bytes 2000000 | tf_op jit(solution)/shard_map/bias/pallas_call | solution.py:180
  57.9 0.2 reduce_sum.87
  58.1 6.4 %collective-permute-start.7 = (f32[32,640]{1,0:T(8,128)S(1)}, f32[32,640]{1,0:T(8,128)S(1)}, u32[]{:S(2)}, u32[]{:S(2)}) collective-permute-start(f32[32,640]{1,0:T(8,128)S(1)} %reduce_sum.87), channel_id=1, source_target_pairs={{0,384},{2,386},{4,388},{6,390},{8,392},{10,394},{12,396},{14,398}... | collective-permute-start | bytes 245768 | tf_op jit(solution)/shard_map/ppermute | solution.py:34
  64.6 2.7 %collective-permute-done.7 = f32[32,640]{1,0:T(8,128)S(1)} collective-permute-done((f32[32,640]{1,0:T(8,128)S(1)}, f32[32,640]{1,0:T(8,128)S(1)}, u32[]{:S(2)}, u32[]{:S(2)}) %collective-permute-start.7) | collective-permute-done | bytes 81952 | tf_op jit(solution)/shard_map/ppermute | solution.py:34
  67.3 1.4 copy-done.1
  68.7 10.8 %attention.1 = (bf16[128,1024]{1,0:T(8,128)(2,1)}, bf16[128,1024]{1,0:T(8,128)(2,1)}, f32[128,256]{1,0:T(8,128)S(1)}, f32[128,256]{1,0:T(8,128)S(1)}, f32[256,25...) custom-call(s32[1]{0:T(128)} %copy.25.len_ref, f32[32]{0:T(128)S(1)} %copy-done.8, f32[32]{0:T(128)S(1)} %copy-done.10, ...), custom_call_target="tpu_custom_call" | custom-call | tf_op jit(solution)/shard_map/attention/pallas_call | solution.py:199
  79.6 4.6 %collective-permute-start.8 = (f32[34,512]{1,0:T(8,128)S(1)}, f32[34,512]{1,0:T(8,128)S(1)}, u32[]{:S(2)}, u32[]{:S(2)}) collective-permute-start(f32[34,512]{1,0:T(8,128)S(1)} %pad_maximum_fusion.7), channel_id=1, source_target_pairs={{0,384},{2,386},{4,388},{6,390},{8,392},{10,394},{12,396},{14,398}... | collective-permute-start | bytes 208904 | tf_op jit(solution)/shard_map/ppermute | solution.py:34
  84.2 2.8 %collective-permute-done.8 = f32[34,512]{1,0:T(8,128)S(1)} collective-permute-done((f32[34,512]{1,0:T(8,128)S(1)}, f32[34,512]{1,0:T(8,128)S(1)}, u32[]{:S(2)}, u32[]{:S(2)}) %collective-permute-start.8) | collective-permute-done | bytes 69664 | tf_op jit(solution)/shard_map/ppermute | solution.py:34
  87.1 3.1 %collective-permute-start.9 = (f32[34,512]{1,0:T(8,128)S(1)}, f32[34,512]{1,0:T(8,128)S(1)}, u32[]{:S(2)}, u32[]{:S(2)}) collective-permute-start(f32[34,512]{1,0:T(8,128)S(1)} %pad_maximum_fusion.8), channel_id=1, source_target_pairs={{0,128},{2,130},{4,132},{6,134},{8,136},{10,138},{12,140},{14,142}... | collective-permute-start | bytes 208904 | tf_op jit(solution)/shard_map/ppermute | solution.py:34
  90.4 2.9 %collective-permute-done.9 = f32[34,512]{1,0:T(8,128)S(1)} collective-permute-done((f32[34,512]{1,0:T(8,128)S(1)}, f32[34,512]{1,0:T(8,128)S(1)}, u32[]{:S(2)}, u32[]{:S(2)}) %collective-permute-start.9) | collective-permute-done | bytes 69664 | tf_op jit(solution)/shard_map/ppermute | solution.py:34
  93.4 3.3 %collective-permute-start.10 = (f32[34,512]{1,0:T(8,128)S(1)}, f32[34,512]{1,0:T(8,128)S(1)}, u32[]{:S(2)}, u32[]{:S(2)}) collective-permute-start(f32[34,512]{1,0:T(8,128)S(1)} %pad_maximum_fusion.9), channel_id=1, source_target_pairs={{0,64},{2,66},{4,68},{6,70},{8,72},{10,74},{12,76},{14,78},{16,80}... | collective-permute-start | bytes 208904 | tf_op jit(solution)/shard_map/ppermute | solution.py:34
  96.8 1.8 %collective-permute-done.10 = f32[34,512]{1,0:T(8,128)S(1)} collective-permute-done((f32[34,512]{1,0:T(8,128)S(1)}, f32[34,512]{1,0:T(8,128)S(1)}, u32[]{:S(2)}, u32[]{:S(2)}) %collective-permute-start.10) | collective-permute-done | bytes 69664 | tf_op jit(solution)/shard_map/ppermute | solution.py:34
  98.7 4.4 %collective-permute-start.11 = (f32[34,512]{1,0:T(8,128)S(1)}, f32[34,512]{1,0:T(8,128)S(1)}, u32[]{:S(2)}, u32[]{:S(2)}) collective-permute-start(f32[34,512]{1,0:T(8,128)S(1)} %pad_maximum_fusion.10), channel_id=1, source_target_pairs={{0,48},{2,50},{4,52},{6,54},{8,56},{10,58},{12,60},{14,62},{16,32}... | collective-permute-start | bytes 208904 | tf_op jit(solution)/shard_map/ppermute | solution.py:34
  103.2 1.9 %collective-permute-done.11 = f32[34,512]{1,0:T(8,128)S(1)} collective-permute-done((f32[34,512]{1,0:T(8,128)S(1)}, f32[34,512]{1,0:T(8,128)S(1)}, u32[]{:S(2)}, u32[]{:S(2)}) %collective-permute-start.11) | collective-permute-done | bytes 69664 | tf_op jit(solution)/shard_map/ppermute | solution.py:34
  105.3 1.9 %collective-permute-start.12 = (f32[34,512]{1,0:T(8,128)S(1)}, f32[34,512]{1,0:T(8,128)S(1)}, u32[]{:S(2)}, u32[]{:S(2)}) collective-permute-start(f32[34,512]{1,0:T(8,128)S(1)} %pad_maximum_fusion.11), channel_id=1, source_target_pairs={{0,16},{2,18},{4,20},{6,22},{8,24},{10,26},{12,28},{14,30},{16,0},... | collective-permute-start | bytes 208904 | tf_op jit(solution)/shard_map/ppermute | solution.py:34
  107.3 3.4 %collective-permute-done.12 = f32[34,512]{1,0:T(8,128)S(1)} collective-permute-done((f32[34,512]{1,0:T(8,128)S(1)}, f32[34,512]{1,0:T(8,128)S(1)}, u32[]{:S(2)}, u32[]{:S(2)}) %collective-permute-start.12) | collective-permute-done | bytes 69664 | tf_op jit(solution)/shard_map/ppermute | solution.py:34
  110.9 6.2 %collective-permute-start.13 = (f32[34,512]{1,0:T(8,128)S(1)}, f32[34,512]{1,0:T(8,128)S(1)}, u32[]{:S(2)}, u32[]{:S(2)}) collective-permute-start(f32[34,512]{1,0:T(8,128)S(1)} %pad_maximum_fusion.12), channel_id=1, source_target_pairs={{0,12},{2,14},{4,8},{6,10},{8,4},{10,6},{12,0},{14,2},{16,28},{18,... | collective-permute-start | bytes 208904 | tf_op jit(solution)/shard_map/ppermute | solution.py:34
  117.2 1.8 %collective-permute-done.13 = f32[34,512]{1,0:T(8,128)S(1)} collective-permute-done((f32[34,512]{1,0:T(8,128)S(1)}, f32[34,512]{1,0:T(8,128)S(1)}, u32[]{:S(2)}, u32[]{:S(2)}) %collective-permute-start.13) | collective-permute-done | bytes 69664 | tf_op jit(solution)/shard_map/ppermute | solution.py:34
  119.2 3.6 %collective-permute-start.14 = (f32[34,512]{1,0:T(8,128)S(1)}, f32[34,512]{1,0:T(8,128)S(1)}, u32[]{:S(2)}, u32[]{:S(2)}) collective-permute-start(f32[34,512]{1,0:T(8,128)S(1)} %pad_maximum_fusion.13), channel_id=1, source_target_pairs={{0,4},{2,6},{4,0},{6,2},{8,12},{10,14},{12,8},{14,10},{16,20},{18,... | collective-permute-start | bytes 208904 | tf_op jit(solution)/shard_map/ppermute | solution.py:34
  122.9 2.4 %collective-permute-done.14 = f32[34,512]{1,0:T(8,128)S(1)} collective-permute-done((f32[34,512]{1,0:T(8,128)S(1)}, f32[34,512]{1,0:T(8,128)S(1)}, u32[]{:S(2)}, u32[]{:S(2)}) %collective-permute-start.14) | collective-permute-done | bytes 69664 | tf_op jit(solution)/shard_map/ppermute | solution.py:34
  125.5 3.5 %collective-permute-start.15 = (f32[34,512]{1,0:T(8,128)S(1)}, f32[34,512]{1,0:T(8,128)S(1)}, u32[]{:S(2)}, u32[]{:S(2)}) collective-permute-start(f32[34,512]{1,0:T(8,128)S(1)} %pad_maximum_fusion.14), channel_id=1, source_target_pairs={{0,2},{2,0},{4,6},{6,4},{8,10},{10,8},{12,14},{14,12},{16,18},{18,... | collective-permute-start | bytes 208904 | tf_op jit(solution)/shard_map/ppermute | solution.py:34
  129.0 1.7 %collective-permute-done.15 = f32[34,512]{1,0:T(8,128)S(1)} collective-permute-done((f32[34,512]{1,0:T(8,128)S(1)}, f32[34,512]{1,0:T(8,128)S(1)}, u32[]{:S(2)}, u32[]{:S(2)}) %collective-permute-start.15) | collective-permute-done | bytes 69664 | tf_op jit(solution)/shard_map/ppermute | solution.py:34
  130.8 19.9 %psum.7 = f32[16,128]{1,0:T(8,128)S(1)} all-reduce(f32[16,128]{1,0:T(8,128)S(1)} %constant_dynamic-update-slice_fusion.10), channel_id=1, replica_groups=mesh['ctx'=256,'mp'=2] {'mp'}, use_global_device_ids=true, to_apply=%region_7.8 | all-reduce | flops 2048 | bytes 16384 | tf_op jit(solution)/shard_map/psum | solution.py:241
  150.7 1.1 slice_reduce_fusion
  151.9 0.1 reshape.105
  152.0 0.7 fusion.1
  (126 shorter events, 2.6 us)
Async XLA Ops:
  0.6 34.7 %copy-start = (f32[32,16]{0,1:T(8,128)S(1)}, f32[32,16]{0,1:T(8,128)}, u32[]{:S(2)}) copy-start(f32[32,16]{0,1:T(8,128)} %param.14) | copy-start | bytes 6148
  3.0 6.1 %collective-permute-start = (f32[32,640]{1,0:T(8,128)}, f32[32,640]{1,0:T(8,128)S(1)}, u32[]{:S(2)}, u32[]{:S(2)}) collective-permute-start(f32[32,640]{1,0:T(8,128)} %leaf.1), channel_id=1, source_target_pairs={{0,2},{2,0},{4,6},{6,4},{8,10},{10,8},{12,14},{14,12},{16,18},{18,... | collective-permute-start | bytes 245768 | tf_op jit(solution)/shard_map/ppermute | solution.py:34
  9.9 18.7 %copy-start.7 = (f32[32]{0:T(128)S(1)}, f32[32]{0:T(128)}, u32[]{:S(2)}) copy-start(f32[32]{0:T(128)} %w1_ref.3) | copy-start | bytes 388
  10.0 18.7 %copy-start.9 = (f32[32]{0:T(128)S(1)}, f32[32]{0:T(128)}, u32[]{:S(2)}) copy-start(f32[32]{0:T(128)} %b1_ref.3) | copy-start | bytes 388
  10.3 6.3 %collective-permute-start.1 = (f32[32,640]{1,0:T(8,128)S(1)}, f32[32,640]{1,0:T(8,128)S(1)}, u32[]{:S(2)}, u32[]{:S(2)}) collective-permute-start(f32[32,640]{1,0:T(8,128)S(1)} %reduce_sum.81), channel_id=1, source_target_pairs={{0,4},{2,6},{4,0},{6,2},{8,12},{10,14},{12,8},{14,10},{16,20},{18,... | collective-permute-start | bytes 245768 | tf_op jit(solution)/shard_map/ppermute | solution.py:34
  16.9 8.2 %collective-permute-start.2 = (f32[32,640]{1,0:T(8,128)S(1)}, f32[32,640]{1,0:T(8,128)S(1)}, u32[]{:S(2)}, u32[]{:S(2)}) collective-permute-start(f32[32,640]{1,0:T(8,128)S(1)} %reduce_sum.82), channel_id=1, source_target_pairs={{0,12},{2,14},{4,8},{6,10},{8,4},{10,6},{12,0},{14,2},{16,28},{18,... | collective-permute-start | bytes 245768 | tf_op jit(solution)/shard_map/ppermute | solution.py:34
  25.4 5.2 %collective-permute-start.3 = (f32[32,640]{1,0:T(8,128)S(1)}, f32[32,640]{1,0:T(8,128)S(1)}, u32[]{:S(2)}, u32[]{:S(2)}) collective-permute-start(f32[32,640]{1,0:T(8,128)S(1)} %reduce_sum.83), channel_id=1, source_target_pairs={{0,16},{2,18},{4,20},{6,22},{8,24},{10,26},{12,28},{14,30},{16,0},... | collective-permute-start | bytes 245768 | tf_op jit(solution)/shard_map/ppermute | solution.py:34
  30.9 6.4 %collective-permute-start.4 = (f32[32,640]{1,0:T(8,128)S(1)}, f32[32,640]{1,0:T(8,128)S(1)}, u32[]{:S(2)}, u32[]{:S(2)}) collective-permute-start(f32[32,640]{1,0:T(8,128)S(1)} %reduce_sum.84), channel_id=1, source_target_pairs={{0,48},{2,50},{4,52},{6,54},{8,56},{10,58},{12,60},{14,62},{16,32}... | collective-permute-start | bytes 245768 | tf_op jit(solution)/shard_map/ppermute | solution.py:34
  37.7 29.6 %copy-start.2 = (bf16[128,1024]{1,0:T(8,128)(2,1)S(1)}, bf16[128,1024]{1,0:T(8,128)(2,1)}, u32[]{:S(2)}) copy-start(bf16[128,1024]{1,0:T(8,128)(2,1)} %q_ref.1) | copy-start | bytes 786436
  37.7 29.6 %copy-start.3 = (bf16[128,1024]{1,0:T(8,128)(2,1)S(1)}, bf16[128,1024]{1,0:T(8,128)(2,1)}, u32[]{:S(2)}) copy-start(bf16[128,1024]{1,0:T(8,128)(2,1)} %g_ref.1) | copy-start | bytes 786436
  37.7 29.6 %copy-start.4 = (bf16[128,256]{1,0:T(8,128)(2,1)S(1)}, bf16[128,256]{1,0:T(8,128)(2,1)}, u32[]{:S(2)}) copy-start(bf16[128,256]{1,0:T(8,128)(2,1)} %k_ref.3) | copy-start | bytes 196612
  37.7 29.6 %copy-start.5 = (bf16[128,256]{1,0:T(8,128)(2,1)S(1)}, bf16[128,256]{1,0:T(8,128)(2,1)}, u32[]{:S(2)}) copy-start(bf16[128,256]{1,0:T(8,128)(2,1)} %v_ref.3) | copy-start | bytes 196612
  37.7 29.6 %copy-start.8 = (f32[32]{0:T(128)S(1)}, f32[32]{0:T(128)}, u32[]{:S(2)}) copy-start(f32[32]{0:T(128)} %w1_ref.3) | copy-start | bytes 388
  37.7 29.6 %copy-start.10 = (f32[32]{0:T(128)S(1)}, f32[32]{0:T(128)}, u32[]{:S(2)}) copy-start(f32[32]{0:T(128)} %b1_ref.3) | copy-start | bytes 388
  37.8 6.0 %collective-permute-start.5 = (f32[32,640]{1,0:T(8,128)S(1)}, f32[32,640]{1,0:T(8,128)S(1)}, u32[]{:S(2)}, u32[]{:S(2)}) collective-permute-start(f32[32,640]{1,0:T(8,128)S(1)} %reduce_sum.85), channel_id=1, source_target_pairs={{0,64},{2,66},{4,68},{6,70},{8,72},{10,74},{12,76},{14,78},{16,80}... | collective-permute-start | bytes 245768 | tf_op jit(solution)/shard_map/ppermute | solution.py:34
  44.1 13.7 %collective-permute-start.6 = (f32[32,640]{1,0:T(8,128)S(1)}, f32[32,640]{1,0:T(8,128)S(1)}, u32[]{:S(2)}, u32[]{:S(2)}) collective-permute-start(f32[32,640]{1,0:T(8,128)S(1)} %reduce_sum.86), channel_id=1, source_target_pairs={{0,128},{2,130},{4,132},{6,134},{8,136},{10,138},{12,140},{14,142}... | collective-permute-start | bytes 245768 | tf_op jit(solution)/shard_map/ppermute | solution.py:34
  57.8 9.5 %copy-start.6 = (f32[128,384]{1,0:T(8,128)S(1)}, f32[128,384]{1,0:T(8,128)}, u32[]{:S(2)}) copy-start(f32[128,384]{1,0:T(8,128)} %get-tuple-element.17.phase_ref) | copy-start | bytes 589828
  58.1 9.1 %collective-permute-start.7 = (f32[32,640]{1,0:T(8,128)S(1)}, f32[32,640]{1,0:T(8,128)S(1)}, u32[]{:S(2)}, u32[]{:S(2)}) collective-permute-start(f32[32,640]{1,0:T(8,128)S(1)} %reduce_sum.87), channel_id=1, source_target_pairs={{0,384},{2,386},{4,388},{6,390},{8,392},{10,394},{12,396},{14,398}... | collective-permute-start | bytes 245768 | tf_op jit(solution)/shard_map/ppermute | solution.py:34
  67.3 1.4 copy-start.1
  79.6 7.4 %collective-permute-start.8 = (f32[34,512]{1,0:T(8,128)S(1)}, f32[34,512]{1,0:T(8,128)S(1)}, u32[]{:S(2)}, u32[]{:S(2)}) collective-permute-start(f32[34,512]{1,0:T(8,128)S(1)} %pad_maximum_fusion.7), channel_id=1, source_target_pairs={{0,384},{2,386},{4,388},{6,390},{8,392},{10,394},{12,396},{14,398}... | collective-permute-start | bytes 208904 | tf_op jit(solution)/shard_map/ppermute | solution.py:34
  87.1 6.1 %collective-permute-start.9 = (f32[34,512]{1,0:T(8,128)S(1)}, f32[34,512]{1,0:T(8,128)S(1)}, u32[]{:S(2)}, u32[]{:S(2)}) collective-permute-start(f32[34,512]{1,0:T(8,128)S(1)} %pad_maximum_fusion.8), channel_id=1, source_target_pairs={{0,128},{2,130},{4,132},{6,134},{8,136},{10,138},{12,140},{14,142}... | collective-permute-start | bytes 208904 | tf_op jit(solution)/shard_map/ppermute | solution.py:34
  93.4 5.2 %collective-permute-start.10 = (f32[34,512]{1,0:T(8,128)S(1)}, f32[34,512]{1,0:T(8,128)S(1)}, u32[]{:S(2)}, u32[]{:S(2)}) collective-permute-start(f32[34,512]{1,0:T(8,128)S(1)} %pad_maximum_fusion.9), channel_id=1, source_target_pairs={{0,64},{2,66},{4,68},{6,70},{8,72},{10,74},{12,76},{14,78},{16,80}... | collective-permute-start | bytes 208904 | tf_op jit(solution)/shard_map/ppermute | solution.py:34
  98.7 6.4 %collective-permute-start.11 = (f32[34,512]{1,0:T(8,128)S(1)}, f32[34,512]{1,0:T(8,128)S(1)}, u32[]{:S(2)}, u32[]{:S(2)}) collective-permute-start(f32[34,512]{1,0:T(8,128)S(1)} %pad_maximum_fusion.10), channel_id=1, source_target_pairs={{0,48},{2,50},{4,52},{6,54},{8,56},{10,58},{12,60},{14,62},{16,32}... | collective-permute-start | bytes 208904 | tf_op jit(solution)/shard_map/ppermute | solution.py:34
  105.3 5.5 %collective-permute-start.12 = (f32[34,512]{1,0:T(8,128)S(1)}, f32[34,512]{1,0:T(8,128)S(1)}, u32[]{:S(2)}, u32[]{:S(2)}) collective-permute-start(f32[34,512]{1,0:T(8,128)S(1)} %pad_maximum_fusion.11), channel_id=1, source_target_pairs={{0,16},{2,18},{4,20},{6,22},{8,24},{10,26},{12,28},{14,30},{16,0},... | collective-permute-start | bytes 208904 | tf_op jit(solution)/shard_map/ppermute | solution.py:34
  110.9 8.1 %collective-permute-start.13 = (f32[34,512]{1,0:T(8,128)S(1)}, f32[34,512]{1,0:T(8,128)S(1)}, u32[]{:S(2)}, u32[]{:S(2)}) collective-permute-start(f32[34,512]{1,0:T(8,128)S(1)} %pad_maximum_fusion.12), channel_id=1, source_target_pairs={{0,12},{2,14},{4,8},{6,10},{8,4},{10,6},{12,0},{14,2},{16,28},{18,... | collective-permute-start | bytes 208904 | tf_op jit(solution)/shard_map/ppermute | solution.py:34
  119.2 6.1 %collective-permute-start.14 = (f32[34,512]{1,0:T(8,128)S(1)}, f32[34,512]{1,0:T(8,128)S(1)}, u32[]{:S(2)}, u32[]{:S(2)}) collective-permute-start(f32[34,512]{1,0:T(8,128)S(1)} %pad_maximum_fusion.13), channel_id=1, source_target_pairs={{0,4},{2,6},{4,0},{6,2},{8,12},{10,14},{12,8},{14,10},{16,20},{18,... | collective-permute-start | bytes 208904 | tf_op jit(solution)/shard_map/ppermute | solution.py:34
  125.5 5.3 %collective-permute-start.15 = (f32[34,512]{1,0:T(8,128)S(1)}, f32[34,512]{1,0:T(8,128)S(1)}, u32[]{:S(2)}, u32[]{:S(2)}) collective-permute-start(f32[34,512]{1,0:T(8,128)S(1)} %pad_maximum_fusion.14), channel_id=1, source_target_pairs={{0,2},{2,0},{4,6},{6,4},{8,10},{10,8},{12,14},{14,12},{16,18},{18,... | collective-permute-start | bytes 208904 | tf_op jit(solution)/shard_map/ppermute | solution.py:34

commit v2 on v1

v2 whole, which is shorter than its diff:
```python
import jax
import jax.numpy as jnp
from jax import lax
from jax.experimental import pallas as pl
from jax.experimental.pallas import tpu as pltpu
from jax.sharding import PartitionSpec as P

D = 128
COARSE = 32
T = 128
LEVELS = 8
KEYS = T + LEVELS * COARSE
HIDDEN = 32
HEADS = 8
KV = 2
GROUP = HEADS // KV
SUB = 8
CHUNK = 8
SIDE = 16
WIDTH = KV * D
LEVEL_TOKENS = float(T * 2**LEVELS)
SCALE = D ** (-0.5)
MASKS = (1, 2, 6, 8, 24, 32, 64, 192)
NT = (((1,), (1,)), ((), ()))
TN = (((0,), (0,)), ((), ()))
VMEM = pl.BlockSpec(memory_space=pltpu.VMEM)
SMEM = pl.BlockSpec(memory_space=pltpu.SMEM)


def dot(a, b, dims=(((1,), (0,)), ((), ()))):
    return lax.dot_general(a, b, dims, preferred_element_type=jnp.float32)


def exchange(value, level):
    pairs = [(i, i ^ MASKS[level]) for i in range(lax.axis_size("ctx"))]
    return lax.ppermute(value, "ctx", pairs)


def leaf_kernel(len_ref, k_ref, v_ref, fine_ref, wide_ref):
    for ref, run in ((fine_ref, T // COARSE), (wide_ref, T // CHUNK)):
        row = lax.broadcasted_iota(jnp.int32, (T // run, T), 0)
        tok = lax.broadcasted_iota(jnp.int32, (T // run, T), 1)
        member = jnp.where((tok // run == row) & (tok < len_ref[0]), 1.0, 0.0)
        member_b = member.astype(jnp.bfloat16)
        ref[:, :WIDTH] = dot(member_b, k_ref[...])
        ref[:, WIDTH : 2 * WIDTH] = dot(member_b, v_ref[...])
        count = jnp.sum(member, axis=1, keepdims=True)
        ref[:, 2 * WIDTH :] = jnp.broadcast_to(count, (T // run, D))


def bias_kernel(ctx_ref, w1_ref, b1_ref, w2_ref, bias_ref, phase_ref):
    ctx = ctx_ref[0]
    col = lax.broadcasted_iota(jnp.int32, (1, KEYS), 1)
    level = (col - T) // COARSE
    pos = col.astype(jnp.float32)
    for k in range(LEVELS):
        run = 2**k * T // COARSE
        start = ((ctx >> k) ^ 1) * 2**k * T - ctx * T
        inside = (col - T - k * COARSE) * run
        here = (start + inside).astype(jnp.float32) + (run - 1) / 2.0
        pos = jnp.where((col >= T) & (level == k), here, pos)
    top = jnp.log1p(jnp.full((1, KEYS), LEVEL_TOKENS, jnp.float32))
    weight = w2_ref[...]
    weight_high = weight.astype(jnp.bfloat16)
    weight_low = (weight - weight_high.astype(jnp.float32)).astype(jnp.bfloat16)
    weight_both = jnp.concatenate([weight_high, weight_low], axis=0)

    def body(i, carry):
        rows = pl.ds(pl.multiple_of(i * SUB, SUB), SUB)
        row = i * SUB + lax.broadcasted_iota(jnp.int32, (SUB, KEYS), 0)
        phase = jnp.log1p(jnp.abs(row.astype(jnp.float32) - pos)) / top
        phase_ref[rows, :] = phase
        hidden = [jnp.maximum(phase * w1_ref[m] + b1_ref[m], 0.0) for m in range(HIDDEN)]
        hidden = jnp.concatenate(hidden, axis=0)
        high = hidden.astype(jnp.bfloat16)
        low = (hidden - high.astype(jnp.float32)).astype(jnp.bfloat16)
        with_high = dot(weight_both, high)
        bias = with_high[: HEADS * SUB] + with_high[HEADS * SUB :] + dot(weight_high, low)
        for h in range(HEADS):
            bias_ref[h, rows, :] = bias[h * SUB : (h + 1) * SUB]
        return carry

    lax.fori_loop(0, T // SUB, body, 0)


def main_kernel(
    len_ref, q_ref, k_ref, v_ref, g_ref, sib_ref, bias_ref,
    out_ref, gq_ref, own_ref, coarse_ref, ds_ref,
):
    length = len_ref[0]
    count = sib_ref[:, 2 * KV * D :]
    safe = jnp.maximum(count, 1.0)
    count_t = jnp.concatenate([count[:T].T[:1], count[T:].T[:1]], axis=1)
    token_live = lax.broadcasted_iota(jnp.int32, (1, T), 1) < length
    live = jnp.concatenate([token_live.astype(jnp.float32), count_t], axis=1) > 0.0
    row_live = lax.broadcasted_iota(jnp.int32, (T, 1), 0) < length
    row_live_f = row_live.astype(jnp.float32)
    for j in range(KV):
        cols = slice(j * D, (j + 1) * D)
        vcols = slice((KV + j) * D, (KV + j + 1) * D)
        keys = jnp.concatenate([k_ref[:, cols], (sib_ref[:, cols] / safe).astype(jnp.bfloat16)], axis=0)
        values = jnp.concatenate([v_ref[:, cols], (sib_ref[:, vcols] / safe).astype(jnp.bfloat16)], axis=0)
        key_grads = jnp.zeros((KEYS, D), jnp.float32)
        value_grads = jnp.zeros((KEYS, D), jnp.float32)
        for g in range(GROUP):
            h = j * GROUP + g
            hcols = slice(h * D, (h + 1) * D)
            query = q_ref[:, hcols]
            scores = dot(query, keys, NT) * SCALE + bias_ref[h]
            scores = jnp.where(live, scores, -jnp.inf)
            top = jnp.max(scores, axis=1, keepdims=True)
            weights = jnp.exp(scores - top)
            probs = weights / jnp.sum(weights, axis=1, keepdims=True)
            probs_b = probs.astype(jnp.bfloat16)
            out_ref[:, hcols] = (dot(probs_b, values) * row_live_f).astype(jnp.bfloat16)
            grad = g_ref[:, hcols]
            grad = jnp.where(row_live, grad, jnp.zeros_like(grad))
            dprobs = dot(grad, values, NT)
            dscores = probs * (dprobs - jnp.sum(probs * dprobs, axis=1, keepdims=True))
            ds_ref[h] = dscores
            dscores_b = dscores.astype(jnp.bfloat16)
            gq_ref[:, hcols] = (SCALE * dot(dscores_b, keys)).astype(jnp.bfloat16)
            key_grads = key_grads + dot(dscores_b, query, TN)
            value_grads = value_grads + dot(probs_b, grad, TN)
        key_grads = key_grads * SCALE
        own_ref[:, cols] = key_grads[:T]
        own_ref[:, vcols] = value_grads[:T]
        coarse_ref[:, cols] = key_grads[T:] / safe
        coarse_ref[:, vcols] = value_grads[T:] / safe


def weight_kernel(w1_ref, b1_ref, coef_ref, ds_ref, phase_ref, w_ref, acc_ref):
    acc_ref[...] = jnp.zeros_like(acc_ref)

    def body(i, carry):
        rows = pl.ds(i * SUB, SUB)
        phase = phase_ref[rows, :]
        parts = [ds_ref[h, rows, :] for h in range(HEADS)]
        parts = jnp.concatenate(parts + [p * phase for p in parts], axis=0)
        high = parts.astype(jnp.bfloat16)
        low = (parts - high.astype(jnp.float32)).astype(jnp.bfloat16)
        both = jnp.concatenate([high, low], axis=0)
        active = [
            jnp.where(phase * w1_ref[m] + b1_ref[m] > 0.0, 1.0, 0.0) for m in range(HIDDEN)
        ]
        active = jnp.concatenate(active, axis=0).astype(jnp.bfloat16)
        acc_ref[...] += dot(both, active, NT)
        return carry

    lax.fori_loop(0, T // SUB, body, 0)
    acc = acc_ref[...]
    rows = 2 * HEADS * SUB
    acc = acc[:rows] + acc[rows:]
    sub_row = lax.broadcasted_iota(jnp.int32, acc.shape, 0) % SUB
    sub_col = lax.broadcasted_iota(jnp.int32, acc.shape, 1) % SUB
    acc = jnp.where(sub_row == sub_col, acc, 0.0)
    acc = acc.reshape(2 * HEADS, SUB, HIDDEN * SUB).sum(axis=1)
    unit = lax.broadcasted_iota(jnp.int32, (HIDDEN * SUB, D), 0) // SUB
    lane = lax.broadcasted_iota(jnp.int32, (HIDDEN * SUB, D), 1) % HIDDEN
    gather = jnp.where(unit == lane, 1.0, 0.0)
    sums = lax.dot_general(
        acc, gather, (((1,), (0,)), ((), ())),
        precision=lax.Precision.HIGHEST, preferred_element_type=jnp.float32,
    )
    w_ref[...] = coef_ref[0] * sums[:HEADS] + coef_ref[1] * sums[HEADS:]


def merge(own, got, upper):
    first = jnp.where(upper, got, own)
    second = jnp.where(upper, own, got)
    return pairs_summed(jnp.concatenate([first, second], 0))


def pairs_summed(rows, by=2):
    return rows.reshape(rows.shape[0] // by, by, rows.shape[1]).sum(1)


def spread(rows, by):
    return jnp.repeat(rows, by, axis=0)


def sibling(rows, group):
    return lax.dynamic_slice_in_dim(rows, (group ^ 1) * COARSE, COARSE, 0)


def placed(mine, other, upper):
    return jnp.where(upper, jnp.concatenate([other, mine], 0), jnp.concatenate([mine, other], 0))


def halves(back, upper):
    low, high = spread(back[: COARSE // 2], 2), spread(back[COARSE // 2 :], 2)
    return jnp.where(upper, high, low), jnp.where(upper, low, high)


def swap_groups(value, groups):
    return lax.all_to_all(value, "ctx", 0, 0, axis_index_groups=groups)


def shards(queries, keys, values, lengths, fire_w1, fire_b1, fire_w2, grad_out):
    f32, bf16 = jnp.float32, jnp.bfloat16
    shape = jax.ShapeDtypeStruct
    ctx = lax.axis_index("ctx")
    mp = lax.axis_index("mp")
    bit = [(ctx >> k) & 1 == 1 for k in range(LEVELS)]
    blocks = range(SIDE)
    low_groups = [[high * SIDE + low for low in blocks] for high in blocks]
    high_groups = [[high * SIDE + (low ^ (8 * (high % 2))) for high in blocks] for low in blocks]

    w2 = lax.dynamic_slice_in_dim(fire_w2, mp * HEADS, HEADS, 1)
    w2_t = w2.T
    same = jnp.eye(SUB, dtype=f32)
    w2_wide = (w2_t[:, None, :, None] * same[None, :, None, :]).reshape(HEADS * SUB, HIDDEN * SUB)
    zero = jnp.zeros((HEADS, HIDDEN), f32)
    own_w2 = lambda row, core: jnp.broadcast_to(jnp.where(mp == core, row, 0.0)[None], (HEADS, HIDDEN))
    coef = jnp.stack([
        jnp.concatenate([own_w2(fire_b1, 0), own_w2(fire_b1, 1), zero, w2_t], axis=1),
        jnp.concatenate([own_w2(fire_w1, 0), own_w2(fire_w1, 1), w2_t, zero], axis=1),
    ])

    fine, wide = pl.pallas_call(
        leaf_kernel,
        out_shape=(shape((COARSE, 2 * WIDTH + D), f32), shape((CHUNK, 2 * WIDTH + D), f32)),
        in_specs=[SMEM, VMEM, VMEM],
        out_specs=(VMEM, VMEM),
        name="leaf",
    )(lengths, keys, values)
    bias, phase = pl.pallas_call(
        bias_kernel,
        out_shape=(shape((HEADS, T, KEYS), f32), shape((T, KEYS), f32)),
        in_specs=[SMEM] * 3 + [VMEM],
        out_specs=(VMEM, VMEM),
        cost_estimate=pl.CostEstimate(flops=600_000_000, bytes_accessed=2_000_000, transcendentals=50_000),
        name="bias",
    )(ctx.reshape(1), fire_w1, fire_b1, w2_wide)

    got0 = exchange(fine, 0)
    got1 = exchange(merge(fine, got0, bit[0]), 1)
    low = swap_groups(jnp.broadcast_to(wide[None], (SIDE,) + wide.shape), low_groups)
    low = low.reshape(SIDE * CHUNK, -1)
    sib2 = sibling(low, (ctx >> 2) & 3)
    low = pairs_summed(low)
    sib3 = sibling(low, (ctx >> 3) & 1)
    own4 = pairs_summed(low)
    got4 = exchange(own4, 4)
    got5 = exchange(merge(own4, got4, bit[4]), 5)
    wide4 = pairs_summed(own4, 4)
    high = swap_groups(jnp.broadcast_to(wide4[None], (SIDE,) + wide4.shape), high_groups)
    high = high.reshape(SIDE * CHUNK, -1)
    sib6 = sibling(high, (ctx >> 6) & 3)
    sib7 = sibling(pairs_summed(high), (ctx >> 7) & 1)
    siblings = jnp.concatenate([got0, got1, sib2, sib3, got4, got5, sib6, sib7], 0)

    attended, grad_q, own_grad, coarse, dscores = pl.pallas_call(
        main_kernel,
        out_shape=(
            shape((T, HEADS * D), bf16),
            shape((T, HEADS * D), bf16),
            shape((T, 2 * WIDTH), f32),
            shape((LEVELS * COARSE, 2 * WIDTH), f32),
            shape((HEADS, T, KEYS), f32),
        ),
        in_specs=[SMEM] + [VMEM] * 6,
        out_specs=(VMEM,) * 5,
        compiler_params=pltpu.CompilerParams(vmem_limit_bytes=32 * 2**20),
        name="attention",
    )(lengths, queries, keys, values, grad_out, siblings, bias)
    w_part = pl.pallas_call(
        weight_kernel,
        out_shape=shape((HEADS, D), f32),
        in_specs=[SMEM, SMEM] + [VMEM] * 3,
        out_specs=VMEM,
        scratch_shapes=[pltpu.VMEM((4 * HEADS * SUB, HIDDEN * SUB), f32)],
        cost_estimate=pl.CostEstimate(flops=900_000_000, bytes_accessed=2_000_000, transcendentals=0),
        name="weights",
    )(fire_w1, fire_b1, coef, dscores, phase)
    w_part = w_part + lax.ppermute(w_part, "mp", [(0, 1), (1, 0)])

    part = [coarse[k * COARSE : (k + 1) * COARSE] for k in range(LEVELS)]
    none = jnp.zeros_like(part[0])
    keep4, send4 = halves(exchange(part[5], 5), bit[4])
    keep0, send0 = halves(exchange(part[1], 1), bit[0])
    came4 = exchange(part[4] + send4, 4)
    came0 = exchange(part[0] + send0, 0)
    away = placed(placed(none, part[6], bit[6]), spread(part[7], 2), bit[7])
    away = sent_back(away, w_part, high_groups)
    group4 = keep4 + came4 + spread(away[:, : 2 * WIDTH], SIDE // 4)
    near = placed(placed(none, part[2], bit[2]), spread(part[3], 2), bit[3])
    near = sent_back(near + spread(group4, SIDE // 4), away[:, 2 * WIDTH :], low_groups)
    back = keep0 + came0 + spread(near[:, : 2 * WIDTH], SIDE // 4)

    token_live = (jnp.arange(T) < lengths[0]).astype(f32)[:, None]
    token_grad = ((own_grad + spread(back, T // COARSE)) * token_live).astype(bf16)
    w_all = near[:, 2 * WIDTH :]
    grad_w2 = jnp.concatenate([w_all[:, :HIDDEN], w_all[:, HIDDEN : 2 * HIDDEN]], 0).T
    grad_w1 = w_all[:, 2 * HIDDEN : 3 * HIDDEN].sum(0)
    grad_b1 = w_all[:, 3 * HIDDEN :].sum(0)
    return (attended, grad_q, token_grad[:, :WIDTH], token_grad[:, WIDTH:], grad_w1, grad_b1, grad_w2)


def sent_back(rows, weights, groups):
    rows = rows.reshape(SIDE, CHUNK, -1)
    weights = jnp.broadcast_to(weights[None], (SIDE,) + weights.shape)
    got = swap_groups(jnp.concatenate([rows, weights], 2), groups)
    return (got[: SIDE // 2] + got[SIDE // 2 :]).sum(0)


def solution(mesh):
    split = P("ctx", "mp")
    return jax.shard_map(
        shards,
        mesh=mesh,
        in_specs=(split, split, split, P("ctx"), P(), P(), P(), split),
        out_specs=(split, split, split, split, P(), P(), P()),
        check_vma=False,
    )
```

time: 154 us -> 129 us (0.84)
  the two profiles are of different devices: /device:TPU:1 before, /device:TPU:16 now
where the time goes in v2:
time: 129 us; the launch traced here: 128 us
  starting transfers between devices  62.7 us (49%)
  waiting for transfers between devices  27.5 us (21%)
  Pallas kernels  20.5 us (16%)
  local copies, waits for them, and re-layouts  8.41 us (7%)
  other arithmetic  7.19 us (6%)
  between operations  2 us (2%)
    all_to_all x4, starting transfers between devices, swap_groups(): return lax.all_to_all(value, 'ctx', 0, 0, axis_index_groups=groups)  30.5 us
    ppermute x8, starting transfers between devices, exchange(): return lax.ppermute(value, 'ctx', pairs)  30.3 us
    all_to_all x4, waiting for transfers between devices, swap_groups(): return lax.all_to_all(value, 'ctx', 0, 0, axis_index_groups=groups)  16.8 us
    ppermute x8, waiting for transfers between devices, exchange(): return lax.ppermute(value, 'ctx', pairs)  10.7 us
    pallas_call x1, Pallas kernels, shards(): pl.pallas_call(weight_kernel, out_shape=shape((HEADS, D), f32), in_specs=...  6.46 us
    pallas_call x1, Pallas kernels, shards(): pl.pallas_call(bias_kernel, out_shape=(shape((HEADS, T, KEYS), f32), shap...  6.31 us
    pallas_call x1, Pallas kernels, shards(): pl.pallas_call(main_kernel, out_shape=(shape((T, HEADS * D), bf16), shape...  6.1 us
  transfers between devices with their start and end apart: 13, of which 6 were waited for; matrix products, arithmetic and copies ran while one was open for 5% of the time, Pallas kernels for 10%

profile of v2, /device:TPU:16, one launch (start us, length us, event | category | flops | bytes accessed | tf_op | source)
XLA Modules:
  0.0 128.3 jit_solution(6114118000856931883)
XLA Ops:
  1.3 1.6 %leaf.1 = (f32[32,640]{1,0:T(8,128)}, f32[8,640]{1,0:T(8,128)}) custom-call(s32[1]{0:T(128)} %copy.22.len_ref, bf16[128,256]{1,0:T(8,128)(2,1)} %k_ref.3, bf16[128,256]{1,0:T(8,128)(2,1)} %v_ref.3), custom_call_target="tpu_custom_call" | custom-call | tf_op jit(solution)/shard_map/leaf/pallas_call | solution.py:220
  3.0 3.6 %collective-permute-start = (f32[32,640]{1,0:T(8,128)}, f32[32,640]{1,0:T(8,128)S(1)}, u32[]{:S(2)}, u32[]{:S(2)}) collective-permute-start(f32[32,640]{1,0:T(8,128)} %get-tuple-element.16), channel_id=1, source_target_pairs={{0,2},{2,0},{4,6},{6,4},{8,10},{10,8},{12,14},{14,12},{16,18},{18,... | collective-permute-start | bytes 245768 | tf_op jit(solution)/shard_map/ppermute | solution.py:36
  6.6 1.5 %broadcast_in_dim.45 = f32[16,8,640]{2,1,0:T(8,128)} broadcast(f32[8,640]{1,0:T(8,128)} %get-tuple-element.17), dimensions={1,2} | broadcast | bytes 348160 | tf_op jit(solution)/shard_map/broadcast_in_dim | solution.py:238
  8.1 7.5 %all-to-all-start = ((f32[16,8,640]{2,1,0:T(8,128)}), f32[16,8,640]{2,1,0:T(8,128)S(1)}, u32[]{:S(2)}, u32[]{:S(2)}) async-start(f32[16,8,640]{2,1,0:T(8,128)} %broadcast_in_dim.45), calls=%async_computation | async-start | bytes 655360 | tf_op jit(solution)/shard_map/all_to_all | solution.py:196
  15.6 0.2 broadcast_multiply_fusion
  16.0 0.1 reshape.102
  16.1 0.2 reduce_sum.90
  16.3 2.1 %collective-permute-start.1 = (f32[32,640]{1,0:T(8,128)S(1)}, f32[32,640]{1,0:T(8,128)S(1)}, u32[]{:S(2)}, u32[]{:S(2)}) collective-permute-start(f32[32,640]{1,0:T(8,128)S(1)} %reduce_sum.90), channel_id=1, source_target_pairs={{0,4},{2,6},{4,0},{6,2},{8,12},{10,14},{12,8},{14,10},{16,20},{18,... | collective-permute-start | bytes 245768 | tf_op jit(solution)/shard_map/ppermute | solution.py:36
  18.6 7.1 %collective-permute-done.1 = f32[32,640]{1,0:T(8,128)S(1)} collective-permute-done((f32[32,640]{1,0:T(8,128)S(1)}, f32[32,640]{1,0:T(8,128)S(1)}, u32[]{:S(2)}, u32[]{:S(2)}) %collective-permute-start.1) | collective-permute-done | bytes 81952 | tf_op jit(solution)/shard_map/ppermute | solution.py:36
  25.7 0.2 all-to-all-done
  25.9 0.2 reshape_reshape.6
  26.1 0.4 reduce_sum.91
  26.6 0.2 reduce_sum.92
  26.8 4.5 %collective-permute-start.2 = (f32[32,640]{1,0:T(8,128)S(1)}, f32[32,640]{1,0:T(8,128)S(1)}, u32[]{:S(2)}, u32[]{:S(2)}) collective-permute-start(f32[32,640]{1,0:T(8,128)S(1)} %reduce_sum.92), channel_id=1, source_target_pairs={{0,48},{2,50},{4,52},{6,54},{8,56},{10,58},{12,60},{14,62},{16,32}... | collective-permute-start | bytes 245768 | tf_op jit(solution)/shard_map/ppermute | solution.py:36
  31.3 0.8 broadcast_in_dim.46
  32.1 10.5 %all-to-all-start.1 = ((f32[16,8,640]{2,1,0:T(8,128)}), f32[16,8,640]{2,1,0:T(8,128)S(1)}, u32[]{:S(2)}, u32[]{:S(2)}) async-start(f32[16,8,640]{2,1,0:T(8,128)} %broadcast_in_dim.46), calls=%async_computation.1 | async-start | bytes 655360 | tf_op jit(solution)/shard_map/all_to_all | solution.py:196
  42.8 0.2 reduce_sum.93
  43.0 3.8 %collective-permute-start.3 = (f32[32,640]{1,0:T(8,128)S(1)}, f32[32,640]{1,0:T(8,128)S(1)}, u32[]{:S(2)}, u32[]{:S(2)}) collective-permute-start(f32[32,640]{1,0:T(8,128)S(1)} %reduce_sum.93), channel_id=1, source_target_pairs={{0,64},{2,66},{4,68},{6,70},{8,72},{10,74},{12,76},{14,78},{16,80}... | collective-permute-start | bytes 245768 | tf_op jit(solution)/shard_map/ppermute | solution.py:36
  46.9 0.6 pad_maximum_fusion.4.coef_ref
  47.5 1.2 mul.48.w2_ref
  48.6 6.3 %bias.1 = (f32[8,128,384]{2,1,0:T(8,128)}, f32[128,384]{1,0:T(8,128)}) custom-call(s32[1]{0:T(128)} %bitcast.2.ctx_ref, f32[32]{0:T(128)} %w1_ref.3, f32[32]{0:T(128)} %b1_ref.3, f32[64,256]{1,0:T(8,128)} %mul.48.w2_ref), custom_call_target="tpu_custom_call" | custom-call | flops 600000000 | bytes 2000000 | tf_op jit(solution)/shard_map/bias/pallas_call | solution.py:227
  55.0 1.1 all-to-all-done.1
  56.1 0.9 reshape_reshape.7
  57.0 1.4 %reduce_sum.95 = f32[64,640]{1,0:T(8,128)S(1)} reduce(f32[64,2,640]{2,1,0:T(2,128)} %reshape_reshape.7, f32[]{:T(128)} %constant.4.clone.1), dimensions={1}, to_apply=%region_5.6 | reduce | flops 40960 | bytes 491524 | tf_op jit(solution)/shard_map/reduce_sum | solution.py:175
  58.5 6.1 %attention.1 = (bf16[128,1024]{1,0:T(8,128)(2,1)}, bf16[128,1024]{1,0:T(8,128)(2,1)}, f32[128,512]{1,0:T(8,128)S(1)}, f32[256,512]{1,0:T(8,128)S(1)}, f32[8,128,384]{2,1,0:T(8,128)S(1)}) custom-call(s32[1]{0:T(128)} %copy.22.len_ref, bf16[128,1024]{1,0:T(8,128)(2,1)S(1)} %copy-done.2, bf16[128,256]{1,0:T(8,128)(2,1)S(1)} %copy-done.4, ...), custom_call_target="tpu_custom_call" | custom-call | tf_op jit(solution)/shard_map/attention/pallas_call | solution.py:253
  64.6 0.7 copy-done.6
  65.3 1.2 copy-done.8
  66.5 5.9 %collective-permute-start.4 = (f32[32,512]{1,0:T(8,128)S(1)}, f32[32,512]{1,0:T(8,128)S(1)}, u32[]{:S(2)}, u32[]{:S(2)}) collective-permute-start(f32[32,512]{1,0:T(8,128)S(1)} %get-tuple-element.33), channel_id=1, source_target_pairs={{0,4},{2,6},{4,0},{6,2},{8,12},{10,14},{12,8},{14,10},{16,20},{18,... | collective-permute-start | bytes 196616 | tf_op jit(solution)/shard_map/ppermute | solution.py:36
  72.4 6.5 %weights.1 = f32[8,128]{1,0:T(8,128)} custom-call(f32[32]{0:T(128)} %w1_ref.3, f32[32]{0:T(128)} %b1_ref.3, f32[2,8,128]{2,1,0:T(8,128)} %pad_maximum_fusion.4.coef_ref, f32[8,128,384]{2,1,0:T(8,128)} %copy-done.8, f32[128,384]{1,0:T(8,128)} %get-tuple-element.24.phase_ref), custom_call_target="tpu_custom_call" | custom-call | flops 900000000 | bytes 2000000 | tf_op jit(solution)/shard_map/weights/pallas_call | solution.py:267
  78.8 1.9 %collective-permute-start.8 = (f32[8,128]{1,0:T(8,128)}, f32[8,128]{1,0:T(8,128)S(1)}, u32[]{:S(2)}, u32[]{:S(2)}) collective-permute-start(f32[8,128]{1,0:T(8,128)} %weights.1), channel_id=1, source_target_pairs={{0,1},{1,0},{2,3},{3,2},{4,5},{5,4},{6,7},{7,6},{8,9},{9,8},{10,11... | collective-permute-start | bytes 12296 | tf_op jit(solution)/shard_map/ppermute | solution.py:276
  80.7 2.0 %collective-permute-start.6 = (f32[32,512]{1,0:T(8,128)S(1)}, f32[32,512]{1,0:T(8,128)S(1)}, u32[]{:S(2)}, u32[]{:S(2)}) collective-permute-start(f32[32,512]{1,0:T(8,128)S(1)} %get-tuple-element.34), channel_id=1, source_target_pairs={{0,64},{2,66},{4,68},{6,70},{8,72},{10,74},{12,76},{14,78},{16,80}... | collective-permute-start | bytes 196616 | tf_op jit(solution)/shard_map/ppermute | solution.py:36
  82.8 0.7 add.66
  83.6 3.5 %collective-permute-done.6 = f32[32,512]{1,0:T(8,128)S(1)} collective-permute-done((f32[32,512]{1,0:T(8,128)S(1)}, f32[32,512]{1,0:T(8,128)S(1)}, u32[]{:S(2)}, u32[]{:S(2)}) %collective-permute-start.6) | collective-permute-done | bytes 65568 | tf_op jit(solution)/shard_map/ppermute | solution.py:36
  87.3 0.1 reshape.110
  87.5 0.7 pad_maximum_fusion
  88.2 6.1 %all-to-all-start.2 = ((f32[16,8,640]{2,1,0:T(8,128)}), f32[16,8,640]{2,1,0:T(8,128)S(1)}, u32[]{:S(2)}, u32[]{:S(2)}) async-start(f32[16,8,640]{2,1,0:T(8,128)} %pad_maximum_fusion), calls=%async_computation.2 | async-start | bytes 655360 | tf_op jit(solution)/shard_map/all_to_all | solution.py:196
  94.4 5.0 %collective-permute-start.7 = (f32[32,512]{1,0:T(8,128)S(1)}, f32[32,512]{1,0:T(8,128)S(1)}, u32[]{:S(2)}, u32[]{:S(2)}) collective-permute-start(f32[32,512]{1,0:T(8,128)S(1)} %get-tuple-element.30), channel_id=1, source_target_pairs={{0,48},{2,50},{4,52},{6,54},{8,56},{10,58},{12,60},{14,62},{16,32}... | collective-permute-start | bytes 196616 | tf_op jit(solution)/shard_map/ppermute | solution.py:36
  99.6 0.1 reshape.109
  99.7 9.1 %all-to-all-done.2 = f32[16,8,640]{2,1,0:T(8,128)S(1)} async-done(((f32[16,8,640]{2,1,0:T(8,128)}), f32[16,8,640]{2,1,0:T(8,128)S(1)}, u32[]{:S(2)}, u32[]{:S(2)}) %all-to-all-start.2) | async-done | bytes 327712 | tf_op jit(solution)/shard_map/all_to_all | solution.py:196
  108.9 0.1 reshape.112
  109.1 0.7 pad_maximum_fusion.1
  109.9 6.3 %all-to-all-start.3 = ((f32[16,8,640]{2,1,0:T(8,128)}), f32[16,8,640]{2,1,0:T(8,128)S(1)}, u32[]{:S(2)}, u32[]{:S(2)}) async-start(f32[16,8,640]{2,1,0:T(8,128)} %pad_maximum_fusion.1), calls=%async_computation.3 | async-start | bytes 655360 | tf_op jit(solution)/shard_map/all_to_all | solution.py:196
  116.2 3.4 %collective-permute-start.5 = (f32[32,512]{1,0:T(8,128)S(1)}, f32[32,512]{1,0:T(8,128)S(1)}, u32[]{:S(2)}, u32[]{:S(2)}) collective-permute-start(f32[32,512]{1,0:T(8,128)S(1)} %get-tuple-element.27), channel_id=1, source_target_pairs={{0,2},{2,0},{4,6},{6,4},{8,10},{10,8},{12,14},{14,12},{16,18},{18,... | collective-permute-start | bytes 196616 | tf_op jit(solution)/shard_map/ppermute | solution.py:36
  119.7 6.4 %all-to-all-done.3 = f32[16,8,640]{2,1,0:T(8,128)S(1)} async-done(((f32[16,8,640]{2,1,0:T(8,128)}), f32[16,8,640]{2,1,0:T(8,128)S(1)}, u32[]{:S(2)}, u32[]{:S(2)}) %all-to-all-start.3) | async-done | bytes 327712 | tf_op jit(solution)/shard_map/all_to_all | solution.py:196
  126.1 0.6 slice_reduce_fusion
  126.8 0.1 reshape.114
  127.0 0.7 fusion.7
  127.7 0.6 maximum_bitcast_fusion
  (85 shorter events, 1.6 us)
Async XLA Ops:
  0.6 14.9 %copy-start = (f32[32,16]{0,1:T(8,128)S(1)}, f32[32,16]{0,1:T(8,128)}, u32[]{:S(2)}) copy-start(f32[32,16]{0,1:T(8,128)} %param.14) | copy-start | bytes 6148
  0.6 15.1 %copy-start.10 = (f32[32]{0:T(128)S(1)}, f32[32]{0:T(128)}, u32[]{:S(2)}) copy-start(f32[32]{0:T(128)} %w1_ref.3) | copy-start | bytes 388
  0.7 15.1 %copy-start.11 = (f32[32]{0:T(128)S(1)}, f32[32]{0:T(128)}, u32[]{:S(2)}) copy-start(f32[32]{0:T(128)} %b1_ref.3) | copy-start | bytes 388
  3.0 13.0 %copy-start.9 = (f32[32,640]{1,0:T(8,128)S(1)}, f32[32,640]{1,0:T(8,128)}, u32[]{:S(2)}) copy-start(f32[32,640]{1,0:T(8,128)} %get-tuple-element.16) | copy-start | bytes 245764
  3.0 13.0 %collective-permute-start = (f32[32,640]{1,0:T(8,128)}, f32[32,640]{1,0:T(8,128)S(1)}, u32[]{:S(2)}, u32[]{:S(2)}) collective-permute-start(f32[32,640]{1,0:T(8,128)} %get-tuple-element.16), channel_id=1, source_target_pairs={{0,2},{2,0},{4,6},{6,4},{8,10},{10,8},{12,14},{14,12},{16,18},{18,... | collective-permute-start | bytes 245768 | tf_op jit(solution)/shard_map/ppermute | solution.py:36
  8.1 17.8 %all-to-all-start = ((f32[16,8,640]{2,1,0:T(8,128)}), f32[16,8,640]{2,1,0:T(8,128)S(1)}, u32[]{:S(2)}, u32[]{:S(2)}) async-start(f32[16,8,640]{2,1,0:T(8,128)} %broadcast_in_dim.45), calls=%async_computation | async-start | bytes 655360 | tf_op jit(solution)/shard_map/all_to_all | solution.py:196
  16.3 9.3 %collective-permute-start.1 = (f32[32,640]{1,0:T(8,128)S(1)}, f32[32,640]{1,0:T(8,128)S(1)}, u32[]{:S(2)}, u32[]{:S(2)}) collective-permute-start(f32[32,640]{1,0:T(8,128)S(1)} %reduce_sum.90), channel_id=1, source_target_pairs={{0,4},{2,6},{4,0},{6,2},{8,12},{10,14},{12,8},{14,10},{16,20},{18,... | collective-permute-start | bytes 245768 | tf_op jit(solution)/shard_map/ppermute | solution.py:36
  26.8 15.9 %collective-permute-start.2 = (f32[32,640]{1,0:T(8,128)S(1)}, f32[32,640]{1,0:T(8,128)S(1)}, u32[]{:S(2)}, u32[]{:S(2)}) collective-permute-start(f32[32,640]{1,0:T(8,128)S(1)} %reduce_sum.92), channel_id=1, source_target_pairs={{0,48},{2,50},{4,52},{6,54},{8,56},{10,58},{12,60},{14,62},{16,32}... | collective-permute-start | bytes 245768 | tf_op jit(solution)/shard_map/ppermute | solution.py:36
  32.1 24.0 %all-to-all-start.1 = ((f32[16,8,640]{2,1,0:T(8,128)}), f32[16,8,640]{2,1,0:T(8,128)S(1)}, u32[]{:S(2)}, u32[]{:S(2)}) async-start(f32[16,8,640]{2,1,0:T(8,128)} %broadcast_in_dim.46), calls=%async_computation.1 | async-start | bytes 655360 | tf_op jit(solution)/shard_map/all_to_all | solution.py:196
  43.0 11.9 %collective-permute-start.3 = (f32[32,640]{1,0:T(8,128)S(1)}, f32[32,640]{1,0:T(8,128)S(1)}, u32[]{:S(2)}, u32[]{:S(2)}) collective-permute-start(f32[32,640]{1,0:T(8,128)S(1)} %reduce_sum.93), channel_id=1, source_target_pairs={{0,64},{2,66},{4,68},{6,70},{8,72},{10,74},{12,76},{14,78},{16,80}... | collective-permute-start | bytes 245768 | tf_op jit(solution)/shard_map/ppermute | solution.py:36
  48.6 9.8 %copy-start.2 = (bf16[128,1024]{1,0:T(8,128)(2,1)S(1)}, bf16[128,1024]{1,0:T(8,128)(2,1)}, u32[]{:S(2)}) copy-start(bf16[128,1024]{1,0:T(8,128)(2,1)} %q_ref.1) | copy-start | bytes 786436
  48.6 9.8 %copy-start.3 = (bf16[128,1024]{1,0:T(8,128)(2,1)S(1)}, bf16[128,1024]{1,0:T(8,128)(2,1)}, u32[]{:S(2)}) copy-start(bf16[128,1024]{1,0:T(8,128)(2,1)} %g_ref.1) | copy-start | bytes 786436
  48.6 9.9 %copy-start.4 = (bf16[128,256]{1,0:T(8,128)(2,1)S(1)}, bf16[128,256]{1,0:T(8,128)(2,1)}, u32[]{:S(2)}) copy-start(bf16[128,256]{1,0:T(8,128)(2,1)} %k_ref.3) | copy-start | bytes 196612
  48.6 9.9 %copy-start.5 = (bf16[128,256]{1,0:T(8,128)(2,1)S(1)}, bf16[128,256]{1,0:T(8,128)(2,1)}, u32[]{:S(2)}) copy-start(bf16[128,256]{1,0:T(8,128)(2,1)} %v_ref.3) | copy-start | bytes 196612
  54.9 3.6 %copy-start.1 = (f32[8,128,384]{2,1,0:T(8,128)S(1)}, f32[8,128,384]{2,1,0:T(8,128)}, u32[]{:S(2)}) copy-start(f32[8,128,384]{2,1,0:T(8,128)} %get-tuple-element.18.bias_ref) | copy-start | bytes 4718596
  64.6 0.7 copy-start.6
  65.3 1.2 copy-start.8
  66.5 17.0 %collective-permute-start.4 = (f32[32,512]{1,0:T(8,128)S(1)}, f32[32,512]{1,0:T(8,128)S(1)}, u32[]{:S(2)}, u32[]{:S(2)}) collective-permute-start(f32[32,512]{1,0:T(8,128)S(1)} %get-tuple-element.33), channel_id=1, source_target_pairs={{0,4},{2,6},{4,0},{6,2},{8,12},{10,14},{12,8},{14,10},{16,20},{18,... | collective-permute-start | bytes 196616 | tf_op jit(solution)/shard_map/ppermute | solution.py:36
  78.8 4.0 %collective-permute-start.8 = (f32[8,128]{1,0:T(8,128)}, f32[8,128]{1,0:T(8,128)S(1)}, u32[]{:S(2)}, u32[]{:S(2)}) collective-permute-start(f32[8,128]{1,0:T(8,128)} %weights.1), channel_id=1, source_target_pairs={{0,1},{1,0},{2,3},{3,2},{4,5},{5,4},{6,7},{7,6},{8,9},{9,8},{10,11... | collective-permute-start | bytes 12296 | tf_op jit(solution)/shard_map/ppermute | solution.py:276
  80.7 6.4 %collective-permute-start.6 = (f32[32,512]{1,0:T(8,128)S(1)}, f32[32,512]{1,0:T(8,128)S(1)}, u32[]{:S(2)}, u32[]{:S(2)}) collective-permute-start(f32[32,512]{1,0:T(8,128)S(1)} %get-tuple-element.34), channel_id=1, source_target_pairs={{0,64},{2,66},{4,68},{6,70},{8,72},{10,74},{12,76},{14,78},{16,80}... | collective-permute-start | bytes 196616 | tf_op jit(solution)/shard_map/ppermute | solution.py:36
  88.2 20.5 %all-to-all-start.2 = ((f32[16,8,640]{2,1,0:T(8,128)}), f32[16,8,640]{2,1,0:T(8,128)S(1)}, u32[]{:S(2)}, u32[]{:S(2)}) async-start(f32[16,8,640]{2,1,0:T(8,128)} %pad_maximum_fusion), calls=%async_computation.2 | async-start | bytes 655360 | tf_op jit(solution)/shard_map/all_to_all | solution.py:196
  94.4 14.5 %collective-permute-start.7 = (f32[32,512]{1,0:T(8,128)S(1)}, f32[32,512]{1,0:T(8,128)S(1)}, u32[]{:S(2)}, u32[]{:S(2)}) collective-permute-start(f32[32,512]{1,0:T(8,128)S(1)} %get-tuple-element.30), channel_id=1, source_target_pairs={{0,48},{2,50},{4,52},{6,54},{8,56},{10,58},{12,60},{14,62},{16,32}... | collective-permute-start | bytes 196616 | tf_op jit(solution)/shard_map/ppermute | solution.py:36
  109.1 17.8 %copy-start.7 = (f32[128,512]{1,0:T(8,128)S(1)}, f32[128,512]{1,0:T(8,128)}, u32[]{:S(2)}) copy-start(f32[128,512]{1,0:T(8,128)} %copy-done.6) | copy-start | bytes 786436
  109.9 16.2 %all-to-all-start.3 = ((f32[16,8,640]{2,1,0:T(8,128)}), f32[16,8,640]{2,1,0:T(8,128)S(1)}, u32[]{:S(2)}, u32[]{:S(2)}) async-start(f32[16,8,640]{2,1,0:T(8,128)} %pad_maximum_fusion.1), calls=%async_computation.3 | async-start | bytes 655360 | tf_op jit(solution)/shard_map/all_to_all | solution.py:196
  116.2 10.6 %collective-permute-start.5 = (f32[32,512]{1,0:T(8,128)S(1)}, f32[32,512]{1,0:T(8,128)S(1)}, u32[]{:S(2)}, u32[]{:S(2)}) collective-permute-start(f32[32,512]{1,0:T(8,128)S(1)} %get-tuple-element.27), channel_id=1, source_target_pairs={{0,2},{2,0},{4,6},{6,4},{8,10},{10,8},{12,14},{14,12},{16,18},{18,... | collective-permute-start | bytes 196616 | tf_op jit(solution)/shard_map/ppermute | solution.py:36

commit v3 on v2

--- a/solution.py
+++ b/solution.py
@@ -1,3 +1,5 @@
+import functools
+
 import jax
 import jax.numpy as jnp
 from jax import lax
@@ -8,6 +10,7 @@
 D = 128
 COARSE = 32
 T = 128
+HALF = T // 2
 LEVELS = 8
 KEYS = T + LEVELS * COARSE
 HIDDEN = 32
@@ -37,18 +40,22 @@
 
 
 def leaf_kernel(len_ref, k_ref, v_ref, fine_ref, wide_ref):
-    for ref, run in ((fine_ref, T // COARSE), (wide_ref, T // CHUNK)):
+    wide = []
+    for run in (T // COARSE, T // CHUNK):
         row = lax.broadcasted_iota(jnp.int32, (T // run, T), 0)
         tok = lax.broadcasted_iota(jnp.int32, (T // run, T), 1)
         member = jnp.where((tok // run == row) & (tok < len_ref[0]), 1.0, 0.0)
         member_b = member.astype(jnp.bfloat16)
-        ref[:, :WIDTH] = dot(member_b, k_ref[...])
-        ref[:, WIDTH : 2 * WIDTH] = dot(member_b, v_ref[...])
         count = jnp.sum(member, axis=1, keepdims=True)
-        ref[:, 2 * WIDTH :] = jnp.broadcast_to(count, (T // run, D))
-
-
-def bias_kernel(ctx_ref, w1_ref, b1_ref, w2_ref, bias_ref, phase_ref):
+        wide = [dot(member_b, k_ref[...]), dot(member_b, v_ref[...]), jnp.broadcast_to(count, (T // run, D))]
+        if run == T // COARSE:
+            fine_ref[...] = jnp.concatenate(wide, axis=1)
+    wide = jnp.concatenate(wide, axis=1)
+    for n in range(SIDE):
+        wide_ref[n] = wide
+
+
+def bias_kernel(first, ctx_ref, w1_ref, b1_ref, w2_ref, after_ref, bias_ref, phase_ref):
     ctx = ctx_ref[0]
     col = lax.broadcasted_iota(jnp.int32, (1, KEYS), 1)
     level = (col - T) // COARSE
@@ -67,7 +74,7 @@
 
     def body(i, carry):
         rows = pl.ds(pl.multiple_of(i * SUB, SUB), SUB)
-        row = i * SUB + lax.broadcasted_iota(jnp.int32, (SUB, KEYS), 0)
+        row = first + i * SUB + lax.broadcasted_iota(jnp.int32, (SUB, KEYS), 0)
         phase = jnp.log1p(jnp.abs(row.astype(jnp.float32) - pos)) / top
         phase_ref[rows, :] = phase
         hidden = [jnp.maximum(phase * w1_ref[m] + b1_ref[m], 0.0) for m in range(HIDDEN)]
@@ -80,14 +87,40 @@
             bias_ref[h, rows, :] = bias[h * SUB : (h + 1) * SUB]
         return carry
 
-    lax.fori_loop(0, T // SUB, body, 0)
+    lax.fori_loop(0, HALF // SUB, body, 0)
+
+
+def pooled(rows, by):
+    shape = (rows.shape[0] // by, rows.shape[0])
+    row = lax.broadcasted_iota(jnp.int32, shape, 0)
+    col = lax.broadcasted_iota(jnp.int32, shape, 1)
+    return lax.dot_general(
+        jnp.where(col // by == row, 1.0, 0.0), rows, (((1,), (0,)), ((), ())),
+        precision=lax.Precision.HIGHEST, preferred_element_type=jnp.float32,
+    )
+
+
+def middle_kernel(low_ref, after_ref, own_ref, wide_ref):
+    own = pooled(low_ref[...], SIDE * CHUNK // COARSE)
+    own_ref[...] = own
+    wide = pooled(own, COARSE // CHUNK)
+    for n in range(SIDE):
+        wide_ref[n] = wide
 
 
 def main_kernel(
-    len_ref, q_ref, k_ref, v_ref, g_ref, sib_ref, bias_ref,
-    out_ref, gq_ref, own_ref, coarse_ref, ds_ref,
+    ctx_ref, len_ref, q_ref, k_ref, v_ref, g_ref, got0_ref, got1_ref, low_ref, got4_ref, got5_ref, high_ref,
+    bias_a_ref, bias_b_ref, out_ref, gq_ref, own_ref, coarse_ref, ds_ref, sib_ref,
 ):
     length = len_ref[0]
+    ctx = ctx_ref[0]
+    for level, ref in ((0, got0_ref), (1, got1_ref), (4, got4_ref), (5, got5_ref)):
+        sib_ref[level * COARSE : (level + 1) * COARSE, :] = ref[...]
+    for level, ref in ((2, low_ref), (6, high_ref)):
+        start = pl.multiple_of((((ctx >> level) & 3) ^ 1) * COARSE, COARSE)
+        sib_ref[level * COARSE : (level + 1) * COARSE, :] = ref[pl.ds(start, COARSE), :]
+        start = pl.multiple_of((((ctx >> level + 1) & 1) ^ 1) * 2 * COARSE, 2 * COARSE)
+        sib_ref[(level + 1) * COARSE : (level + 2) * COARSE, :] = pooled(ref[pl.ds(start, 2 * COARSE), :], 2)
     count = sib_ref[:, 2 * KV * D :]
     safe = jnp.maximum(count, 1.0)
     count_t = jnp.concatenate([count[:T].T[:1], count[T:].T[:1]], axis=1)
@@ -106,7 +139,8 @@
             h = j * GROUP + g
             hcols = slice(h * D, (h + 1) * D)
             query = q_ref[:, hcols]
-            scores = dot(query, keys, NT) * SCALE + bias_ref[h]
+            scores = dot(query, keys, NT) * SCALE
+            scores = scores + jnp.concatenate([bias_a_ref[h], bias_b_ref[h]], axis=0)
             scores = jnp.where(live, scores, -jnp.inf)
             top = jnp.max(scores, axis=1, keepdims=True)
             weights = jnp.exp(scores - top)
@@ -129,12 +163,13 @@
         coarse_ref[:, vcols] = value_grads[T:] / safe
 
 
-def weight_kernel(w1_ref, b1_ref, coef_ref, ds_ref, phase_ref, w_ref, acc_ref):
+def weight_kernel(ctx_ref, w1_ref, b1_ref, coef_ref, ds_ref, phase_a_ref, phase_b_ref, coarse_ref, away_ref, acc_ref):
     acc_ref[...] = jnp.zeros_like(acc_ref)
 
-    def body(i, carry):
-        rows = pl.ds(i * SUB, SUB)
-        phase = phase_ref[rows, :]
+    def body(phase_of, first, i, carry):
+        rows = pl.ds(pl.multiple_of(i * SUB, SUB), SUB)
+        phase = phase_of[rows, :]
+        rows = pl.ds(pl.multiple_of(first + i * SUB, SUB), SUB)
         parts = [ds_ref[h, rows, :] for h in range(HEADS)]
         parts = jnp.concatenate(parts + [p * phase for p in parts], axis=0)
         high = parts.astype(jnp.bfloat16)
@@ -147,7 +182,8 @@
         acc_ref[...] += dot(both, active, NT)
         return carry
 
-    lax.fori_loop(0, T // SUB, body, 0)
+    lax.fori_loop(0, HALF // SUB, functools.partial(body, phase_a_ref, 0), 0)
+    lax.fori_loop(0, HALF // SUB, functools.partial(body, phase_b_ref, HALF), 0)
     acc = acc_ref[...]
     rows = 2 * HEADS * SUB
     acc = acc[:rows] + acc[rows:]
@@ -162,33 +198,56 @@
         acc, gather, (((1,), (0,)), ((), ())),
         precision=lax.Precision.HIGHEST, preferred_element_type=jnp.float32,
     )
-    w_ref[...] = coef_ref[0] * sums[:HEADS] + coef_ref[1] * sums[HEADS:]
+    weights = coef_ref[0] * sums[:HEADS] + coef_ref[1] * sums[HEADS:]
+    place_levels(ctx_ref[0], 6, coarse_ref, away_ref, None, weights)
+
+
+def place_levels(ctx, level, coarse_ref, out_ref, base, weights):
+    quarter = (ctx >> level) & 3
+    near = coarse_ref[level * COARSE : (level + 1) * COARSE, :]
+    far = coarse_ref[(level + 1) * COARSE : (level + 2) * COARSE, :]
+    far = jnp.broadcast_to(far[:, None, :], (COARSE, 2, 2 * WIDTH)).reshape(2 * COARSE, 2 * WIDTH)
+    for q in range(4):
+        rows = jnp.where(quarter == q ^ 1, near, 0.0)
+        rows = jnp.where(quarter >> 1 != q >> 1, far[(q & 1) * COARSE : (q & 1) * COARSE + COARSE], rows)
+        if base is not None:
+            rows = rows + base[q * COARSE : (q + 1) * COARSE]
+        for n in range(4):
+            out_ref[q * 4 + n, :, : 2 * WIDTH] = rows[n * CHUNK : (n + 1) * CHUNK]
+            out_ref[q * 4 + n, :, 2 * WIDTH :] = weights
+
+
+def summed(ref):
+    return sum(ref[n] + ref[n + SIDE // 2] for n in range(SIDE // 2))
+
+
+def repeated(rows, by):
+    return jnp.broadcast_to(rows[:, None, :], (rows.shape[0], by, rows.shape[1])).reshape(-1, rows.shape[1])
+
+
+def return_kernel(ctx_ref, away_ref, keep_ref, came_ref, coarse_ref, near_ref):
+    away = summed(away_ref)
+    group = keep_ref[...] + came_ref[...] + repeated(away[:, : 2 * WIDTH], SIDE // 4)
+    place_levels(ctx_ref[0], 2, coarse_ref, near_ref, repeated(group, SIDE // 4), away[:, 2 * WIDTH :])
+
+
+def final_kernel(len_ref, near_ref, keep_ref, came_ref, own_ref, gk_ref, gv_ref):
+    near = summed(near_ref)
+    back = keep_ref[...] + came_ref[...] + repeated(near[:, : 2 * WIDTH], SIDE // 4)
+    live = lax.broadcasted_iota(jnp.int32, (T, 1), 0) < len_ref[0]
+    grad = (own_ref[...] + repeated(back, T // COARSE)) * live.astype(jnp.float32)
+    gk_ref[...] = grad[:, :WIDTH].astype(jnp.bfloat16)
+    gv_ref[...] = grad[:, WIDTH:].astype(jnp.bfloat16)
 
 
 def merge(own, got, upper):
     first = jnp.where(upper, got, own)
     second = jnp.where(upper, own, got)
-    return pairs_summed(jnp.concatenate([first, second], 0))
-
-
-def pairs_summed(rows, by=2):
-    return rows.reshape(rows.shape[0] // by, by, rows.shape[1]).sum(1)
-
-
-def spread(rows, by):
-    return jnp.repeat(rows, by, axis=0)
-
-
-def sibling(rows, group):
-    return lax.dynamic_slice_in_dim(rows, (group ^ 1) * COARSE, COARSE, 0)
-
-
-def placed(mine, other, upper):
-    return jnp.where(upper, jnp.concatenate([other, mine], 0), jnp.concatenate([mine, other], 0))
+    return jnp.concatenate([first, second], 0).reshape(COARSE, 2, -1).sum(1)
 
 
 def halves(back, upper):
-    low, high = spread(back[: COARSE // 2], 2), spread(back[COARSE // 2 :], 2)
+    low, high = jnp.repeat(back[: COARSE // 2], 2, axis=0), jnp.repeat(back[COARSE // 2 :], 2, axis=0)
     return jnp.where(upper, high, low), jnp.where(upper, low, high)
 
 
@@ -201,6 +260,7 @@
     shape = jax.ShapeDtypeStruct
     ctx = lax.axis_index("ctx")
     mp = lax.axis_index("mp")
+    ctx_1 = ctx.reshape(1)
     bit = [(ctx >> k) & 1 == 1 for k in range(LEVELS)]
     blocks = range(SIDE)
     low_groups = [[high * SIDE + low for low in blocks] for high in blocks]
@@ -217,38 +277,41 @@
         jnp.concatenate([own_w2(fire_w1, 0), own_w2(fire_w1, 1), w2_t, zero], axis=1),
     ])
 
+    payload = shape((SIDE, CHUNK, 2 * WIDTH + D), f32)
+    sums = shape((COARSE, 2 * WIDTH + D), f32)
     fine, wide = pl.pallas_call(
         leaf_kernel,
-        out_shape=(shape((COARSE, 2 * WIDTH + D), f32), shape((CHUNK, 2 * WIDTH + D), f32)),
+        out_shape=(sums, payload),
         in_specs=[SMEM, VMEM, VMEM],
         out_specs=(VMEM, VMEM),
         name="leaf",
     )(lengths, keys, values)
-    bias, phase = pl.pallas_call(
-        bias_kernel,
-        out_shape=(shape((HEADS, T, KEYS), f32), shape((T, KEYS), f32)),
-        in_specs=[SMEM] * 3 + [VMEM],
+
+    def bias_half(first, after):
+        return pl.pallas_call(
+            functools.partial(bias_kernel, first),
+            out_shape=(shape((HEADS, HALF, KEYS), f32), shape((HALF, KEYS), f32)),
+            in_specs=[SMEM] * 3 + [VMEM, pl.BlockSpec(memory_space=pl.ANY)],
+            out_specs=(VMEM, VMEM),
+            cost_estimate=pl.CostEstimate(flops=300_000_000, bytes_accessed=1_000_000, transcendentals=25_000),
+            name="bias",
+        )(ctx_1, fire_w1, fire_b1, w2_wide, after)
+
+    low = swap_groups(wide, low_groups).reshape(SIDE * CHUNK, -1)
+    bias_a, phase_a = bias_half(0, fine)
+    own4, wide4 = pl.pallas_call(
+        middle_kernel,
+        out_shape=(sums, payload),
+        in_specs=[VMEM, pl.BlockSpec(memory_space=pl.ANY)],
         out_specs=(VMEM, VMEM),
-        cost_estimate=pl.CostEstimate(flops=600_000_000, bytes_accessed=2_000_000, transcendentals=50_000),
-        name="bias",
-    )(ctx.reshape(1), fire_w1, fire_b1, w2_wide)
-
+        name="middle",
+    )(low, phase_a)
+    high = swap_groups(wide4, high_groups).reshape(SIDE * CHUNK, -1)
+    bias_b, phase_b = bias_half(HALF, own4)
     got0 = exchange(fine, 0)
     got1 = exchange(merge(fine, got0, bit[0]), 1)
-    low = swap_groups(jnp.broadcast_to(wide[None], (SIDE,) + wide.shape), low_groups)
-    low = low.reshape(SIDE * CHUNK, -1)
-    sib2 = sibling(low, (ctx >> 2) & 3)
-    low = pairs_summed(low)
-    sib3 = sibling(low, (ctx >> 3) & 1)
-    own4 = pairs_summed(low)
     got4 = exchange(own4, 4)
     got5 = exchange(merge(own4, got4, bit[4]), 5)
-    wide4 = pairs_summed(own4, 4)
-    high = swap_groups(jnp.broadcast_to(wide4[None], (SIDE,) + wide4.shape), high_groups)
-    high = high.reshape(SIDE * CHUNK, -1)
-    sib6 = sibling(high, (ctx >> 6) & 3)
-    sib7 = sibling(pairs_summed(high), (ctx >> 7) & 1)
-    siblings = jnp.concatenate([got0, got1, sib2, sib3, got4, got5, sib6, sib7], 0)
 
     attended, grad_q, own_grad, coarse, dscores = pl.pallas_call(
         main_kernel,
@@ -259,49 +322,49 @@
             shape((LEVELS * COARSE, 2 * WIDTH), f32),
             shape((HEADS, T, KEYS), f32),
         ),
-        in_specs=[SMEM] + [VMEM] * 6,
+        in_specs=[SMEM, SMEM] + [VMEM] * 12,
         out_specs=(VMEM,) * 5,
+        scratch_shapes=[pltpu.VMEM((LEVELS * COARSE, 2 * WIDTH + D), f32)],
         compiler_params=pltpu.CompilerParams(vmem_limit_bytes=32 * 2**20),
         name="attention",
-    )(lengths, queries, keys, values, grad_out, siblings, bias)
-    w_part = pl.pallas_call(
+    )(ctx_1, lengths, queries, keys, values, grad_out, got0, got1, low, got4, got5, high, bias_a, bias_b)
+    part = [coarse[k * COARSE : (k + 1) * COARSE] for k in range(LEVELS)]
+    keep4, send4 = halves(exchange(part[5], 5), bit[4])
+    keep0, send0 = halves(exchange(part[1], 1), bit[0])
+    away = pl.pallas_call(
         weight_kernel,
-        out_shape=shape((HEADS, D), f32),
-        in_specs=[SMEM, SMEM] + [VMEM] * 3,
+        out_shape=payload,
+        in_specs=[SMEM] * 3 + [VMEM] * 5,
         out_specs=VMEM,
         scratch_shapes=[pltpu.VMEM((4 * HEADS * SUB, HIDDEN * SUB), f32)],
         cost_estimate=pl.CostEstimate(flops=900_000_000, bytes_accessed=2_000_000, transcendentals=0),
         name="weights",
-    )(fire_w1, fire_b1, coef, dscores, phase)
-    w_part = w_part + lax.ppermute(w_part, "mp", [(0, 1), (1, 0)])
-
-    part = [coarse[k * COARSE : (k + 1) * COARSE] for k in range(LEVELS)]
-    none = jnp.zeros_like(part[0])
-    keep4, send4 = halves(exchange(part[5], 5), bit[4])
-    keep0, send0 = halves(exchange(part[1], 1), bit[0])
+    )(ctx_1, fire_w1, fire_b1, coef, dscores, phase_a, phase_b, coarse)
+    away = swap_groups(away, high_groups)
     came4 = exchange(part[4] + send4, 4)
     came0 = exchange(part[0] + send0, 0)
-    away = placed(placed(none, part[6], bit[6]), spread(part[7], 2), bit[7])
-    away = sent_back(away, w_part, high_groups)
-    group4 = keep4 + came4 + spread(away[:, : 2 * WIDTH], SIDE // 4)
-    near = placed(placed(none, part[2], bit[2]), spread(part[3], 2), bit[3])
-    near = sent_back(near + spread(group4, SIDE // 4), away[:, 2 * WIDTH :], low_groups)
-    back = keep0 + came0 + spread(near[:, : 2 * WIDTH], SIDE // 4)
-
-    token_live = (jnp.arange(T) < lengths[0]).astype(f32)[:, None]
-    token_grad = ((own_grad + spread(back, T // COARSE)) * token_live).astype(bf16)
-    w_all = near[:, 2 * WIDTH :]
+    near = pl.pallas_call(
+        return_kernel,
+        out_shape=payload,
+        in_specs=[SMEM] + [VMEM] * 4,
+        out_specs=VMEM,
+        name="return",
+    )(ctx_1, away, keep4, came4, coarse)
+    near = swap_groups(near, low_groups)
+    grad_k, grad_v = pl.pallas_call(
+        final_kernel,
+        out_shape=(shape((T, WIDTH), bf16), shape((T, WIDTH), bf16)),
+        in_specs=[SMEM] + [VMEM] * 4,
+        out_specs=(VMEM, VMEM),
+        name="final",
+    )(lengths, near, keep0, came0, own_grad)
+    w_all = near[:, :, 2 * WIDTH :]
+    w_all = (w_all[: SIDE // 2] + w_all[SIDE // 2 :]).sum(0)
+    w_all = w_all + lax.ppermute(w_all, "mp", [(0, 1), (1, 0)])
     grad_w2 = jnp.concatenate([w_all[:, :HIDDEN], w_all[:, HIDDEN : 2 * HIDDEN]], 0).T
     grad_w1 = w_all[:, 2 * HIDDEN : 3 * HIDDEN].sum(0)
     grad_b1 = w_all[:, 3 * HIDDEN :].sum(0)
-    return (attended, grad_q, token_grad[:, :WIDTH], token_grad[:, WIDTH:], grad_w1, grad_b1, grad_w2)
-
-
-def sent_back(rows, weights, groups):
-    rows = rows.reshape(SIDE, CHUNK, -1)
-    weights = jnp.broadcast_to(weights[None], (SIDE,) + weights.shape)
-    got = swap_groups(jnp.concatenate([rows, weights], 2), groups)
-    return (got[: SIDE // 2] + got[SIDE // 2 :]).sum(0)
+    return (attended, grad_q, grad_k, grad_v, grad_w1, grad_b1, grad_w2)
 
 
 def solution(mesh):

time: 129 us -> 125 us (0.969)
  the two profiles are of different devices: /device:TPU:16 before, /device:TPU:1 now
where the time goes in v3:
time: 125 us; the launch traced here: 124 us
  starting transfers between devices  71.6 us (57%)
  Pallas kernels  28.9 us (23%)
  waiting for transfers between devices  9.18 us (7%)
  local copies, waits for them, and re-layouts  8.04 us (6%)
  other arithmetic  4.28 us (3%)
  between operations  1.78 us (1%)
    all_to_all x4, starting transfers between devices, swap_groups(): return lax.all_to_all(value, 'ctx', 0, 0, axis_index_groups=groups)  35.3 us
    ppermute x8, starting transfers between devices, exchange(): return lax.ppermute(value, 'ctx', pairs)  28.1 us
    ppermute x1, starting transfers between devices, shards(): w_all = w_all + lax.ppermute(w_all, 'mp', [(0, 1), (1, 0)])  8.2 us
    all_to_all x4, waiting for transfers between devices, swap_groups(): return lax.all_to_all(value, 'ctx', 0, 0, axis_index_groups=groups)  8.04 us
    pallas_call x2, Pallas kernels, bias_half(): pl.pallas_call(functools.partial(bias_kernel, first), out_shape=(shape((H...  7.8 us
    pallas_call x1, Pallas kernels, shards(): pl.pallas_call(weight_kernel, out_shape=payload, in_specs=[SMEM] * 3 + [V...  6.81 us
    pallas_call x1, Pallas kernels, shards(): pl.pallas_call(main_kernel, out_shape=(shape((T, HEADS * D), bf16), shape...  6.36 us
    unnamed x36, local copies, waits for them, and re-layouts  5.15 us
  transfers between devices with their start and end apart: 13, of which 3 were waited for; matrix products, arithmetic and copies ran while one was open for 5% of the time, Pallas kernels for 15%

profile of v3, /device:TPU:1, one launch (start us, length us, event | category | flops | bytes accessed | tf_op | source)
XLA Modules:
  0.0 123.8 jit_solution(9802312466916723490)
XLA Ops:
  0.6 0.0 copy-start
  1.3 1.8 %leaf.1 = (f32[32,640]{1,0:T(8,128)}, f32[16,8,640]{2,1,0:T(8,128)}) custom-call(s32[1]{0:T(128)S(6)} %copy.15.len_ref, bf16[128,256]{1,0:T(8,128)(2,1)} %k_ref.3, bf16[128,256]{1,0:T(8,128)(2,1)} %v_ref.3), custom_call_target="tpu_custom_call" | custom-call | tf_op jit(solution)/shard_map/leaf/pallas_call | solution.py:282
  3.1 8.7 %all-to-all-start = ((f32[16,8,640]{2,1,0:T(8,128)}), f32[16,8,640]{2,1,0:T(8,128)S(1)}, u32[]{:S(2)}, u32[]{:S(2)}) async-start(f32[16,8,640]{2,1,0:T(8,128)} %get-tuple-element.23), calls=%async_computation | async-start | bytes 655360 | tf_op jit(solution)/shard_map/all_to_all | solution.py:255
  11.8 3.3 %collective-permute-start = (f32[32,640]{1,0:T(8,128)}, f32[32,640]{1,0:T(8,128)S(1)}, u32[]{:S(2)}, u32[]{:S(2)}) collective-permute-start(f32[32,640]{1,0:T(8,128)} %get-tuple-element.22.after_ref), channel_id=1, source_target_pairs={{0,2},{2,0},{4,6},{6,4},{8,10},{10,8},{12,14},{14,12},{16,18},{18,... | collective-permute-start | bytes 245768 | tf_op jit(solution)/shard_map/ppermute | solution.py:39
  15.1 0.7 broadcast_select_fusion.6
  15.8 0.1 pad_maximum_fusion.3
  15.9 0.1 pad_maximum_fusion.4
  15.9 0.2 broadcast_multiply_fusion
  16.1 0.1 maximum_bitcast_fusion.1
  16.2 1.2 mul.24.w2_ref
  17.4 3.9 %bias.2 = (f32[8,64,384]{2,1,0:T(8,128)}, f32[64,384]{1,0:T(8,128)}) custom-call(s32[1]{0:T(128)} %bitcast.ctx_ref, f32[32]{0:T(128)} %w1_ref.5, f32[32]{0:T(128)} %b1_ref.5, f32[64,256]{1,0:T(8,128)} %mul.24.w2_ref, f32[32,640]{1,0:T(8,128)} %get-tuple-element.22.after_ref), custom_call_target="tpu_custom_call" | custom-call | flops 300000000 | bytes 1000000 | tf_op jit(solution)/shard_map/bias/pallas_call | solution.py:291
  21.2 0.7 copy-done.1
  22.0 2.2 %middle.1 = (f32[32,640]{1,0:T(8,128)}, f32[16,8,640]{2,1,0:T(8,128)}) custom-call(f32[128,640]{1,0:T(8,128)} %bitcast.13, f32[64,384]{1,0:T(8,128)} %get-tuple-element.24.after_ref.phase_a_ref), custom_call_target="tpu_custom_call" | custom-call | tf_op jit(solution)/shard_map/middle/pallas_call | solution.py:302
  24.1 12.4 %all-to-all-start.1 = ((f32[16,8,640]{2,1,0:T(8,128)}), f32[16,8,640]{2,1,0:T(8,128)S(1)}, u32[]{:S(2)}, u32[]{:S(2)}) async-start(f32[16,8,640]{2,1,0:T(8,128)} %get-tuple-element.26), calls=%async_computation.1 | async-start | bytes 655360 | tf_op jit(solution)/shard_map/all_to_all | solution.py:255
  36.6 4.5 %collective-permute-start.2 = (f32[32,640]{1,0:T(8,128)}, f32[32,640]{1,0:T(8,128)S(1)}, u32[]{:S(2)}, u32[]{:S(2)}) collective-permute-start(f32[32,640]{1,0:T(8,128)} %get-tuple-element.25.after_ref), channel_id=1, source_target_pairs={{0,48},{2,50},{4,52},{6,54},{8,56},{10,58},{12,60},{14,62},{16,32}... | collective-permute-start | bytes 245768 | tf_op jit(solution)/shard_map/ppermute | solution.py:39
  41.2 0.0 copy-start.6
  41.2 0.1 reshape.59
  41.3 0.2 reduce_sum.45
  41.5 4.2 %collective-permute-start.1 = (f32[32,640]{1,0:T(8,128)S(1)}, f32[32,640]{1,0:T(8,128)S(1)}, u32[]{:S(2)}, u32[]{:S(2)}) collective-permute-start(f32[32,640]{1,0:T(8,128)S(1)} %reduce_sum.45), channel_id=1, source_target_pairs={{0,4},{2,6},{4,0},{6,2},{8,12},{10,14},{12,8},{14,10},{16,20},{18,... | collective-permute-start | bytes 245768 | tf_op jit(solution)/shard_map/ppermute | solution.py:39
  45.8 0.1 reshape.61
  45.9 0.2 reduce_sum.46
  46.1 3.1 %collective-permute-start.3 = (f32[32,640]{1,0:T(8,128)S(1)}, f32[32,640]{1,0:T(8,128)S(1)}, u32[]{:S(2)}, u32[]{:S(2)}) collective-permute-start(f32[32,640]{1,0:T(8,128)S(1)} %reduce_sum.46), channel_id=1, source_target_pairs={{0,64},{2,66},{4,68},{6,70},{8,72},{10,74},{12,76},{14,78},{16,80}... | collective-permute-start | bytes 245768 | tf_op jit(solution)/shard_map/ppermute | solution.py:39
  49.2 0.6 pad_maximum_fusion.2.coef_ref
  49.8 3.9 %bias.3 = (f32[8,64,384]{2,1,0:T(8,128)}, f32[64,384]{1,0:T(8,128)}) custom-call(s32[1]{0:T(128)} %bitcast.ctx_ref, f32[32]{0:T(128)} %w1_ref.5, f32[32]{0:T(128)} %b1_ref.5, f32[64,256]{1,0:T(8,128)} %mul.24.w2_ref, f32[32,640]{1,0:T(8,128)} %get-tuple-element.25.after_ref), custom_call_target="tpu_custom_call" | custom-call | flops 300000000 | bytes 1000000 | tf_op jit(solution)/shard_map/bias/pallas_call | solution.py:291
  53.8 1.1 copy-done.5
  54.9 6.4 %attention.1 = (bf16[128,1024]{1,0:T(8,128)(2,1)}, bf16[128,1024]{1,0:T(8,128)(2,1)}, f32[128,512]{1,0:T(8,128)S(1)}, f32[256,512]{1,0:T(8,128)S(1)}, f32[8,128,384]{2,1,0:T(8,128)S(1)}) custom-call(s32[1]{0:T(128)} %bitcast.ctx_ref, s32[1]{0:T(128)S(6)} %copy.15.len_ref, bf16[128,1024]{1,0:T(8,128)(2,1)S(1)} %copy-done.6, bf16[128,256]{1,0:T(8,128)(2,1)S(1)} %copy-done.8, ...), custom_call_target="tpu_custom_call" | custom-call | tf_op jit(solution)/shard_map/attention/pallas_call | solution.py:316
  61.3 0.7 copy-done.10
  62.0 1.2 copy-done.11
  63.2 2.7 %collective-permute-start.6 = (f32[32,512]{1,0:T(8,128)S(1)}, f32[32,512]{1,0:T(8,128)S(1)}, u32[]{:S(2)}, u32[]{:S(2)}) collective-permute-start(f32[32,512]{1,0:T(8,128)S(1)} %get-tuple-element.41), channel_id=1, source_target_pairs={{0,4},{2,6},{4,0},{6,2},{8,12},{10,14},{12,8},{14,10},{16,20},{18,... | collective-permute-start | bytes 196616 | tf_op jit(solution)/shard_map/ppermute | solution.py:39
  65.9 1.9 %collective-permute-start.4 = (f32[32,512]{1,0:T(8,128)S(1)}, f32[32,512]{1,0:T(8,128)S(1)}, u32[]{:S(2)}, u32[]{:S(2)}) collective-permute-start(f32[32,512]{1,0:T(8,128)S(1)} %get-tuple-element.42), channel_id=1, source_target_pairs={{0,64},{2,66},{4,68},{6,70},{8,72},{10,74},{12,76},{14,78},{16,80}... | collective-permute-start | bytes 196616 | tf_op jit(solution)/shard_map/ppermute | solution.py:39
  67.8 6.8 %weights.1 = f32[16,8,640]{2,1,0:T(8,128)} custom-call(s32[1]{0:T(128)} %bitcast.ctx_ref, f32[32]{0:T(128)} %w1_ref.5, f32[32]{0:T(128)} %b1_ref.5, f32[2,8,128]{2,1,0:T(8,128)} %pad_maximum_fusion.2.coef_ref, f32[8,128,384]{2,1,0:T(8,128)} %copy-done.11, f32[64,384]{1,0:T(8,128)} %get-tuple-element.24.after_ref.phase_a_ref, ...), custom_call_target="tpu_custom_call" | custom-call | flops 900000000 | bytes 2000000 | tf_op jit(solution)/shard_map/weights/pallas_call | solution.py:334
  74.6 8.3 %all-to-all-start.2 = ((f32[16,8,640]{2,1,0:T(8,128)}), f32[16,8,640]{2,1,0:T(8,128)S(1)}, u32[]{:S(2)}, u32[]{:S(2)}) async-start(f32[16,8,640]{2,1,0:T(8,128)} %weights.1), calls=%async_computation.2 | async-start | bytes 655360 | tf_op jit(solution)/shard_map/all_to_all | solution.py:255
  83.2 0.9 slice_add_fusion
  84.1 4.5 %collective-permute-start.5 = (f32[32,512]{1,0:T(8,128)S(1)}, f32[32,512]{1,0:T(8,128)S(1)}, u32[]{:S(2)}, u32[]{:S(2)}) collective-permute-start(f32[32,512]{1,0:T(8,128)S(1)} %get-tuple-element.40), channel_id=1, source_target_pairs={{0,48},{2,50},{4,52},{6,54},{8,56},{10,58},{12,60},{14,62},{16,32}... | collective-permute-start | bytes 196616 | tf_op jit(solution)/shard_map/ppermute | solution.py:39
  88.6 0.7 select_n.96.keep_ref
  89.2 1.1 collective-permute-done.5.came_ref
  90.4 3.9 %all-to-all-done.2.away_ref = f32[16,8,640]{2,1,0:T(8,128)S(1)} async-done(((f32[16,8,640]{2,1,0:T(8,128)}), f32[16,8,640]{2,1,0:T(8,128)S(1)}, u32[]{:S(2)}, u32[]{:S(2)}) %all-to-all-start.2) | async-done | bytes 327712 | tf_op jit(solution)/shard_map/all_to_all | solution.py:255
  94.3 0.7 copy-done.13
  95.0 2.1 %return.1 = f32[16,8,640]{2,1,0:T(8,128)} custom-call(s32[1]{0:T(128)} %bitcast.ctx_ref, f32[16,8,640]{2,1,0:T(8,128)} %copy-done.13, f32[32,512]{1,0:T(8,128)} %select_n.96.keep_ref, f32[32,512]{1,0:T(8,128)} %copy-done.17, f32[256,512]{1,0:T(8,128)} %copy-done.3), custom_call_target="tpu_custom_call" | custom-call | tf_op jit(solution)/shard_map/return/pallas_call | solution.py:346
  97.2 5.9 %all-to-all-start.3 = ((f32[16,8,640]{2,1,0:T(8,128)}), f32[16,8,640]{2,1,0:T(8,128)S(1)}, u32[]{:S(2)}, u32[]{:S(2)}) async-start(f32[16,8,640]{2,1,0:T(8,128)} %return.1), calls=%async_computation.3 | async-start | bytes 655360 | tf_op jit(solution)/shard_map/all_to_all | solution.py:255
  103.1 4.0 %collective-permute-start.7 = (f32[32,512]{1,0:T(8,128)S(1)}, f32[32,512]{1,0:T(8,128)S(1)}, u32[]{:S(2)}, u32[]{:S(2)}) collective-permute-start(f32[32,512]{1,0:T(8,128)S(1)} %get-tuple-element.39), channel_id=1, source_target_pairs={{0,2},{2,0},{4,6},{6,4},{8,10},{10,8},{12,14},{14,12},{16,18},{18,... | collective-permute-start | bytes 196616 | tf_op jit(solution)/shard_map/ppermute | solution.py:39
  107.1 4.1 %all-to-all-done.3.near_ref = f32[16,8,640]{2,1,0:T(8,128)S(1)} async-done(((f32[16,8,640]{2,1,0:T(8,128)}), f32[16,8,640]{2,1,0:T(8,128)S(1)}, u32[]{:S(2)}, u32[]{:S(2)}) %all-to-all-start.3) | async-done | bytes 327712 | tf_op jit(solution)/shard_map/all_to_all | solution.py:255
  111.2 8.2 %collective-permute-start.8 = (f32[8,128]{1,0:T(8,128)S(1)}, f32[8,128]{1,0:T(8,128)S(1)}, u32[]{:S(2)}, u32[]{:S(2)}) collective-permute-start(f32[8,128]{1,0:T(8,128)S(1)} %fusion), channel_id=1, source_target_pairs={{0,1},{1,0},{2,3},{3,2},{4,5},{5,4},{6,7},{7,6},{8,9},{9,8},{10,11... | collective-permute-start | bytes 12296 | tf_op jit(solution)/shard_map/ppermute | solution.py:363
  119.4 0.7 select_n.101.keep_ref
  120.1 0.6 copy-done.16
  120.7 1.8 %final.1 = (bf16[128,256]{1,0:T(8,128)(2,1)}, bf16[128,256]{1,0:T(8,128)(2,1)}) custom-call(s32[1]{0:T(128)S(6)} %copy.15.len_ref, f32[16,8,640]{2,1,0:T(8,128)} %copy-done.12, f32[32,512]{1,0:T(8,128)} %select_n.101.keep_ref, f32[32,512]{1,0:T(8,128)} %copy-done.16, f32[128,512]{1,0:T(8,128)} %copy-done.10), custom_call_target="tpu_custom_call" | custom-call | tf_op jit(solution)/shard_map/final/pallas_call | solution.py:354
  122.6 0.6 slice_reduce_fusion
  123.2 0.6 maximum_bitcast_fusion
  (56 shorter events, 0.4 us)
Async XLA Ops:
  0.6 14.4 %copy-start = (f32[32,16]{0,1:T(8,128)S(1)}, f32[32,16]{0,1:T(8,128)}, u32[]{:S(2)}) copy-start(f32[32,16]{0,1:T(8,128)} %param.14) | copy-start | bytes 6148
  3.1 18.2 %all-to-all-start = ((f32[16,8,640]{2,1,0:T(8,128)}), f32[16,8,640]{2,1,0:T(8,128)S(1)}, u32[]{:S(2)}, u32[]{:S(2)}) async-start(f32[16,8,640]{2,1,0:T(8,128)} %get-tuple-element.23), calls=%async_computation | async-start | bytes 655360 | tf_op jit(solution)/shard_map/all_to_all | solution.py:255
  11.8 24.8 %collective-permute-start = (f32[32,640]{1,0:T(8,128)}, f32[32,640]{1,0:T(8,128)S(1)}, u32[]{:S(2)}, u32[]{:S(2)}) collective-permute-start(f32[32,640]{1,0:T(8,128)} %get-tuple-element.22.after_ref), channel_id=1, source_target_pairs={{0,2},{2,0},{4,6},{6,4},{8,10},{10,8},{12,14},{14,12},{16,18},{18,... | collective-permute-start | bytes 245768 | tf_op jit(solution)/shard_map/ppermute | solution.py:39
  16.2 20.4 %copy-start.14 = (f32[32,640]{1,0:T(8,128)S(1)}, f32[32,640]{1,0:T(8,128)}, u32[]{:S(2)}) copy-start(f32[32,640]{1,0:T(8,128)} %get-tuple-element.22.after_ref) | copy-start | bytes 245764
  21.2 0.7 copy-start.1
  24.1 21.6 %copy-start.15 = (f32[32,640]{1,0:T(8,128)S(1)}, f32[32,640]{1,0:T(8,128)}, u32[]{:S(2)}) copy-start(f32[32,640]{1,0:T(8,128)} %get-tuple-element.25.after_ref) | copy-start | bytes 245764
  24.1 29.6 %all-to-all-start.1 = ((f32[16,8,640]{2,1,0:T(8,128)}), f32[16,8,640]{2,1,0:T(8,128)S(1)}, u32[]{:S(2)}, u32[]{:S(2)}) async-start(f32[16,8,640]{2,1,0:T(8,128)} %get-tuple-element.26), calls=%async_computation.1 | async-start | bytes 655360 | tf_op jit(solution)/shard_map/all_to_all | solution.py:255
  36.6 9.1 %collective-permute-start.2 = (f32[32,640]{1,0:T(8,128)}, f32[32,640]{1,0:T(8,128)S(1)}, u32[]{:S(2)}, u32[]{:S(2)}) collective-permute-start(f32[32,640]{1,0:T(8,128)} %get-tuple-element.25.after_ref), channel_id=1, source_target_pairs={{0,48},{2,50},{4,52},{6,54},{8,56},{10,58},{12,60},{14,62},{16,32}... | collective-permute-start | bytes 245768 | tf_op jit(solution)/shard_map/ppermute | solution.py:39
  41.1 12.6 %copy-start.2 = (f32[16,8,640]{2,1,0:T(8,128)S(1)}, f32[16,8,640]{2,1,0:T(8,128)}, u32[]{:S(2)}) copy-start(f32[16,8,640]{2,1,0:T(8,128)} %copy-done.1) | copy-start | bytes 983044
  41.1 12.6 %copy-start.4 = (f32[8,64,384]{2,1,0:T(8,128)S(1)}, f32[8,64,384]{2,1,0:T(8,128)}, u32[]{:S(2)}) copy-start(f32[8,64,384]{2,1,0:T(8,128)} %get-tuple-element.27.bias_a_ref) | copy-start | bytes 2359300
  41.2 12.6 %copy-start.6 = (bf16[128,1024]{1,0:T(8,128)(2,1)S(1)}, bf16[128,1024]{1,0:T(8,128)(2,1)}, u32[]{:S(2)}) copy-start(bf16[128,1024]{1,0:T(8,128)(2,1)} %q_ref.1) | copy-start | bytes 786436
  41.2 12.6 %copy-start.7 = (bf16[128,1024]{1,0:T(8,128)(2,1)S(1)}, bf16[128,1024]{1,0:T(8,128)(2,1)}, u32[]{:S(2)}) copy-start(bf16[128,1024]{1,0:T(8,128)(2,1)} %g_ref.1) | copy-start | bytes 786436
  41.2 12.6 %copy-start.8 = (bf16[128,256]{1,0:T(8,128)(2,1)S(1)}, bf16[128,256]{1,0:T(8,128)(2,1)}, u32[]{:S(2)}) copy-start(bf16[128,256]{1,0:T(8,128)(2,1)} %k_ref.3) | copy-start | bytes 196612
  41.2 12.6 %copy-start.9 = (bf16[128,256]{1,0:T(8,128)(2,1)S(1)}, bf16[128,256]{1,0:T(8,128)(2,1)}, u32[]{:S(2)}) copy-start(bf16[128,256]{1,0:T(8,128)(2,1)} %v_ref.3) | copy-start | bytes 196612
  41.5 12.2 %collective-permute-start.1 = (f32[32,640]{1,0:T(8,128)S(1)}, f32[32,640]{1,0:T(8,128)S(1)}, u32[]{:S(2)}, u32[]{:S(2)}) collective-permute-start(f32[32,640]{1,0:T(8,128)S(1)} %reduce_sum.45), channel_id=1, source_target_pairs={{0,4},{2,6},{4,0},{6,2},{8,12},{10,14},{12,8},{14,10},{16,20},{18,... | collective-permute-start | bytes 245768 | tf_op jit(solution)/shard_map/ppermute | solution.py:39
  46.1 7.6 %collective-permute-start.3 = (f32[32,640]{1,0:T(8,128)S(1)}, f32[32,640]{1,0:T(8,128)S(1)}, u32[]{:S(2)}, u32[]{:S(2)}) collective-permute-start(f32[32,640]{1,0:T(8,128)S(1)} %reduce_sum.46), channel_id=1, source_target_pairs={{0,64},{2,66},{4,68},{6,70},{8,72},{10,74},{12,76},{14,78},{16,80}... | collective-permute-start | bytes 245768 | tf_op jit(solution)/shard_map/ppermute | solution.py:39
  53.8 1.1 copy-start.5
  61.3 0.7 copy-start.10
  62.0 1.2 copy-start.11
  63.2 4.6 %copy-start.3 = (f32[256,512]{1,0:T(8,128)}, f32[256,512]{1,0:T(8,128)S(1)}, u32[]{:S(2)}) copy-start(f32[256,512]{1,0:T(8,128)S(1)} %get-tuple-element.33.coarse_ref) | copy-start | bytes 1572868
  63.2 19.7 %collective-permute-start.6 = (f32[32,512]{1,0:T(8,128)S(1)}, f32[32,512]{1,0:T(8,128)S(1)}, u32[]{:S(2)}, u32[]{:S(2)}) collective-permute-start(f32[32,512]{1,0:T(8,128)S(1)} %get-tuple-element.41), channel_id=1, source_target_pairs={{0,4},{2,6},{4,0},{6,2},{8,12},{10,14},{12,8},{14,10},{16,20},{18,... | collective-permute-start | bytes 196616 | tf_op jit(solution)/shard_map/ppermute | solution.py:39
  65.9 17.2 %collective-permute-start.4 = (f32[32,512]{1,0:T(8,128)S(1)}, f32[32,512]{1,0:T(8,128)S(1)}, u32[]{:S(2)}, u32[]{:S(2)}) collective-permute-start(f32[32,512]{1,0:T(8,128)S(1)} %get-tuple-element.42), channel_id=1, source_target_pairs={{0,64},{2,66},{4,68},{6,70},{8,72},{10,74},{12,76},{14,78},{16,80}... | collective-permute-start | bytes 196616 | tf_op jit(solution)/shard_map/ppermute | solution.py:39
  74.6 19.7 %all-to-all-start.2 = ((f32[16,8,640]{2,1,0:T(8,128)}), f32[16,8,640]{2,1,0:T(8,128)S(1)}, u32[]{:S(2)}, u32[]{:S(2)}) async-start(f32[16,8,640]{2,1,0:T(8,128)} %weights.1), calls=%async_computation.2 | async-start | bytes 655360 | tf_op jit(solution)/shard_map/all_to_all | solution.py:255
  84.1 6.3 %collective-permute-start.5 = (f32[32,512]{1,0:T(8,128)S(1)}, f32[32,512]{1,0:T(8,128)S(1)}, u32[]{:S(2)}, u32[]{:S(2)}) collective-permute-start(f32[32,512]{1,0:T(8,128)S(1)} %get-tuple-element.40), channel_id=1, source_target_pairs={{0,48},{2,50},{4,52},{6,54},{8,56},{10,58},{12,60},{14,62},{16,32}... | collective-permute-start | bytes 196616 | tf_op jit(solution)/shard_map/ppermute | solution.py:39
  90.4 3.9 %copy-start.17 = (f32[32,512]{1,0:T(8,128)}, f32[32,512]{1,0:T(8,128)S(1)}, u32[]{:S(2)}) copy-start(f32[32,512]{1,0:T(8,128)S(1)} %collective-permute-done.5.came_ref) | copy-start | bytes 196612
  94.3 0.7 copy-start.13
  97.2 14.0 %all-to-all-start.3 = ((f32[16,8,640]{2,1,0:T(8,128)}), f32[16,8,640]{2,1,0:T(8,128)S(1)}, u32[]{:S(2)}, u32[]{:S(2)}) async-start(f32[16,8,640]{2,1,0:T(8,128)} %return.1), calls=%async_computation.3 | async-start | bytes 655360 | tf_op jit(solution)/shard_map/all_to_all | solution.py:255
  103.1 17.0 %collective-permute-start.7 = (f32[32,512]{1,0:T(8,128)S(1)}, f32[32,512]{1,0:T(8,128)S(1)}, u32[]{:S(2)}, u32[]{:S(2)}) collective-permute-start(f32[32,512]{1,0:T(8,128)S(1)} %get-tuple-element.39), channel_id=1, source_target_pairs={{0,2},{2,0},{4,6},{6,4},{8,10},{10,8},{12,14},{14,12},{16,18},{18,... | collective-permute-start | bytes 196616 | tf_op jit(solution)/shard_map/ppermute | solution.py:39
  111.2 8.9 %copy-start.12 = (f32[16,8,640]{2,1,0:T(8,128)}, f32[16,8,640]{2,1,0:T(8,128)S(1)}, u32[]{:S(2)}) copy-start(f32[16,8,640]{2,1,0:T(8,128)S(1)} %all-to-all-done.3.near_ref) | copy-start | bytes 983044
  111.2 11.4 %collective-permute-start.8 = (f32[8,128]{1,0:T(8,128)S(1)}, f32[8,128]{1,0:T(8,128)S(1)}, u32[]{:S(2)}, u32[]{:S(2)}) collective-permute-start(f32[8,128]{1,0:T(8,128)S(1)} %fusion), channel_id=1, source_target_pairs={{0,1},{1,0},{2,3},{3,2},{4,5},{5,4},{6,7},{7,6},{8,9},{9,8},{10,11... | collective-permute-start | bytes 12296 | tf_op jit(solution)/shard_map/ppermute | solution.py:363
  120.1 0.6 copy-start.16

commit v4 on v2

v4 whole, which is shorter than its diff:
```python
import functools

import jax
import jax.numpy as jnp
from jax import lax
from jax.experimental import pallas as pl
from jax.experimental.pallas import tpu as pltpu
from jax.sharding import PartitionSpec as P

D = 128
COARSE = 32
T = 128
LEVELS = 8
KEYS = T + LEVELS * COARSE
HIDDEN = 32
HEADS = 8
KV = 2
GROUP = HEADS // KV
SUB = 8
BATCH = 4
UNROLL = 2
CHUNK = 8
SIDE = 16
WIDTH = KV * D
LEVEL_TOKENS = float(T * 2**LEVELS)
SCALE = D ** (-0.5)
MASKS = (1, 2, 6, 8, 24, 32, 64, 192)
NT = (((1,), (1,)), ((), ()))
TN = (((0,), (0,)), ((), ()))
VMEM = pl.BlockSpec(memory_space=pltpu.VMEM)
SMEM = pl.BlockSpec(memory_space=pltpu.SMEM)
HBM = pl.BlockSpec(memory_space=pltpu.HBM)
ANY = pl.BlockSpec(memory_space=pl.ANY)
SMALL = pltpu.CompilerParams(vmem_limit_bytes=12 * 2**20)


def dot(a, b, dims=(((1,), (0,)), ((), ()))):
    return lax.dot_general(a, b, dims, preferred_element_type=jnp.float32)


def shifted(value, mask):
    return lax.ppermute(value, "ctx", [(i, i ^ mask) for i in range(lax.axis_size("ctx"))])


def exchange(value, level):
    return shifted(value, MASKS[level])


def fetch(pairs, sems):
    copies = [pltpu.make_async_copy(src, dst, sems.at[n]) for n, (src, dst) in enumerate(pairs)]
    for copy in copies:
        copy.start()
    return copies


def leaf_kernel(len_ref, k_hbm, v_hbm, fine_ref, wide_ref, k_ref, v_ref, sems):
    copies = fetch([(k_hbm, k_ref), (v_hbm, v_ref)], sems)
    row = lax.broadcasted_iota(jnp.int32, (COARSE + CHUNK, T), 0)
    tok = lax.broadcasted_iota(jnp.int32, (COARSE + CHUNK, T), 1)
    run = jnp.where(row < COARSE, tok // (T // COARSE), tok // (T // CHUNK) + COARSE)
    member = jnp.where((run == row) & (tok < len_ref[0]), 1.0, 0.0)
    member_b = member.astype(jnp.bfloat16)
    count = jnp.broadcast_to(jnp.sum(member, axis=1, keepdims=True), (COARSE + CHUNK, D))
    for copy in copies:
        copy.wait()
    rows = jnp.concatenate([dot(member_b, k_ref[...]), dot(member_b, v_ref[...]), count], axis=1)
    fine_ref[...] = rows[:COARSE, : 2 * WIDTH]
    for n in range(SIDE):
        wide_ref[n] = rows[COARSE:]


def exact_dot(a, b, dims=(((1,), (0,)), ((), ()))):
    return lax.dot_general(a, b, dims, precision=lax.Precision.HIGHEST, preferred_element_type=jnp.float32)


def unit_weights(core, w2_ref, rows, columns, by_row, by_column):
    shape = (rows, 2 * HEADS)
    head = lax.broadcasted_iota(jnp.int32, shape, 0) // by_row + core * HEADS
    pick = jnp.where(lax.broadcasted_iota(jnp.int32, shape, 1) == head, 1.0, 0.0)
    return exact_dot(exact_dot(pick, w2_ref[...]), unit_columns(columns, by_column))


def unit_columns(columns, by):
    unit = lax.broadcasted_iota(jnp.int32, (HIDDEN, columns), 0)
    column = lax.broadcasted_iota(jnp.int32, (HIDDEN, columns), 1)
    return jnp.where(column // by % HIDDEN == unit, 1.0, 0.0)


def bias_kernel(
    place_ref, w1_hbm, b1_hbm, w2_hbm, after_ref, bias_ref, phase_ref, line_ref, slot_ref, w1_ref, b1_ref, w2_ref, sems
):
    copies = fetch([(w1_hbm, w1_ref), (b1_hbm, b1_ref), (w2_hbm, w2_ref)], sems)
    ctx, core = place_ref[0], place_ref[1]
    col = lax.broadcasted_iota(jnp.int32, (1, KEYS), 1)
    level = (col - T) // COARSE
    pos = col.astype(jnp.float32)
    for k in range(LEVELS):
        run = 2**k * T // COARSE
        start = ((ctx >> k) ^ 1) * 2**k * T - ctx * T
        inside = (col - T - k * COARSE) * run
        here = (start + inside).astype(jnp.float32) + (run - 1) / 2.0
        pos = jnp.where((col >= T) & (level == k), here, pos)
    top = jnp.log1p(jnp.full((1, KEYS), LEVEL_TOKENS, jnp.float32))
    row = lax.broadcasted_iota(jnp.int32, (T, KEYS), 0).astype(jnp.float32)
    phase_ref[...] = jnp.log1p(jnp.abs(row - pos)) / top
    for copy in copies:
        copy.wait()
    lane = lax.broadcasted_iota(jnp.int32, (HEADS, D), 1) // HIDDEN
    w2 = unit_weights(core, w2_ref, HEADS, D, 1, 1)
    spread = unit_columns(HIDDEN * SUB, SUB)
    for n, ref in enumerate((w1_ref, b1_ref)):
        line = jnp.broadcast_to(ref[...], (D, HIDDEN))
        line_ref[n] = exact_dot(spread, line, (((0,), (1,)), ((), ())))
        slot_ref[n] = jnp.where(lane == core, exact_dot(ref[...], unit_columns(D, 1)), jnp.where(lane == 2 + n, w2, 0.0))
    weight = unit_weights(core, w2_ref, HEADS * SUB, HIDDEN * SUB, SUB, SUB)
    row = lax.broadcasted_iota(jnp.int32, weight.shape, 0)
    column = lax.broadcasted_iota(jnp.int32, weight.shape, 1)
    weight = jnp.where(row % SUB == column % SUB, weight, 0.0)
    weight_high = weight.astype(jnp.bfloat16)
    weight_low = (weight - weight_high.astype(jnp.float32)).astype(jnp.bfloat16)
    weight_both = jnp.concatenate([weight_high, weight_low], axis=0)

    def body(i, carry):
        rows = pl.ds(pl.multiple_of(i * SUB, SUB), SUB)
        hidden = jnp.maximum(by_units(line_ref, phase_ref[rows, :]), 0.0)
        high = hidden.astype(jnp.bfloat16)
        low = (hidden - high.astype(jnp.float32)).astype(jnp.bfloat16)
        with_high = dot(weight_both, high)
        bias = with_high[: HEADS * SUB] + with_high[HEADS * SUB :] + dot(weight_high, low)
        for h in range(HEADS):
            bias_ref[h, rows, :] = bias[h * SUB : (h + 1) * SUB]
        return carry

    lax.fori_loop(0, T // SUB, body, 0, unroll=UNROLL)


def by_units(line_ref, phase):
    slope = line_ref[0].reshape(HIDDEN, SUB, D)
    offset = line_ref[1].reshape(HIDDEN, SUB, D)
    tiles = [phase[None, :, n * D : (n + 1) * D] * slope + offset for n in range(KEYS // D)]
    return jnp.concatenate(tiles, axis=2).reshape(HIDDEN * SUB, KEYS)


def pooled(rows, by):
    shape = (rows.shape[0] // by, rows.shape[0])
    row = lax.broadcasted_iota(jnp.int32, shape, 0)
    col = lax.broadcasted_iota(jnp.int32, shape, 1)
    return picked(jnp.where(col // by == row, 1.0, 0.0).astype(jnp.bfloat16), rows)


def middle_kernel(low_ref, after_bias_ref, after_merge_ref, own_ref, wide_ref):
    row = lax.broadcasted_iota(jnp.int32, (COARSE + CHUNK, SIDE * CHUNK), 0)
    col = lax.broadcasted_iota(jnp.int32, (COARSE + CHUNK, SIDE * CHUNK), 1)
    run = jnp.where(row < COARSE, col >> 2, (col >> 4) + COARSE)
    rows = picked(jnp.where(run == row, 1.0, 0.0).astype(jnp.bfloat16), low_ref[...])
    own_ref[...] = rows[:COARSE]
    for n in range(SIDE):
        wide_ref[n] = rows[COARSE:]


def main_kernel(
    place_ref, len_ref, q_hbm, k_hbm, v_hbm, g_hbm, got0_ref, got1_ref, low_ref, got4_ref, got5_ref, high_ref, bias_ref,
    out_ref, gq_ref, own_ref, coarse_ref, ds_ref, q_ref, k_ref, v_ref, g_ref, sib_ref, sems,
):
    copies = fetch([(k_hbm, k_ref), (q_hbm, q_ref), (v_hbm, v_ref), (g_hbm, g_ref)], sems)
    length = len_ref[0]
    ctx = place_ref[0]
    for level, ref in ((0, got0_ref), (1, got1_ref), (4, got4_ref), (5, got5_ref)):
        sib_ref[level * COARSE : (level + 1) * COARSE, : ref.shape[1]] = ref[...]
    for level, ref in ((2, low_ref), (6, high_ref)):
        start = pl.multiple_of((((ctx >> level) & 3) ^ 1) * COARSE, COARSE)
        sib_ref[level * COARSE : (level + 1) * COARSE, :] = ref[pl.ds(start, COARSE), :]
        start = pl.multiple_of((((ctx >> level + 1) & 1) ^ 1) * 2 * COARSE, 2 * COARSE)
        sib_ref[(level + 1) * COARSE : (level + 2) * COARSE, :] = pooled(ref[pl.ds(start, 2 * COARSE), :], 2)
    group = (((ctx >> 1) & 7) ^ 1) * 2
    blocks = ((0, COARSE, (ctx & 15) ^ 1), (COARSE, COARSE // 2, group), (COARSE * 3 // 2, COARSE // 2, group + 1))
    for first, rows, block in blocks:
        block = low_ref[pl.ds(pl.multiple_of(block * CHUNK, CHUNK), CHUNK), 2 * WIDTH :]
        run = T // rows
        before = lax.broadcasted_iota(jnp.int32, (rows, D), 0) * run
        here = jnp.sum(block, axis=0, keepdims=True) - before.astype(jnp.float32)
        sib_ref[first : first + rows, 2 * WIDTH :] = jnp.clip(here, 0.0, float(run))
    count = sib_ref[:, 2 * WIDTH :]
    inverse = 1.0 / jnp.maximum(count, 1.0)
    count_t = jnp.concatenate([count[:T].T[:1], count[T:].T[:1]], axis=1)
    token_live = lax.broadcasted_iota(jnp.int32, (1, T), 1) < length
    live = jnp.concatenate([token_live.astype(jnp.float32), count_t], axis=1) > 0.0
    row_live = lax.broadcasted_iota(jnp.int32, (T, 1), 0) < length
    for copy in copies:
        copy.wait()
    for j in range(KV):
        cols = slice(j * D, (j + 1) * D)
        vcols = slice((KV + j) * D, (KV + j + 1) * D)
        keys = jnp.concatenate([k_ref[:, cols], (sib_ref[:, cols] * inverse).astype(jnp.bfloat16)], axis=0)
        values = jnp.concatenate([v_ref[:, cols], (sib_ref[:, vcols] * inverse).astype(jnp.bfloat16)], axis=0)
        heads = range(j * GROUP, (j + 1) * GROUP)
        key_grads = jnp.zeros((KEYS, D), jnp.float32)
        value_grads = jnp.zeros((KEYS, D), jnp.float32)
        for first in range(j * GROUP, (j + 1) * GROUP, BATCH):
            heads = range(first, first + BATCH)
            query = jnp.concatenate([q_ref[:, h * D : (h + 1) * D] for h in heads], axis=0)
            grad = [g_ref[:, h * D : (h + 1) * D] for h in heads]
            grad = jnp.concatenate([jnp.where(row_live, part, jnp.zeros_like(part)) for part in grad], axis=0)
            scores = dot(query, keys, NT) * SCALE + bias_ref[first : first + BATCH].reshape(BATCH * T, KEYS)
            scores = jnp.where(live, scores, -jnp.inf)
            weights = jnp.exp(scores - jnp.max(scores, axis=1, keepdims=True))
            probs = weights * (1.0 / jnp.sum(weights, axis=1, keepdims=True))
            probs_b = probs.astype(jnp.bfloat16)
            attended = dot(probs_b, values)
            dprobs = dot(grad, values, NT)
            dscores = probs * (dprobs - jnp.sum(probs * dprobs, axis=1, keepdims=True))
            ds_ref[first : first + BATCH] = dscores.reshape(BATCH, T, KEYS)
            dscores_b = dscores.astype(jnp.bfloat16)
            grad_query = dot(dscores_b, keys) * SCALE
            for n, h in enumerate(heads):
                rows = slice(n * T, (n + 1) * T)
                out_ref[:, h * D : (h + 1) * D] = jnp.where(row_live, attended[rows], 0.0).astype(jnp.bfloat16)
                gq_ref[:, h * D : (h + 1) * D] = grad_query[rows].astype(jnp.bfloat16)
            key_grads = key_grads + dot(dscores_b, query, TN)
            value_grads = value_grads + dot(probs_b, grad, TN)
        key_grads = key_grads * SCALE
        own_ref[:, cols] = key_grads[:T]
        own_ref[:, vcols] = value_grads[:T]
        coarse_ref[:, cols] = key_grads[T:] * inverse
        coarse_ref[:, vcols] = value_grads[T:] * inverse


def weight_kernel(
    line_ref, slot_ref, ds_ref, phase_ref, out_ref, gq_ref, w_ref, out_hbm, gq_hbm, acc_ref, sems
):
    copies = fetch([(out_ref, out_hbm), (gq_ref, gq_hbm)], sems)
    acc_ref[...] = jnp.zeros_like(acc_ref)

    def body(i, carry):
        rows = pl.ds(pl.multiple_of(i * SUB, SUB), SUB)
        phase = phase_ref[rows, :]
        parts = [ds_ref[h, rows, :] for h in range(HEADS)]
        parts = jnp.concatenate(parts + [p * phase for p in parts], axis=0)
        high = parts.astype(jnp.bfloat16)
        low = (parts - high.astype(jnp.float32)).astype(jnp.bfloat16)
        both = jnp.concatenate([high, low], axis=0)
        active = jnp.where(by_units(line_ref, phase) > 0.0, 1.0, 0.0).astype(jnp.bfloat16)
        acc_ref[...] += dot(both, active, NT)
        return carry

    lax.fori_loop(0, T // SUB, body, 0, unroll=UNROLL)
    acc = acc_ref[...]
    rows = 2 * HEADS * SUB
    acc = acc[:rows] + acc[rows:]
    sub_row = lax.broadcasted_iota(jnp.int32, acc.shape, 0) % SUB
    sub_col = lax.broadcasted_iota(jnp.int32, acc.shape, 1) % SUB
    acc = jnp.where(sub_row == sub_col, acc, 0.0)
    acc = acc.reshape(2 * HEADS, SUB, HIDDEN * SUB).sum(axis=1)
    unit = lax.broadcasted_iota(jnp.int32, (HIDDEN * SUB, D), 0) // SUB
    lane = lax.broadcasted_iota(jnp.int32, (HIDDEN * SUB, D), 1) % HIDDEN
    sums = exact_dot(acc, jnp.where(unit == lane, 1.0, 0.0))
    w_ref[...] = slot_ref[1] * sums[:HEADS] + slot_ref[0] * sums[HEADS:]
    for copy in copies:
        copy.wait()


def chosen(rows, parts):
    sizes = [value.shape[0] for value, _ in parts]
    depth = -(-sum(sizes) // 16) * 16
    row = lax.broadcasted_iota(jnp.int32, (rows, 1), 0)
    col = lax.broadcasted_iota(jnp.int32, (rows, depth), 1)
    pick, first = col < 0, 0
    for size, (_, name) in zip(sizes, parts):
        pick = pick | (col == name(row, first))
        first += size
    pick = jnp.where(pick, 1.0, 0.0).astype(jnp.bfloat16)
    value = [value for value, _ in parts]
    if first < depth:
        value.append(jnp.zeros((depth - first, value[0].shape[1]), jnp.float32))
    return picked(pick, jnp.concatenate(value, axis=0))


def picked(pick, value):
    total = 0.0
    for _ in range(3):
        part = value.astype(jnp.bfloat16)
        total = total + dot(pick, part)
        value = value - part.astype(jnp.float32)
    return total


def level_parts(ctx, level, coarse_ref):
    quarter = (ctx >> level) & 3

    def near(i, first):
        return jnp.where(i >> 5 == quarter ^ 1, (i & 31) + first, -1)

    def far(i, first):
        return jnp.where(i >> 6 != quarter >> 1, ((i & 63) >> 1) + first, -1)

    return [
        (coarse_ref[level * COARSE : (level + 1) * COARSE, :], near),
        (coarse_ref[(level + 1) * COARSE : (level + 2) * COARSE, :], far),
    ]


def half_of(ctx, level, shift):
    return lambda i, first: first + ((ctx >> level) & 1) * (COARSE // 2) + (i >> shift)


def every(shift):
    return lambda i, first: first + (i >> shift)


def sibling_rows(ctx, level, coarse_ref, came_ref):
    return chosen(
        COARSE,
        [
            (coarse_ref[level * COARSE : (level + 1) * COARSE, :], every(0)),
            (came_ref[...], half_of(ctx ^ (1 << level), level, 1)),
        ],
    )


def fill(payload_ref, rows, weights):
    for n in range(SIDE):
        payload_ref[n, :, : 2 * WIDTH] = rows[n * CHUNK : (n + 1) * CHUNK]
        payload_ref[n, :, 2 * WIDTH :] = weights


def away_kernel(place_ref, w_ref, coarse_ref, came5_ref, away_ref, send_ref):
    ctx = place_ref[0]
    fill(away_ref, chosen(SIDE * CHUNK, level_parts(ctx, 6, coarse_ref)), w_ref[...])
    send_ref[...] = sibling_rows(ctx, 4, coarse_ref, came5_ref)


def summed(ref):
    return sum(ref[n] + ref[n + SIDE // 2] for n in range(SIDE // 2))


def return_kernel(place_ref, away_ref, came5_ref, came4_ref, came1_ref, coarse_ref, near_ref, send_ref):
    ctx = place_ref[0]
    away = summed(away_ref)
    parts = level_parts(ctx, 2, coarse_ref)
    parts += [(came5_ref[...], half_of(ctx, 4, 3)), (came4_ref[...], every(2))]
    parts += [(away[:, : 2 * WIDTH], every(4))]
    fill(near_ref, chosen(SIDE * CHUNK, parts), away[:, 2 * WIDTH :])
    send_ref[...] = sibling_rows(ctx, 0, coarse_ref, came1_ref)


def final_kernel(place_ref, len_ref, near_ref, came1_ref, came0_ref, own_ref, gk_ref, gv_ref):
    ctx = place_ref[0]
    near = sum(near_ref[n, :, : 2 * WIDTH] for n in range(SIDE))
    parts = [(came1_ref[...], half_of(ctx, 0, 3)), (came0_ref[...], every(2)), (near, every(4))]
    live = lax.broadcasted_iota(jnp.int32, (T, 1), 0) < len_ref[0]
    grad = jnp.where(live, own_ref[...] + chosen(T, parts), 0.0)
    gk_ref[...] = grad[:, :WIDTH].astype(jnp.bfloat16)
    gv_ref[...] = grad[:, WIDTH:].astype(jnp.bfloat16)


def outputs_kernel(mine_ref, got_ref, w1_ref, b1_ref, w2_ref):
    total = mine_ref[...] + got_ref[...]
    for core in range(2):
        w2_ref[core * HEADS : (core + 1) * HEADS, :] = total[:, core * HIDDEN : (core + 1) * HIDDEN]
    sums = jnp.sum(total, axis=0, keepdims=True)
    w1_ref[...] = sums[:, 2 * HIDDEN : 3 * HIDDEN]
    b1_ref[...] = sums[:, 3 * HIDDEN :]


def merge_kernel(place_ref, own_ref, got_ref, out_ref):
    shape = (COARSE, 2 * COARSE)
    row = lax.broadcasted_iota(jnp.int32, shape, 0)
    col = lax.broadcasted_iota(jnp.int32, shape, 1)
    upper = (place_ref[0] >> 4) & 1
    pick = jnp.where((row & 15 == (col & 31) >> 1) & (row >> 4 == (col >> 5) ^ upper), 1.0, 0.0)
    out_ref[...] = picked(pick.astype(jnp.bfloat16), jnp.concatenate([own_ref[...], got_ref[...]], axis=0))


def merge(own, got, upper):
    first = jnp.where(upper, got, own)
    second = jnp.where(upper, own, got)
    return jnp.concatenate([first, second], 0).reshape(COARSE, 2, -1).sum(1)


def in_hbm(value):
    return pltpu.with_memory_space_constraint(value, pltpu.HBM)


def swap_groups(value, groups):
    return lax.all_to_all(value, "ctx", 0, 0, axis_index_groups=groups)


def shards(queries, keys, values, lengths, fire_w1, fire_b1, fire_w2, grad_out):
    f32, bf16 = jnp.float32, jnp.bfloat16
    shape = jax.ShapeDtypeStruct
    ctx = lax.axis_index("ctx")
    mp = lax.axis_index("mp")
    place = jnp.stack([ctx, mp])
    bit = [(ctx >> k) & 1 == 1 for k in range(LEVELS)]
    blocks = range(SIDE)
    low_groups = [[high * SIDE + low for low in blocks] for high in blocks]
    high_groups = [[high * SIDE + (low ^ (8 * (high % 2))) for high in blocks] for low in blocks]

    payload = shape((SIDE, CHUNK, 2 * WIDTH + D), f32)
    sums = shape((COARSE, 2 * WIDTH + D), f32)
    rows = shape((COARSE, 2 * WIDTH), f32)
    dma = pltpu.SemaphoreType.DMA
    fine, wide = pl.pallas_call(
        leaf_kernel,
        out_shape=(rows, payload),
        in_specs=[SMEM, HBM, HBM],
        out_specs=(VMEM, VMEM),
        scratch_shapes=[pltpu.VMEM((T, WIDTH), bf16)] * 2 + [dma((2,))],
        compiler_params=SMALL,
        name="leaf",
    )(lengths, in_hbm(keys), in_hbm(values))
    low = swap_groups(wide, low_groups).reshape(SIDE * CHUNK, -1)
    got0 = exchange(fine, 0)
    own1 = merge(fine, got0, bit[0])
    wide_tokens, tokens = shape((T, HEADS * D), bf16), shape((T, WIDTH), bf16)
    bias, phase, line, slot = pl.pallas_call(
        bias_kernel,
        out_shape=(
            shape((HEADS, T, KEYS), f32),
            shape((T, KEYS), f32),
            shape((2, HIDDEN * SUB, D), f32),
            shape((2, HEADS, D), f32),
        ),
        in_specs=[SMEM] + [HBM] * 3 + [ANY],
        out_specs=(VMEM,) * 4,
        scratch_shapes=[
            pltpu.VMEM((1, HIDDEN), f32),
            pltpu.VMEM((1, HIDDEN), f32),
            pltpu.VMEM((2 * HEADS, HIDDEN), f32),
            dma((3,)),
        ],
        compiler_params=SMALL,
        cost_estimate=pl.CostEstimate(flops=600_000_000, bytes_accessed=2_000_000, transcendentals=50_000),
        name="bias",
    )(place, *map(in_hbm, (fire_w1.reshape(1, -1), fire_b1.reshape(1, -1), fire_w2.T)), fine)
    own4, wide4 = pl.pallas_call(
        middle_kernel,
        out_shape=(sums, payload),
        in_specs=[VMEM, ANY, ANY],
        out_specs=(VMEM, VMEM),
        compiler_params=SMALL,
        name="middle",
    )(low, slot, own1)
    high = swap_groups(wide4, high_groups).reshape(SIDE * CHUNK, -1)
    got4 = exchange(own4, 4)
    got1 = exchange(jnp.pad(own1, ((0, 0), (0, D))), 1)
    own5 = pl.pallas_call(
        merge_kernel,
        out_shape=sums,
        in_specs=[SMEM, VMEM, VMEM],
        out_specs=VMEM,
        compiler_params=SMALL,
        name="merge",
    )(place, own4, got4)
    got5 = exchange(own5, 5)

    attended, grad_q, own_grad, coarse, dscores = pl.pallas_call(
        main_kernel,
        out_shape=(
            wide_tokens,
            wide_tokens,
            shape((T, 2 * WIDTH), f32),
            shape((LEVELS * COARSE, 2 * WIDTH), f32),
            shape((HEADS, T, KEYS), f32),
        ),
        in_specs=[SMEM, SMEM] + [HBM] * 4 + [VMEM] * 7,
        out_specs=(VMEM,) * 5,
        scratch_shapes=[pltpu.VMEM((T, n), bf16) for n in (HEADS * D, WIDTH, WIDTH, HEADS * D)]
        + [pltpu.VMEM((LEVELS * COARSE, 2 * WIDTH + D), f32), dma((4,))],
        compiler_params=SMALL,
        name="attention",
    )(place, lengths, *map(in_hbm, (queries, keys, values, grad_out)), got0, got1, low, got4, got5, high, bias)

    came5 = exchange(coarse[5 * COARSE : 6 * COARSE], 5)
    w_part, attended, grad_q = pl.pallas_call(
        weight_kernel,
        out_shape=(shape((HEADS, D), f32), wide_tokens, wide_tokens),
        in_specs=[VMEM] * 6,
        out_specs=(VMEM, HBM, HBM),
        scratch_shapes=[pltpu.VMEM((4 * HEADS * SUB, HIDDEN * SUB), f32), dma((2,))],
        compiler_params=SMALL,
        cost_estimate=pl.CostEstimate(flops=900_000_000, bytes_accessed=2_000_000, transcendentals=0),
        name="weights",
    )(line, slot, dscores, phase, attended, grad_q)
    away, send4 = pl.pallas_call(
        away_kernel,
        out_shape=(payload, rows),
        in_specs=[SMEM] + [VMEM] * 3,
        out_specs=(VMEM, VMEM),
        compiler_params=SMALL,
        name="away",
    )(place, w_part, coarse, came5)
    away = swap_groups(away, high_groups)
    came4 = exchange(send4, 4)
    came1 = exchange(coarse[COARSE : 2 * COARSE], 1)
    near, send0 = pl.pallas_call(
        return_kernel,
        out_shape=(payload, rows),
        in_specs=[SMEM] + [VMEM] * 5,
        out_specs=(VMEM, VMEM),
        compiler_params=SMALL,
        name="return",
    )(place, away, came5, came4, came1, coarse)
    near = swap_groups(near, low_groups)
    came0 = exchange(send0, 0)
    w_all = near[:, :, 2 * WIDTH :]
    w_all = (w_all[: SIDE // 2] + w_all[SIDE // 2 :]).sum(0)
    w_other = lax.ppermute(w_all, "mp", [(0, 1), (1, 0)])
    grad_k, grad_v = pl.pallas_call(
        final_kernel,
        out_shape=(tokens, tokens),
        in_specs=[SMEM, SMEM] + [VMEM] * 4,
        out_specs=(VMEM, VMEM),
        compiler_params=SMALL,
        name="final",
    )(place, lengths, near, came1, came0, own_grad)
    grad_w1, grad_b1, grad_w2 = pl.pallas_call(
        outputs_kernel,
        out_shape=(shape((1, HIDDEN), f32), shape((1, HIDDEN), f32), shape((2 * HEADS, HIDDEN), f32)),
        in_specs=[VMEM] * 2,
        out_specs=(VMEM,) * 3,
        compiler_params=SMALL,
        name="outputs",
    )(w_all, w_other)
    grad_w1, grad_b1, grad_w2 = grad_w1.reshape(-1), grad_b1.reshape(-1), grad_w2.T
    return (attended, grad_q, grad_k, grad_v, grad_w1, grad_b1, grad_w2)


def solution(mesh):
    split = P("ctx", "mp")
    return jax.shard_map(
        shards,
        mesh=mesh,
        in_specs=(split, split, split, P("ctx"), P(), P(), P(), split),
        out_specs=(split, split, split, split, P(), P(), P()),
        check_vma=False,
    )
```

time: 129 us -> 108 us (0.84)
  the two profiles are of different devices: /device:TPU:16 before, /device:TPU:1 now
where the time goes in v4:
time: 108 us
  starting transfers between devices  72.6 us (67%)
  Pallas kernels  20.7 us (19%)
  waiting for transfers between devices  12.5 us (12%)
  between operations  1.54 us (1%)
    all_to_all x4, starting transfers between devices, swap_groups(): return lax.all_to_all(value, 'ctx', 0, 0, axis_index_groups=groups)  36.8 us
    ppermute x8, starting transfers between devices, shifted(): lax.ppermute(value, 'ctx', [(i, i ^ mask) for i in range(lax.axis_size('c...  28 us
    ppermute x1, starting transfers between devices, shards(): w_other = lax.ppermute(w_all, 'mp', [(0, 1), (1, 0)])  7.74 us
    all_to_all x4, waiting for transfers between devices, swap_groups(): return lax.all_to_all(value, 'ctx', 0, 0, axis_index_groups=groups)  6.77 us
    ppermute x8, waiting for transfers between devices, shifted(): lax.ppermute(value, 'ctx', [(i, i ^ mask) for i in range(lax.axis_size('c...  5.71 us
    pallas_call x1, Pallas kernels, shards(): pl.pallas_call(bias_kernel, out_shape=(shape((HEADS, T, KEYS), f32), shap...  4.76 us
    pallas_call x1, Pallas kernels, shards(): pl.pallas_call(main_kernel, out_shape=(wide_tokens, wide_tokens, shape((T...  4.34 us
    pallas_call x1, Pallas kernels, shards(): pl.pallas_call(weight_kernel, out_shape=(shape((HEADS, D), f32), wide_tok...  2.84 us
  transfers between devices with their start and end apart: 13, of which 5 were waited for; matrix products, arithmetic and copies ran while one was open for 0% of the time, Pallas kernels for 9%

profile of v4, /device:TPU:1, one launch (start us, length us, event | category | flops | bytes accessed | tf_op | source)
XLA Modules:
  0.0 107.6 jit_solution(59151268264440426)
XLA Ops:
  1.3 1.8 %leaf.1 = (f32[32,512]{1,0:T(8,128)S(1)}, f32[16,8,640]{2,1,0:T(8,128)}) custom-call(s32[1]{0:T(128)S(6)} %copy.15.len_ref, bf16[128,256]{1,0:T(8,128)(2,1)} %k_hbm.3, bf16[128,256]{1,0:T(8,128)(2,1)} %v_hbm.3), custom_call_target="tpu_custom_call" | custom-call | tf_op jit(solution)/shard_map/leaf/pallas_call | solution.py:403
  3.1 8.7 %all-to-all-start = ((f32[16,8,640]{2,1,0:T(8,128)}), f32[16,8,640]{2,1,0:T(8,128)S(1)}, u32[]{:S(2)}, u32[]{:S(2)}) async-start(f32[16,8,640]{2,1,0:T(8,128)} %get-tuple-element.35), calls=%async_computation | async-start | bytes 655360 | tf_op jit(solution)/shard_map/all_to_all | solution.py:385
  11.8 3.3 %collective-permute-start = (f32[32,512]{1,0:T(8,128)S(1)}, f32[32,512]{1,0:T(8,128)S(1)}, u32[]{:S(2)}, u32[]{:S(2)}) collective-permute-start(f32[32,512]{1,0:T(8,128)S(1)} %get-tuple-element.32.after_ref), channel_id=1, source_target_pairs={{0,2},{2,0},{4,6},{6,4},{8,10},{10,8},{12,14},{14,12},{16,18},{18,... | collective-permute-start | bytes 196616 | tf_op jit(solution)/shard_map/ppermute | solution.py:42
  15.0 0.1 pad_add_fusion.place_ref
  15.1 4.8 %bias.1 = (f32[8,128,384]{2,1,0:T(8,128)S(1)}, f32[128,384]{1,0:T(8,128)S(1)}, f32[2,256,128]{2,1,0:T(8,128)S(1)}, f32[2,8,128]{2,1,0:T(8,128)S(1)}) custom-call(s32[2]{0:T(128)S(1)} %pad_add_fusion.place_ref, f32[1,32]{1,0:T(1,128)} %bitcast.15, f32[1,32]{1,0:T(1,128)} %bitcast.16, f32[16,32]{1,0:T(8,128)} %bitcast.13, ...), custom_call_target="tpu_custom_call" | custom-call | flops 600000000 | bytes 2000000 | tf_op jit(solution)/shard_map/bias/pallas_call | solution.py:416
  19.9 0.0 copy-start
  19.9 1.5 %collective-permute-done.got0_ref = f32[32,512]{1,0:T(8,128)S(1)} collective-permute-done((f32[32,512]{1,0:T(8,128)S(1)}, f32[32,512]{1,0:T(8,128)S(1)}, u32[]{:S(2)}, u32[]{:S(2)}) %collective-permute-start) | collective-permute-done | bytes 65568 | tf_op jit(solution)/shard_map/ppermute | solution.py:42
  21.4 0.1 reshape.37
  21.5 0.2 reduce_sum.18.after_merge_ref
  21.7 0.0 all-to-all-done
  21.7 1.0 middle.1
  22.6 12.7 %all-to-all-start.1 = ((f32[16,8,640]{2,1,0:T(8,128)}), f32[16,8,640]{2,1,0:T(8,128)S(1)}, u32[]{:S(2)}, u32[]{:S(2)}) async-start(f32[16,8,640]{2,1,0:T(8,128)} %get-tuple-element.37), calls=%async_computation.1 | async-start | bytes 655360 | tf_op jit(solution)/shard_map/all_to_all | solution.py:385
  35.3 4.5 %collective-permute-start.2 = (f32[32,640]{1,0:T(8,128)S(1)}, f32[32,640]{1,0:T(8,128)S(1)}, u32[]{:S(2)}, u32[]{:S(2)}) collective-permute-start(f32[32,640]{1,0:T(8,128)S(1)} %get-tuple-element.36.own_ref), channel_id=1, source_target_pairs={{0,48},{2,50},{4,52},{6,54},{8,56},{10,58},{12,60},{14,62},{16,32}... | collective-permute-start | bytes 245768 | tf_op jit(solution)/shard_map/ppermute | solution.py:42
  39.8 3.3 %collective-permute-start.1 = (f32[32,640]{1,0:T(8,128)S(1)}, f32[32,640]{1,0:T(8,128)S(1)}, u32[]{:S(2)}, u32[]{:S(2)}) collective-permute-start(f32[32,640]{1,0:T(8,128)S(1)} %pad.4), channel_id=1, source_target_pairs={{0,4},{2,6},{4,0},{6,2},{8,12},{10,14},{12,8},{14,10},{16,20},{18,... | collective-permute-start | bytes 245768 | tf_op jit(solution)/shard_map/ppermute | solution.py:42
  43.1 0.0 collective-permute-done.2.got_ref.got4_ref
  43.1 0.7 merge.1
  43.8 3.1 %collective-permute-start.3 = (f32[32,640]{1,0:T(8,128)S(1)}, f32[32,640]{1,0:T(8,128)S(1)}, u32[]{:S(2)}, u32[]{:S(2)}) collective-permute-start(f32[32,640]{1,0:T(8,128)S(1)} %merge.1), channel_id=1, source_target_pairs={{0,64},{2,66},{4,68},{6,70},{8,72},{10,74},{12,76},{14,78},{16,80}... | collective-permute-start | bytes 245768 | tf_op jit(solution)/shard_map/ppermute | solution.py:42
  46.9 0.0 collective-permute-done.1.got1_ref
  46.9 2.4 %collective-permute-done.3.got5_ref = f32[32,640]{1,0:T(8,128)S(1)} collective-permute-done((f32[32,640]{1,0:T(8,128)S(1)}, f32[32,640]{1,0:T(8,128)S(1)}, u32[]{:S(2)}, u32[]{:S(2)}) %collective-permute-start.3) | collective-permute-done | bytes 81952 | tf_op jit(solution)/shard_map/ppermute | solution.py:42
  49.3 0.0 all-to-all-done.1
  49.3 0.0 copy-done
  49.3 0.0 copy-start.1
  49.3 4.3 %attention.1 = (bf16[128,1024]{1,0:T(8,128)(2,1)S(1)}, bf16[128,1024]{1,0:T(8,128)(2,1)S(1)}, f32[128,512]{1,0:T(8,128)S(1)}, f32[256,512]{1,0:T(8,128)S(1)}, f32[8,128,384]{2,1,0:T(8,128)S(1)}) custom-call(s32[2]{0:T(128)S(1)} %pad_add_fusion.place_ref, s32[1]{0:T(128)S(6)} %copy.15.len_ref, bf16[128,1024]{1,0:T(8,128)(2,1)} %q_hbm.1, ...), custom_call_target="tpu_custom_call" | custom-call | tf_op jit(solution)/shard_map/attention/pallas_call | solution.py:457
  53.7 3.1 %collective-permute-start.4 = (f32[32,512]{1,0:T(8,128)S(1)}, f32[32,512]{1,0:T(8,128)S(1)}, u32[]{:S(2)}, u32[]{:S(2)}) collective-permute-start(f32[32,512]{1,0:T(8,128)S(1)} %get-tuple-element.58), channel_id=1, source_target_pairs={{0,64},{2,66},{4,68},{6,70},{8,72},{10,74},{12,76},{14,78},{16,80}... | collective-permute-start | bytes 196616 | tf_op jit(solution)/shard_map/ppermute | solution.py:42
  56.7 0.0 copy-done.1
  56.8 2.8 %weights.1 = (f32[8,128]{1,0:T(8,128)S(1)}, bf16[128,1024]{1,0:T(8,128)(2,1)}, bf16[128,1024]{1,0:T(8,128)(2,1)}) custom-call(f32[2,256,128]{2,1,0:T(8,128)S(1)} %copy-done.1, f32[2,8,128]{2,1,0:T(8,128)S(1)} %get-tuple-element.34.after_bias_ref.slot_ref, f32[8,128,384]{2,1,0:T(8,128)S(1)} %get-tuple-element.39.ds_ref, ...), custom_call_target="tpu_custom_call" | custom-call | flops 900000000 | bytes 2000000 | tf_op jit(solution)/shard_map/weights/pallas_call | solution.py:475
  59.6 0.0 collective-permute-done.4.came5_ref
  59.6 1.5 %away.1 = (f32[16,8,640]{2,1,0:T(8,128)}, f32[32,512]{1,0:T(8,128)S(1)}) custom-call(s32[2]{0:T(128)S(1)} %pad_add_fusion.place_ref, f32[8,128]{1,0:T(8,128)S(1)} %get-tuple-element.45.w_ref, f32[256,512]{1,0:T(8,128)S(1)} %get-tuple-element.46.coarse_ref, f32[32,512]{1,0:T(8,128)S(1)} %collective-permute-done.4.came5_ref), custom_call_target="tpu_custom_call" | custom-call | tf_op jit(solution)/shard_map/away/pallas_call | solution.py:485
  61.2 7.0 %all-to-all-start.2 = ((f32[16,8,640]{2,1,0:T(8,128)}), f32[16,8,640]{2,1,0:T(8,128)S(1)}, u32[]{:S(2)}, u32[]{:S(2)}) async-start(f32[16,8,640]{2,1,0:T(8,128)} %get-tuple-element.47), calls=%async_computation.2 | async-start | bytes 655360 | tf_op jit(solution)/shard_map/all_to_all | solution.py:385
  68.2 3.1 %collective-permute-start.6 = (f32[32,512]{1,0:T(8,128)S(1)}, f32[32,512]{1,0:T(8,128)S(1)}, u32[]{:S(2)}, u32[]{:S(2)}) collective-permute-start(f32[32,512]{1,0:T(8,128)S(1)} %get-tuple-element.57), channel_id=1, source_target_pairs={{0,4},{2,6},{4,0},{6,2},{8,12},{10,14},{12,8},{14,10},{16,20},{18,... | collective-permute-start | bytes 196616 | tf_op jit(solution)/shard_map/ppermute | solution.py:42
  71.3 4.5 %collective-permute-start.5 = (f32[32,512]{1,0:T(8,128)S(1)}, f32[32,512]{1,0:T(8,128)S(1)}, u32[]{:S(2)}, u32[]{:S(2)}) collective-permute-start(f32[32,512]{1,0:T(8,128)S(1)} %get-tuple-element.48), channel_id=1, source_target_pairs={{0,48},{2,50},{4,52},{6,54},{8,56},{10,58},{12,60},{14,62},{16,32}... | collective-permute-start | bytes 196616 | tf_op jit(solution)/shard_map/ppermute | solution.py:42
  75.8 0.0 collective-permute-done.6.came1_ref
  75.8 1.9 %collective-permute-done.5.came4_ref = f32[32,512]{1,0:T(8,128)S(1)} collective-permute-done((f32[32,512]{1,0:T(8,128)S(1)}, f32[32,512]{1,0:T(8,128)S(1)}, u32[]{:S(2)}, u32[]{:S(2)}) %collective-permute-start.5) | collective-permute-done | bytes 65568 | tf_op jit(solution)/shard_map/ppermute | solution.py:42
  77.6 1.9 %all-to-all-done.2.away_ref = f32[16,8,640]{2,1,0:T(8,128)S(1)} async-done(((f32[16,8,640]{2,1,0:T(8,128)}), f32[16,8,640]{2,1,0:T(8,128)S(1)}, u32[]{:S(2)}, u32[]{:S(2)}) %all-to-all-start.2) | async-done | bytes 327712 | tf_op jit(solution)/shard_map/all_to_all | solution.py:385
  79.6 1.6 %return.1 = (f32[16,8,640]{2,1,0:T(8,128)}, f32[32,512]{1,0:T(8,128)S(1)}) custom-call(s32[2]{0:T(128)S(1)} %pad_add_fusion.place_ref, f32[16,8,640]{2,1,0:T(8,128)S(1)} %all-to-all-done.2.away_ref, f32[32,512]{1,0:T(8,128)S(1)} %collective-permute-done.4.came5_ref, f32[32,512]{1,0:T(8,128)S(1)} %collective-permute-done.5.came4_ref, ...), custom_call_target="tpu_custom_call" | custom-call | tf_op jit(solution)/shard_map/return/pallas_call | solution.py:496
  81.2 8.4 %all-to-all-start.3 = ((f32[16,8,640]{2,1,0:T(8,128)}), f32[16,8,640]{2,1,0:T(8,128)S(1)}, u32[]{:S(2)}, u32[]{:S(2)}) async-start(f32[16,8,640]{2,1,0:T(8,128)} %get-tuple-element.49), calls=%async_computation.3 | async-start | bytes 655360 | tf_op jit(solution)/shard_map/all_to_all | solution.py:385
  89.6 3.3 %collective-permute-start.7 = (f32[32,512]{1,0:T(8,128)S(1)}, f32[32,512]{1,0:T(8,128)S(1)}, u32[]{:S(2)}, u32[]{:S(2)}) collective-permute-start(f32[32,512]{1,0:T(8,128)S(1)} %get-tuple-element.50), channel_id=1, source_target_pairs={{0,2},{2,0},{4,6},{6,4},{8,10},{10,8},{12,14},{14,12},{16,18},{18,... | collective-permute-start | bytes 196616 | tf_op jit(solution)/shard_map/ppermute | solution.py:42
  92.9 4.8 %all-to-all-done.3.near_ref = f32[16,8,640]{2,1,0:T(8,128)S(1)} async-done(((f32[16,8,640]{2,1,0:T(8,128)}), f32[16,8,640]{2,1,0:T(8,128)S(1)}, u32[]{:S(2)}, u32[]{:S(2)}) %all-to-all-start.3) | async-done | bytes 327712 | tf_op jit(solution)/shard_map/all_to_all | solution.py:385
  97.7 7.7 %collective-permute-start.8 = (f32[8,128]{1,0:T(8,128)S(1)}, f32[8,128]{1,0:T(8,128)S(1)}, u32[]{:S(2)}, u32[]{:S(2)}) collective-permute-start(f32[8,128]{1,0:T(8,128)S(1)} %fusion.mine_ref), channel_id=1, source_target_pairs={{0,1},{1,0},{2,3},{3,2},{4,5},{5,4},{6,7},{7,6},{8,9},{9,8},{10,11... | collective-permute-start | bytes 12296 | tf_op jit(solution)/shard_map/ppermute | solution.py:508
  105.5 0.0 collective-permute-done.7.came0_ref
  105.5 1.5 %final.1 = (bf16[128,256]{1,0:T(8,128)(2,1)}, bf16[128,256]{1,0:T(8,128)(2,1)}) custom-call(s32[2]{0:T(128)S(1)} %pad_add_fusion.place_ref, s32[1]{0:T(128)S(6)} %copy.15.len_ref, f32[16,8,640]{2,1,0:T(8,128)S(1)} %all-to-all-done.3.near_ref, f32[32,512]{1,0:T(8,128)S(1)} %collective-permute-done.6.came1_ref, ...), custom_call_target="tpu_custom_call" | custom-call | tf_op jit(solution)/shard_map/final/pallas_call | solution.py:509
  107.0 0.0 collective-permute-done.8.got_ref
  107.0 0.7 outputs.1
  (5 shorter events, 0.1 us)
Async XLA Ops:
  3.1 18.6 %all-to-all-start = ((f32[16,8,640]{2,1,0:T(8,128)}), f32[16,8,640]{2,1,0:T(8,128)S(1)}, u32[]{:S(2)}, u32[]{:S(2)}) async-start(f32[16,8,640]{2,1,0:T(8,128)} %get-tuple-element.35), calls=%async_computation | async-start | bytes 655360 | tf_op jit(solution)/shard_map/all_to_all | solution.py:385
  11.8 9.6 %collective-permute-start = (f32[32,512]{1,0:T(8,128)S(1)}, f32[32,512]{1,0:T(8,128)S(1)}, u32[]{:S(2)}, u32[]{:S(2)}) collective-permute-start(f32[32,512]{1,0:T(8,128)S(1)} %get-tuple-element.32.after_ref), channel_id=1, source_target_pairs={{0,2},{2,0},{4,6},{6,4},{8,10},{10,8},{12,14},{14,12},{16,18},{18,... | collective-permute-start | bytes 196616 | tf_op jit(solution)/shard_map/ppermute | solution.py:42
  19.9 29.4 %copy-start = (f32[2,256,128]{2,1,0:T(8,128)}, f32[2,256,128]{2,1,0:T(8,128)S(1)}, u32[]{:S(2)}) copy-start(f32[2,256,128]{2,1,0:T(8,128)S(1)} %get-tuple-element.33.line_ref) | copy-start | bytes 786436
  22.6 26.6 %all-to-all-start.1 = ((f32[16,8,640]{2,1,0:T(8,128)}), f32[16,8,640]{2,1,0:T(8,128)S(1)}, u32[]{:S(2)}, u32[]{:S(2)}) async-start(f32[16,8,640]{2,1,0:T(8,128)} %get-tuple-element.37), calls=%async_computation.1 | async-start | bytes 655360 | tf_op jit(solution)/shard_map/all_to_all | solution.py:385
  35.3 7.8 %collective-permute-start.2 = (f32[32,640]{1,0:T(8,128)S(1)}, f32[32,640]{1,0:T(8,128)S(1)}, u32[]{:S(2)}, u32[]{:S(2)}) collective-permute-start(f32[32,640]{1,0:T(8,128)S(1)} %get-tuple-element.36.own_ref), channel_id=1, source_target_pairs={{0,48},{2,50},{4,52},{6,54},{8,56},{10,58},{12,60},{14,62},{16,32}... | collective-permute-start | bytes 245768 | tf_op jit(solution)/shard_map/ppermute | solution.py:42
  39.8 7.1 %collective-permute-start.1 = (f32[32,640]{1,0:T(8,128)S(1)}, f32[32,640]{1,0:T(8,128)S(1)}, u32[]{:S(2)}, u32[]{:S(2)}) collective-permute-start(f32[32,640]{1,0:T(8,128)S(1)} %pad.4), channel_id=1, source_target_pairs={{0,4},{2,6},{4,0},{6,2},{8,12},{10,14},{12,8},{14,10},{16,20},{18,... | collective-permute-start | bytes 245768 | tf_op jit(solution)/shard_map/ppermute | solution.py:42
  43.8 5.5 %collective-permute-start.3 = (f32[32,640]{1,0:T(8,128)S(1)}, f32[32,640]{1,0:T(8,128)S(1)}, u32[]{:S(2)}, u32[]{:S(2)}) collective-permute-start(f32[32,640]{1,0:T(8,128)S(1)} %merge.1), channel_id=1, source_target_pairs={{0,64},{2,66},{4,68},{6,70},{8,72},{10,74},{12,76},{14,78},{16,80}... | collective-permute-start | bytes 245768 | tf_op jit(solution)/shard_map/ppermute | solution.py:42
  49.3 7.5 %copy-start.1 = (f32[2,256,128]{2,1,0:T(8,128)S(1)}, f32[2,256,128]{2,1,0:T(8,128)}, u32[]{:S(2)}) copy-start(f32[2,256,128]{2,1,0:T(8,128)} %copy-done) | copy-start | bytes 786436
  53.7 6.0 %collective-permute-start.4 = (f32[32,512]{1,0:T(8,128)S(1)}, f32[32,512]{1,0:T(8,128)S(1)}, u32[]{:S(2)}, u32[]{:S(2)}) collective-permute-start(f32[32,512]{1,0:T(8,128)S(1)} %get-tuple-element.58), channel_id=1, source_target_pairs={{0,64},{2,66},{4,68},{6,70},{8,72},{10,74},{12,76},{14,78},{16,80}... | collective-permute-start | bytes 196616 | tf_op jit(solution)/shard_map/ppermute | solution.py:42
  61.2 18.4 %all-to-all-start.2 = ((f32[16,8,640]{2,1,0:T(8,128)}), f32[16,8,640]{2,1,0:T(8,128)S(1)}, u32[]{:S(2)}, u32[]{:S(2)}) async-start(f32[16,8,640]{2,1,0:T(8,128)} %get-tuple-element.47), calls=%async_computation.2 | async-start | bytes 655360 | tf_op jit(solution)/shard_map/all_to_all | solution.py:385
  68.2 7.6 %collective-permute-start.6 = (f32[32,512]{1,0:T(8,128)S(1)}, f32[32,512]{1,0:T(8,128)S(1)}, u32[]{:S(2)}, u32[]{:S(2)}) collective-permute-start(f32[32,512]{1,0:T(8,128)S(1)} %get-tuple-element.57), channel_id=1, source_target_pairs={{0,4},{2,6},{4,0},{6,2},{8,12},{10,14},{12,8},{14,10},{16,20},{18,... | collective-permute-start | bytes 196616 | tf_op jit(solution)/shard_map/ppermute | solution.py:42
  71.3 6.3 %collective-permute-start.5 = (f32[32,512]{1,0:T(8,128)S(1)}, f32[32,512]{1,0:T(8,128)S(1)}, u32[]{:S(2)}, u32[]{:S(2)}) collective-permute-start(f32[32,512]{1,0:T(8,128)S(1)} %get-tuple-element.48), channel_id=1, source_target_pairs={{0,48},{2,50},{4,52},{6,54},{8,56},{10,58},{12,60},{14,62},{16,32}... | collective-permute-start | bytes 196616 | tf_op jit(solution)/shard_map/ppermute | solution.py:42
  81.2 16.5 %all-to-all-start.3 = ((f32[16,8,640]{2,1,0:T(8,128)}), f32[16,8,640]{2,1,0:T(8,128)S(1)}, u32[]{:S(2)}, u32[]{:S(2)}) async-start(f32[16,8,640]{2,1,0:T(8,128)} %get-tuple-element.49), calls=%async_computation.3 | async-start | bytes 655360 | tf_op jit(solution)/shard_map/all_to_all | solution.py:385
  89.6 15.9 %collective-permute-start.7 = (f32[32,512]{1,0:T(8,128)S(1)}, f32[32,512]{1,0:T(8,128)S(1)}, u32[]{:S(2)}, u32[]{:S(2)}) collective-permute-start(f32[32,512]{1,0:T(8,128)S(1)} %get-tuple-element.50), channel_id=1, source_target_pairs={{0,2},{2,0},{4,6},{6,4},{8,10},{10,8},{12,14},{14,12},{16,18},{18,... | collective-permute-start | bytes 196616 | tf_op jit(solution)/shard_map/ppermute | solution.py:42
  97.7 9.2 %collective-permute-start.8 = (f32[8,128]{1,0:T(8,128)S(1)}, f32[8,128]{1,0:T(8,128)S(1)}, u32[]{:S(2)}, u32[]{:S(2)}) collective-permute-start(f32[8,128]{1,0:T(8,128)S(1)} %fusion.mine_ref), channel_id=1, source_target_pairs={{0,1},{1,0},{2,3},{3,2},{4,5},{5,4},{6,7},{7,6},{8,9},{9,8},{10,11... | collective-permute-start | bytes 12296 | tf_op jit(solution)/shard_map/ppermute | solution.py:508

commit v5 on v4

--- a/solution.py
+++ b/solution.py
@@ -21,6 +21,7 @@
 UNROLL = 2
 CHUNK = 8
 SIDE = 16
+FIRST = {"low": 12, "high": 12, "away": 3, "near": 2}
 WIDTH = KV * D
 LEVEL_TOKENS = float(T * 2**LEVELS)
 SCALE = D ** (-0.5)
@@ -151,7 +152,8 @@
 def middle_kernel(low_ref, after_bias_ref, after_merge_ref, own_ref, wide_ref):
     row = lax.broadcasted_iota(jnp.int32, (COARSE + CHUNK, SIDE * CHUNK), 0)
     col = lax.broadcasted_iota(jnp.int32, (COARSE + CHUNK, SIDE * CHUNK), 1)
-    run = jnp.where(row < COARSE, col >> 2, (col >> 4) + COARSE)
+    member = (col >> 3) ^ FIRST["low"]
+    run = jnp.where(row < COARSE, (member << 1) + ((col & 7) >> 2), (member >> 1) + COARSE)
     rows = picked(jnp.where(run == row, 1.0, 0.0).astype(jnp.bfloat16), low_ref[...])
     own_ref[...] = rows[:COARSE]
     for n in range(SIDE):
@@ -167,15 +169,19 @@
     ctx = place_ref[0]
     for level, ref in ((0, got0_ref), (1, got1_ref), (4, got4_ref), (5, got5_ref)):
         sib_ref[level * COARSE : (level + 1) * COARSE, : ref.shape[1]] = ref[...]
-    for level, ref in ((2, low_ref), (6, high_ref)):
-        start = pl.multiple_of((((ctx >> level) & 3) ^ 1) * COARSE, COARSE)
+    for level, ref, first in ((2, low_ref, FIRST["low"] >> 2), (6, high_ref, FIRST["high"] >> 2)):
+        quarter = ((ctx >> level) & 3) ^ 1
+        start = pl.multiple_of((quarter ^ first) * COARSE, COARSE)
         sib_ref[level * COARSE : (level + 1) * COARSE, :] = ref[pl.ds(start, COARSE), :]
-        start = pl.multiple_of((((ctx >> level + 1) & 1) ^ 1) * 2 * COARSE, 2 * COARSE)
-        sib_ref[(level + 1) * COARSE : (level + 2) * COARSE, :] = pooled(ref[pl.ds(start, 2 * COARSE), :], 2)
+        for n in range(2):
+            quarter = (((ctx >> level + 1) & 1) ^ 1) * 2 + n
+            start = pl.multiple_of((quarter ^ first) * COARSE, COARSE)
+            place = (level + 1) * COARSE + n * COARSE // 2
+            sib_ref[place : place + COARSE // 2, :] = pooled(ref[pl.ds(start, COARSE), :], 2)
     group = (((ctx >> 1) & 7) ^ 1) * 2
     blocks = ((0, COARSE, (ctx & 15) ^ 1), (COARSE, COARSE // 2, group), (COARSE * 3 // 2, COARSE // 2, group + 1))
     for first, rows, block in blocks:
-        block = low_ref[pl.ds(pl.multiple_of(block * CHUNK, CHUNK), CHUNK), 2 * WIDTH :]
+        block = low_ref[pl.ds(pl.multiple_of((block ^ FIRST["low"]) * CHUNK, CHUNK), CHUNK), 2 * WIDTH :]
         run = T // rows
         before = lax.broadcasted_iota(jnp.int32, (rows, D), 0) * run
         here = jnp.sum(block, axis=0, keepdims=True) - before.astype(jnp.float32)
@@ -317,15 +323,15 @@
     )
 
 
-def fill(payload_ref, rows, weights):
+def fill(payload_ref, first, rows, weights):
     for n in range(SIDE):
-        payload_ref[n, :, : 2 * WIDTH] = rows[n * CHUNK : (n + 1) * CHUNK]
-        payload_ref[n, :, 2 * WIDTH :] = weights
+        payload_ref[n ^ first, :, : 2 * WIDTH] = rows[n * CHUNK : (n + 1) * CHUNK]
+        payload_ref[n ^ first, :, 2 * WIDTH :] = weights
 
 
 def away_kernel(place_ref, w_ref, coarse_ref, came5_ref, away_ref, send_ref):
     ctx = place_ref[0]
-    fill(away_ref, chosen(SIDE * CHUNK, level_parts(ctx, 6, coarse_ref)), w_ref[...])
+    fill(away_ref, FIRST["away"], chosen(SIDE * CHUNK, level_parts(ctx, 6, coarse_ref)), w_ref[...])
     send_ref[...] = sibling_rows(ctx, 4, coarse_ref, came5_ref)
 
 
@@ -339,7 +345,7 @@
     parts = level_parts(ctx, 2, coarse_ref)
     parts += [(came5_ref[...], half_of(ctx, 4, 3)), (came4_ref[...], every(2))]
     parts += [(away[:, : 2 * WIDTH], every(4))]
-    fill(near_ref, chosen(SIDE * CHUNK, parts), away[:, 2 * WIDTH :])
+    fill(near_ref, FIRST["near"] ^ (((ctx >> 4) & 1) * 8), chosen(SIDE * CHUNK, parts), away[:, 2 * WIDTH :])
     send_ref[...] = sibling_rows(ctx, 0, coarse_ref, came1_ref)
 
 
@@ -393,8 +399,12 @@
     place = jnp.stack([ctx, mp])
     bit = [(ctx >> k) & 1 == 1 for k in range(LEVELS)]
     blocks = range(SIDE)
-    low_groups = [[high * SIDE + low for low in blocks] for high in blocks]
-    high_groups = [[high * SIDE + (low ^ (8 * (high % 2))) for high in blocks] for low in blocks]
+    def low_groups(first, odd=0):
+        return [[high * SIDE + (low ^ first ^ (odd * (high % 2))) for low in blocks] for high in blocks]
+
+    def high_groups(first):
+        order = [high ^ first for high in blocks]
+        return [[high * SIDE + (low ^ (8 * (high % 2))) for high in order] for low in blocks]
 
     payload = shape((SIDE, CHUNK, 2 * WIDTH + D), f32)
     sums = shape((COARSE, 2 * WIDTH + D), f32)
@@ -409,7 +419,7 @@
         compiler_params=SMALL,
         name="leaf",
     )(lengths, in_hbm(keys), in_hbm(values))
-    low = swap_groups(wide, low_groups).reshape(SIDE * CHUNK, -1)
+    low = swap_groups(wide, low_groups(FIRST["low"])).reshape(SIDE * CHUNK, -1)
     got0 = exchange(fine, 0)
     own1 = merge(fine, got0, bit[0])
     wide_tokens, tokens = shape((T, HEADS * D), bf16), shape((T, WIDTH), bf16)
@@ -441,7 +451,7 @@
         compiler_params=SMALL,
         name="middle",
     )(low, slot, own1)
-    high = swap_groups(wide4, high_groups).reshape(SIDE * CHUNK, -1)
+    high = swap_groups(wide4, high_groups(FIRST["high"])).reshape(SIDE * CHUNK, -1)
     got4 = exchange(own4, 4)
     got1 = exchange(jnp.pad(own1, ((0, 0), (0, D))), 1)
     own5 = pl.pallas_call(
@@ -490,7 +500,7 @@
         compiler_params=SMALL,
         name="away",
     )(place, w_part, coarse, came5)
-    away = swap_groups(away, high_groups)
+    away = swap_groups(away, high_groups(FIRST["away"]))
     came4 = exchange(send4, 4)
     came1 = exchange(coarse[COARSE : 2 * COARSE], 1)
     near, send0 = pl.pallas_call(
@@ -501,7 +511,7 @@
         compiler_params=SMALL,
         name="return",
     )(place, away, came5, came4, came1, coarse)
-    near = swap_groups(near, low_groups)
+    near = swap_groups(near, low_groups(FIRST["near"], 8))
     came0 = exchange(send0, 0)
     w_all = near[:, :, 2 * WIDTH :]
     w_all = (w_all[: SIDE // 2] + w_all[SIDE // 2 :]).sum(0)

time: 108 us -> 104 us (0.963)
  starting transfers between devices: 72.6 us -> 67.2 us
  waiting for transfers between devices: 12.5 us -> 13.7 us
    ppermute x8, starting transfers between devices: 28 us -> 20.1 us  [shifted(): lax.ppermute(value, 'ctx', [(i, i ^ mask) for i in range(lax.axis_size('c...]
    all_to_all x4, starting transfers between devices: 36.8 us -> 39.2 us  [swap_groups(): return lax.all_to_all(value, 'ctx', 0, 0, axis_index_groups=groups)]
    ppermute x8, waiting for transfers between devices: 5.71 us -> 7.86 us  [shifted(): lax.ppermute(value, 'ctx', [(i, i ^ mask) for i in range(lax.axis_size('c...]
  transfers between devices with their start and end apart: 13 -> 13, of which waited for: 5 -> 7; matrix products, arithmetic and copies ran while one was open for 0% -> 0% of each run, Pallas kernels for 9% -> 9%
where the time goes in v5:
time: 104 us; the launch traced here: 103 us
  starting transfers between devices  67.2 us (65%)
  Pallas kernels  20.5 us (20%)
  waiting for transfers between devices  13.7 us (13%)
  between operations  1.5 us (1%)
    all_to_all x4, starting transfers between devices, swap_groups(): return lax.all_to_all(value, 'ctx', 0, 0, axis_index_groups=groups)  39.2 us
    ppermute x8, starting transfers between devices, shifted(): lax.ppermute(value, 'ctx', [(i, i ^ mask) for i in range(lax.axis_size('c...  20.1 us
    ppermute x1, starting transfers between devices, shards(): w_other = lax.ppermute(w_all, 'mp', [(0, 1), (1, 0)])  7.92 us
    ppermute x8, waiting for transfers between devices, shifted(): lax.ppermute(value, 'ctx', [(i, i ^ mask) for i in range(lax.axis_size('c...  7.86 us
    all_to_all x4, waiting for transfers between devices, swap_groups(): return lax.all_to_all(value, 'ctx', 0, 0, axis_index_groups=groups)  5.83 us
    pallas_call x1, Pallas kernels, shards(): pl.pallas_call(bias_kernel, out_shape=(shape((HEADS, T, KEYS), f32), shap...  4.77 us
    pallas_call x1, Pallas kernels, shards(): pl.pallas_call(main_kernel, out_shape=(wide_tokens, wide_tokens, shape((T...  4.11 us
    pallas_call x1, Pallas kernels, shards(): pl.pallas_call(weight_kernel, out_shape=(shape((HEADS, D), f32), wide_tok...  2.84 us
  transfers between devices with their start and end apart: 13, of which 7 were waited for; matrix products, arithmetic and copies ran while one was open for 0% of the time, Pallas kernels for 9%

profile of v5, /device:TPU:1, one launch (start us, length us, event | category | flops | bytes accessed | tf_op | source)
XLA Modules:
  0.0 103.2 jit_solution(11991868055523569100)
XLA Ops:
  1.3 1.8 %leaf.1 = (f32[32,512]{1,0:T(8,128)S(1)}, f32[16,8,640]{2,1,0:T(8,128)}) custom-call(s32[1]{0:T(128)S(6)} %copy.15.len_ref, bf16[128,256]{1,0:T(8,128)(2,1)} %k_hbm.3, bf16[128,256]{1,0:T(8,128)(2,1)} %v_hbm.3), custom_call_target="tpu_custom_call" | custom-call | tf_op jit(solution)/shard_map/leaf/pallas_call | solution.py:413
  3.1 10.7 %all-to-all-start = ((f32[16,8,640]{2,1,0:T(8,128)}), f32[16,8,640]{2,1,0:T(8,128)S(1)}, u32[]{:S(2)}, u32[]{:S(2)}) async-start(f32[16,8,640]{2,1,0:T(8,128)} %get-tuple-element.35), calls=%async_computation | async-start | bytes 655360 | tf_op jit(solution)/shard_map/all_to_all | solution.py:391
  13.8 2.2 %collective-permute-start = (f32[32,512]{1,0:T(8,128)S(1)}, f32[32,512]{1,0:T(8,128)S(1)}, u32[]{:S(2)}, u32[]{:S(2)}) collective-permute-start(f32[32,512]{1,0:T(8,128)S(1)} %get-tuple-element.32.after_ref), channel_id=1, source_target_pairs={{0,2},{2,0},{4,6},{6,4},{8,10},{10,8},{12,14},{14,12},{16,18},{18,... | collective-permute-start | bytes 196616 | tf_op jit(solution)/shard_map/ppermute | solution.py:43
  16.0 0.1 pad_add_fusion.place_ref
  16.1 4.8 %bias.1 = (f32[8,128,384]{2,1,0:T(8,128)S(1)}, f32[128,384]{1,0:T(8,128)S(1)}, f32[2,256,128]{2,1,0:T(8,128)S(1)}, f32[2,8,128]{2,1,0:T(8,128)S(1)}) custom-call(s32[2]{0:T(128)S(1)} %pad_add_fusion.place_ref, f32[1,32]{1,0:T(1,128)} %bitcast.15, f32[1,32]{1,0:T(1,128)} %bitcast.16, f32[16,32]{1,0:T(8,128)} %bitcast.13, ...), custom_call_target="tpu_custom_call" | custom-call | flops 600000000 | bytes 2000000 | tf_op jit(solution)/shard_map/bias/pallas_call | solution.py:426
  20.8 0.0 copy-start
  20.9 0.0 collective-permute-done.got0_ref
  20.9 0.1 reshape.37
  21.0 0.2 reduce_sum.18.after_merge_ref
  21.1 0.0 all-to-all-done
  21.2 1.0 middle.1
  22.1 15.0 %all-to-all-start.1 = ((f32[16,8,640]{2,1,0:T(8,128)}), f32[16,8,640]{2,1,0:T(8,128)S(1)}, u32[]{:S(2)}, u32[]{:S(2)}) async-start(f32[16,8,640]{2,1,0:T(8,128)} %get-tuple-element.37), calls=%async_computation.1 | async-start | bytes 655360 | tf_op jit(solution)/shard_map/all_to_all | solution.py:391
  37.1 4.3 %collective-permute-start.2 = (f32[32,640]{1,0:T(8,128)S(1)}, f32[32,640]{1,0:T(8,128)S(1)}, u32[]{:S(2)}, u32[]{:S(2)}) collective-permute-start(f32[32,640]{1,0:T(8,128)S(1)} %get-tuple-element.36.own_ref), channel_id=1, source_target_pairs={{0,48},{2,50},{4,52},{6,54},{8,56},{10,58},{12,60},{14,62},{16,32}... | collective-permute-start | bytes 245768 | tf_op jit(solution)/shard_map/ppermute | solution.py:43
  41.5 2.1 %collective-permute-start.1 = (f32[32,640]{1,0:T(8,128)S(1)}, f32[32,640]{1,0:T(8,128)S(1)}, u32[]{:S(2)}, u32[]{:S(2)}) collective-permute-start(f32[32,640]{1,0:T(8,128)S(1)} %pad.4), channel_id=1, source_target_pairs={{0,4},{2,6},{4,0},{6,2},{8,12},{10,14},{12,8},{14,10},{16,20},{18,... | collective-permute-start | bytes 245768 | tf_op jit(solution)/shard_map/ppermute | solution.py:43
  43.5 1.2 %collective-permute-done.2.got_ref.got4_ref = f32[32,640]{1,0:T(8,128)S(1)} collective-permute-done((f32[32,640]{1,0:T(8,128)S(1)}, f32[32,640]{1,0:T(8,128)S(1)}, u32[]{:S(2)}, u32[]{:S(2)}) %collective-permute-start.2) | collective-permute-done | bytes 81952 | tf_op jit(solution)/shard_map/ppermute | solution.py:43
  44.7 0.7 merge.1
  45.5 2.6 %collective-permute-start.3 = (f32[32,640]{1,0:T(8,128)S(1)}, f32[32,640]{1,0:T(8,128)S(1)}, u32[]{:S(2)}, u32[]{:S(2)}) collective-permute-start(f32[32,640]{1,0:T(8,128)S(1)} %merge.1), channel_id=1, source_target_pairs={{0,64},{2,66},{4,68},{6,70},{8,72},{10,74},{12,76},{14,78},{16,80}... | collective-permute-start | bytes 245768 | tf_op jit(solution)/shard_map/ppermute | solution.py:43
  48.0 0.7 collective-permute-done.1.got1_ref
  48.7 1.9 %collective-permute-done.3.got5_ref = f32[32,640]{1,0:T(8,128)S(1)} collective-permute-done((f32[32,640]{1,0:T(8,128)S(1)}, f32[32,640]{1,0:T(8,128)S(1)}, u32[]{:S(2)}, u32[]{:S(2)}) %collective-permute-start.3) | collective-permute-done | bytes 81952 | tf_op jit(solution)/shard_map/ppermute | solution.py:43
  50.6 0.0 all-to-all-done.1
  50.6 0.0 copy-done
  50.6 0.0 copy-start.1
  50.7 4.1 %attention.1 = (bf16[128,1024]{1,0:T(8,128)(2,1)S(1)}, bf16[128,1024]{1,0:T(8,128)(2,1)S(1)}, f32[128,512]{1,0:T(8,128)S(1)}, f32[256,512]{1,0:T(8,128)S(1)}, f32[8,128,384]{2,1,0:T(8,128)S(1)}) custom-call(s32[2]{0:T(128)S(1)} %pad_add_fusion.place_ref, s32[1]{0:T(128)S(6)} %copy.15.len_ref, bf16[128,1024]{1,0:T(8,128)(2,1)} %q_hbm.1, ...), custom_call_target="tpu_custom_call" | custom-call | tf_op jit(solution)/shard_map/attention/pallas_call | solution.py:467
  54.8 2.6 %collective-permute-start.4 = (f32[32,512]{1,0:T(8,128)S(1)}, f32[32,512]{1,0:T(8,128)S(1)}, u32[]{:S(2)}, u32[]{:S(2)}) collective-permute-start(f32[32,512]{1,0:T(8,128)S(1)} %get-tuple-element.58), channel_id=1, source_target_pairs={{0,64},{2,66},{4,68},{6,70},{8,72},{10,74},{12,76},{14,78},{16,80}... | collective-permute-start | bytes 196616 | tf_op jit(solution)/shard_map/ppermute | solution.py:43
  57.4 0.0 copy-done.1
  57.4 2.8 %weights.1 = (f32[8,128]{1,0:T(8,128)S(1)}, bf16[128,1024]{1,0:T(8,128)(2,1)}, bf16[128,1024]{1,0:T(8,128)(2,1)}) custom-call(f32[2,256,128]{2,1,0:T(8,128)S(1)} %copy-done.1, f32[2,8,128]{2,1,0:T(8,128)S(1)} %get-tuple-element.34.after_bias_ref.slot_ref, f32[8,128,384]{2,1,0:T(8,128)S(1)} %get-tuple-element.39.ds_ref, ...), custom_call_target="tpu_custom_call" | custom-call | flops 900000000 | bytes 2000000 | tf_op jit(solution)/shard_map/weights/pallas_call | solution.py:485
  60.2 0.0 collective-permute-done.4.came5_ref
  60.2 1.5 %away.1 = (f32[16,8,640]{2,1,0:T(8,128)}, f32[32,512]{1,0:T(8,128)S(1)}) custom-call(s32[2]{0:T(128)S(1)} %pad_add_fusion.place_ref, f32[8,128]{1,0:T(8,128)S(1)} %get-tuple-element.45.w_ref, f32[256,512]{1,0:T(8,128)S(1)} %get-tuple-element.46.coarse_ref, f32[32,512]{1,0:T(8,128)S(1)} %collective-permute-done.4.came5_ref), custom_call_target="tpu_custom_call" | custom-call | tf_op jit(solution)/shard_map/away/pallas_call | solution.py:495
  61.8 7.2 %all-to-all-start.2 = ((f32[16,8,640]{2,1,0:T(8,128)}), f32[16,8,640]{2,1,0:T(8,128)S(1)}, u32[]{:S(2)}, u32[]{:S(2)}) async-start(f32[16,8,640]{2,1,0:T(8,128)} %get-tuple-element.47), calls=%async_computation.2 | async-start | bytes 655360 | tf_op jit(solution)/shard_map/all_to_all | solution.py:391
  69.0 2.0 %collective-permute-start.6 = (f32[32,512]{1,0:T(8,128)S(1)}, f32[32,512]{1,0:T(8,128)S(1)}, u32[]{:S(2)}, u32[]{:S(2)}) collective-permute-start(f32[32,512]{1,0:T(8,128)S(1)} %get-tuple-element.57), channel_id=1, source_target_pairs={{0,4},{2,6},{4,0},{6,2},{8,12},{10,14},{12,8},{14,10},{16,20},{18,... | collective-permute-start | bytes 196616 | tf_op jit(solution)/shard_map/ppermute | solution.py:43
  71.0 2.2 %collective-permute-start.5 = (f32[32,512]{1,0:T(8,128)S(1)}, f32[32,512]{1,0:T(8,128)S(1)}, u32[]{:S(2)}, u32[]{:S(2)}) collective-permute-start(f32[32,512]{1,0:T(8,128)S(1)} %get-tuple-element.48), channel_id=1, source_target_pairs={{0,48},{2,50},{4,52},{6,54},{8,56},{10,58},{12,60},{14,62},{16,32}... | collective-permute-start | bytes 196616 | tf_op jit(solution)/shard_map/ppermute | solution.py:43
  73.2 2.0 %collective-permute-done.6.came1_ref = f32[32,512]{1,0:T(8,128)S(1)} collective-permute-done((f32[32,512]{1,0:T(8,128)S(1)}, f32[32,512]{1,0:T(8,128)S(1)}, u32[]{:S(2)}, u32[]{:S(2)}) %collective-permute-start.6) | collective-permute-done | bytes 65568 | tf_op jit(solution)/shard_map/ppermute | solution.py:43
  75.2 2.1 %collective-permute-done.5.came4_ref = f32[32,512]{1,0:T(8,128)S(1)} collective-permute-done((f32[32,512]{1,0:T(8,128)S(1)}, f32[32,512]{1,0:T(8,128)S(1)}, u32[]{:S(2)}, u32[]{:S(2)}) %collective-permute-start.5) | collective-permute-done | bytes 65568 | tf_op jit(solution)/shard_map/ppermute | solution.py:43
  77.2 0.4 all-to-all-done.2.away_ref
  77.7 1.6 %return.1 = (f32[16,8,640]{2,1,0:T(8,128)}, f32[32,512]{1,0:T(8,128)S(1)}) custom-call(s32[2]{0:T(128)S(1)} %pad_add_fusion.place_ref, f32[16,8,640]{2,1,0:T(8,128)S(1)} %all-to-all-done.2.away_ref, f32[32,512]{1,0:T(8,128)S(1)} %collective-permute-done.4.came5_ref, f32[32,512]{1,0:T(8,128)S(1)} %collective-permute-done.5.came4_ref, ...), custom_call_target="tpu_custom_call" | custom-call | tf_op jit(solution)/shard_map/return/pallas_call | solution.py:506
  79.3 6.2 %all-to-all-start.3 = ((f32[16,8,640]{2,1,0:T(8,128)}), f32[16,8,640]{2,1,0:T(8,128)S(1)}, u32[]{:S(2)}, u32[]{:S(2)}) async-start(f32[16,8,640]{2,1,0:T(8,128)} %get-tuple-element.49), calls=%async_computation.3 | async-start | bytes 655360 | tf_op jit(solution)/shard_map/all_to_all | solution.py:391
  85.5 2.2 %collective-permute-start.7 = (f32[32,512]{1,0:T(8,128)S(1)}, f32[32,512]{1,0:T(8,128)S(1)}, u32[]{:S(2)}, u32[]{:S(2)}) collective-permute-start(f32[32,512]{1,0:T(8,128)S(1)} %get-tuple-element.50), channel_id=1, source_target_pairs={{0,2},{2,0},{4,6},{6,4},{8,10},{10,8},{12,14},{14,12},{16,18},{18,... | collective-permute-start | bytes 196616 | tf_op jit(solution)/shard_map/ppermute | solution.py:43
  87.7 5.4 %all-to-all-done.3.near_ref = f32[16,8,640]{2,1,0:T(8,128)S(1)} async-done(((f32[16,8,640]{2,1,0:T(8,128)}), f32[16,8,640]{2,1,0:T(8,128)S(1)}, u32[]{:S(2)}, u32[]{:S(2)}) %all-to-all-start.3) | async-done | bytes 327712 | tf_op jit(solution)/shard_map/all_to_all | solution.py:391
  93.1 7.9 %collective-permute-start.8 = (f32[8,128]{1,0:T(8,128)S(1)}, f32[8,128]{1,0:T(8,128)S(1)}, u32[]{:S(2)}, u32[]{:S(2)}) collective-permute-start(f32[8,128]{1,0:T(8,128)S(1)} %fusion.mine_ref), channel_id=1, source_target_pairs={{0,1},{1,0},{2,3},{3,2},{4,5},{5,4},{6,7},{7,6},{8,9},{9,8},{10,11... | collective-permute-start | bytes 12296 | tf_op jit(solution)/shard_map/ppermute | solution.py:518
  101.0 0.0 collective-permute-done.7.came0_ref
  101.0 1.5 %final.1 = (bf16[128,256]{1,0:T(8,128)(2,1)}, bf16[128,256]{1,0:T(8,128)(2,1)}) custom-call(s32[2]{0:T(128)S(1)} %pad_add_fusion.place_ref, s32[1]{0:T(128)S(6)} %copy.15.len_ref, f32[16,8,640]{2,1,0:T(8,128)S(1)} %all-to-all-done.3.near_ref, f32[32,512]{1,0:T(8,128)S(1)} %collective-permute-done.6.came1_ref, ...), custom_call_target="tpu_custom_call" | custom-call | tf_op jit(solution)/shard_map/final/pallas_call | solution.py:519
  102.5 0.0 collective-permute-done.8.got_ref
  102.5 0.7 outputs.1
  (5 shorter events, 0.1 us)
Async XLA Ops:
  3.1 18.1 %all-to-all-start = ((f32[16,8,640]{2,1,0:T(8,128)}), f32[16,8,640]{2,1,0:T(8,128)S(1)}, u32[]{:S(2)}, u32[]{:S(2)}) async-start(f32[16,8,640]{2,1,0:T(8,128)} %get-tuple-element.35), calls=%async_computation | async-start | bytes 655360 | tf_op jit(solution)/shard_map/all_to_all | solution.py:391
  13.8 7.1 %collective-permute-start = (f32[32,512]{1,0:T(8,128)S(1)}, f32[32,512]{1,0:T(8,128)S(1)}, u32[]{:S(2)}, u32[]{:S(2)}) collective-permute-start(f32[32,512]{1,0:T(8,128)S(1)} %get-tuple-element.32.after_ref), channel_id=1, source_target_pairs={{0,2},{2,0},{4,6},{6,4},{8,10},{10,8},{12,14},{14,12},{16,18},{18,... | collective-permute-start | bytes 196616 | tf_op jit(solution)/shard_map/ppermute | solution.py:43
  20.8 29.8 %copy-start = (f32[2,256,128]{2,1,0:T(8,128)}, f32[2,256,128]{2,1,0:T(8,128)S(1)}, u32[]{:S(2)}) copy-start(f32[2,256,128]{2,1,0:T(8,128)S(1)} %get-tuple-element.33.line_ref) | copy-start | bytes 786436
  22.1 28.5 %all-to-all-start.1 = ((f32[16,8,640]{2,1,0:T(8,128)}), f32[16,8,640]{2,1,0:T(8,128)S(1)}, u32[]{:S(2)}, u32[]{:S(2)}) async-start(f32[16,8,640]{2,1,0:T(8,128)} %get-tuple-element.37), calls=%async_computation.1 | async-start | bytes 655360 | tf_op jit(solution)/shard_map/all_to_all | solution.py:391
  37.1 7.6 %collective-permute-start.2 = (f32[32,640]{1,0:T(8,128)S(1)}, f32[32,640]{1,0:T(8,128)S(1)}, u32[]{:S(2)}, u32[]{:S(2)}) collective-permute-start(f32[32,640]{1,0:T(8,128)S(1)} %get-tuple-element.36.own_ref), channel_id=1, source_target_pairs={{0,48},{2,50},{4,52},{6,54},{8,56},{10,58},{12,60},{14,62},{16,32}... | collective-permute-start | bytes 245768 | tf_op jit(solution)/shard_map/ppermute | solution.py:43
  41.5 7.2 %collective-permute-start.1 = (f32[32,640]{1,0:T(8,128)S(1)}, f32[32,640]{1,0:T(8,128)S(1)}, u32[]{:S(2)}, u32[]{:S(2)}) collective-permute-start(f32[32,640]{1,0:T(8,128)S(1)} %pad.4), channel_id=1, source_target_pairs={{0,4},{2,6},{4,0},{6,2},{8,12},{10,14},{12,8},{14,10},{16,20},{18,... | collective-permute-start | bytes 245768 | tf_op jit(solution)/shard_map/ppermute | solution.py:43
  45.5 5.2 %collective-permute-start.3 = (f32[32,640]{1,0:T(8,128)S(1)}, f32[32,640]{1,0:T(8,128)S(1)}, u32[]{:S(2)}, u32[]{:S(2)}) collective-permute-start(f32[32,640]{1,0:T(8,128)S(1)} %merge.1), channel_id=1, source_target_pairs={{0,64},{2,66},{4,68},{6,70},{8,72},{10,74},{12,76},{14,78},{16,80}... | collective-permute-start | bytes 245768 | tf_op jit(solution)/shard_map/ppermute | solution.py:43
  50.6 6.7 %copy-start.1 = (f32[2,256,128]{2,1,0:T(8,128)S(1)}, f32[2,256,128]{2,1,0:T(8,128)}, u32[]{:S(2)}) copy-start(f32[2,256,128]{2,1,0:T(8,128)} %copy-done) | copy-start | bytes 786436
  54.8 5.4 %collective-permute-start.4 = (f32[32,512]{1,0:T(8,128)S(1)}, f32[32,512]{1,0:T(8,128)S(1)}, u32[]{:S(2)}, u32[]{:S(2)}) collective-permute-start(f32[32,512]{1,0:T(8,128)S(1)} %get-tuple-element.58), channel_id=1, source_target_pairs={{0,64},{2,66},{4,68},{6,70},{8,72},{10,74},{12,76},{14,78},{16,80}... | collective-permute-start | bytes 196616 | tf_op jit(solution)/shard_map/ppermute | solution.py:43
  61.8 15.9 %all-to-all-start.2 = ((f32[16,8,640]{2,1,0:T(8,128)}), f32[16,8,640]{2,1,0:T(8,128)S(1)}, u32[]{:S(2)}, u32[]{:S(2)}) async-start(f32[16,8,640]{2,1,0:T(8,128)} %get-tuple-element.47), calls=%async_computation.2 | async-start | bytes 655360 | tf_op jit(solution)/shard_map/all_to_all | solution.py:391
  69.0 6.2 %collective-permute-start.6 = (f32[32,512]{1,0:T(8,128)S(1)}, f32[32,512]{1,0:T(8,128)S(1)}, u32[]{:S(2)}, u32[]{:S(2)}) collective-permute-start(f32[32,512]{1,0:T(8,128)S(1)} %get-tuple-element.57), channel_id=1, source_target_pairs={{0,4},{2,6},{4,0},{6,2},{8,12},{10,14},{12,8},{14,10},{16,20},{18,... | collective-permute-start | bytes 196616 | tf_op jit(solution)/shard_map/ppermute | solution.py:43
  71.0 6.3 %collective-permute-start.5 = (f32[32,512]{1,0:T(8,128)S(1)}, f32[32,512]{1,0:T(8,128)S(1)}, u32[]{:S(2)}, u32[]{:S(2)}) collective-permute-start(f32[32,512]{1,0:T(8,128)S(1)} %get-tuple-element.48), channel_id=1, source_target_pairs={{0,48},{2,50},{4,52},{6,54},{8,56},{10,58},{12,60},{14,62},{16,32}... | collective-permute-start | bytes 196616 | tf_op jit(solution)/shard_map/ppermute | solution.py:43
  79.3 13.8 %all-to-all-start.3 = ((f32[16,8,640]{2,1,0:T(8,128)}), f32[16,8,640]{2,1,0:T(8,128)S(1)}, u32[]{:S(2)}, u32[]{:S(2)}) async-start(f32[16,8,640]{2,1,0:T(8,128)} %get-tuple-element.49), calls=%async_computation.3 | async-start | bytes 655360 | tf_op jit(solution)/shard_map/all_to_all | solution.py:391
  85.5 15.5 %collective-permute-start.7 = (f32[32,512]{1,0:T(8,128)S(1)}, f32[32,512]{1,0:T(8,128)S(1)}, u32[]{:S(2)}, u32[]{:S(2)}) collective-permute-start(f32[32,512]{1,0:T(8,128)S(1)} %get-tuple-element.50), channel_id=1, source_target_pairs={{0,2},{2,0},{4,6},{6,4},{8,10},{10,8},{12,14},{14,12},{16,18},{18,... | collective-permute-start | bytes 196616 | tf_op jit(solution)/shard_map/ppermute | solution.py:43
  93.1 9.4 %collective-permute-start.8 = (f32[8,128]{1,0:T(8,128)S(1)}, f32[8,128]{1,0:T(8,128)S(1)}, u32[]{:S(2)}, u32[]{:S(2)}) collective-permute-start(f32[8,128]{1,0:T(8,128)S(1)} %fusion.mine_ref), channel_id=1, source_target_pairs={{0,1},{1,0},{2,3},{3,2},{4,5},{5,4},{6,7},{7,6},{8,9},{9,8},{10,11... | collective-permute-start | bytes 12296 | tf_op jit(solution)/shard_map/ppermute | solution.py:518

commit v6 on v5

--- a/solution.py
+++ b/solution.py
@@ -21,7 +21,7 @@
 UNROLL = 2
 CHUNK = 8
 SIDE = 16
-FIRST = {"low": 12, "high": 12, "away": 3, "near": 2}
+FIRST = {"low": 12, "high": 14, "away": 3, "near": 2}
 WIDTH = KV * D
 LEVEL_TOKENS = float(T * 2**LEVELS)
 SCALE = D ** (-0.5)
@@ -143,41 +143,38 @@
 
 
 def pooled(rows, by):
-    shape = (rows.shape[0] // by, rows.shape[0])
-    row = lax.broadcasted_iota(jnp.int32, shape, 0)
-    col = lax.broadcasted_iota(jnp.int32, shape, 1)
-    return picked(jnp.where(col // by == row, 1.0, 0.0).astype(jnp.bfloat16), rows)
+    row = lax.broadcasted_iota(jnp.int32, (rows.shape[0] // by, 1), 0)
+    return picked(twice(rows.shape[0] // by, rows.shape[0]) // by == row, rows)
 
 
 def middle_kernel(low_ref, after_bias_ref, after_merge_ref, own_ref, wide_ref):
-    row = lax.broadcasted_iota(jnp.int32, (COARSE + CHUNK, SIDE * CHUNK), 0)
-    col = lax.broadcasted_iota(jnp.int32, (COARSE + CHUNK, SIDE * CHUNK), 1)
+    row = lax.broadcasted_iota(jnp.int32, (COARSE + CHUNK, 1), 0)
+    col = twice(COARSE + CHUNK, SIDE * CHUNK)
     member = (col >> 3) ^ FIRST["low"]
     run = jnp.where(row < COARSE, (member << 1) + ((col & 7) >> 2), (member >> 1) + COARSE)
-    rows = picked(jnp.where(run == row, 1.0, 0.0).astype(jnp.bfloat16), low_ref[...])
+    rows = picked(run == row, low_ref[...])
     own_ref[...] = rows[:COARSE]
     for n in range(SIDE):
         wide_ref[n] = rows[COARSE:]
 
 
-def main_kernel(
-    place_ref, len_ref, q_hbm, k_hbm, v_hbm, g_hbm, got0_ref, got1_ref, low_ref, got4_ref, got5_ref, high_ref, bias_ref,
-    out_ref, gq_ref, own_ref, coarse_ref, ds_ref, q_ref, k_ref, v_ref, g_ref, sib_ref, sems,
+def gather_kernel(
+    place_ref, len_ref, q_hbm, k_hbm, v_hbm, g_hbm, got0_ref, got1_ref, low_ref, got4_ref, high_ref, after_ref,
+    q_ref, g_ref, keys_ref, values_ref, count_ref, k_ref, v_ref, sib_ref, sems,
 ):
     copies = fetch([(k_hbm, k_ref), (q_hbm, q_ref), (v_hbm, v_ref), (g_hbm, g_ref)], sems)
-    length = len_ref[0]
     ctx = place_ref[0]
-    for level, ref in ((0, got0_ref), (1, got1_ref), (4, got4_ref), (5, got5_ref)):
+    for level, ref in ((0, got0_ref), (1, got1_ref), (4, got4_ref), (5, got4_ref)):
         sib_ref[level * COARSE : (level + 1) * COARSE, : ref.shape[1]] = ref[...]
-    for level, ref, first in ((2, low_ref, FIRST["low"] >> 2), (6, high_ref, FIRST["high"] >> 2)):
+    row = lax.broadcasted_iota(jnp.int32, (2 * COARSE, 1), 0)
+    col = twice(2 * COARSE, SIDE * CHUNK)
+    for level, ref, first in ((2, low_ref, FIRST["low"]), (6, high_ref, FIRST["high"])):
         quarter = ((ctx >> level) & 3) ^ 1
-        start = pl.multiple_of((quarter ^ first) * COARSE, COARSE)
-        sib_ref[level * COARSE : (level + 1) * COARSE, :] = ref[pl.ds(start, COARSE), :]
-        for n in range(2):
-            quarter = (((ctx >> level + 1) & 1) ^ 1) * 2 + n
-            start = pl.multiple_of((quarter ^ first) * COARSE, COARSE)
-            place = (level + 1) * COARSE + n * COARSE // 2
-            sib_ref[place : place + COARSE // 2, :] = pooled(ref[pl.ds(start, COARSE), :], 2)
+        half = ((ctx >> level + 1) & 1) ^ 1
+        place = (((col >> 3) ^ first) << 3) + (col & 7)
+        want = jnp.where(row < COARSE, quarter * COARSE + row, (half - 1) * COARSE + row)
+        rows = picked(jnp.where(row < COARSE, place, place >> 1) == want, ref[...])
+        sib_ref[level * COARSE : (level + 2) * COARSE, :] = rows
     group = (((ctx >> 1) & 7) ^ 1) * 2
     blocks = ((0, COARSE, (ctx & 15) ^ 1), (COARSE, COARSE // 2, group), (COARSE * 3 // 2, COARSE // 2, group + 1))
     for first, rows, block in blocks:
@@ -187,26 +184,47 @@
         here = jnp.sum(block, axis=0, keepdims=True) - before.astype(jnp.float32)
         sib_ref[first : first + rows, 2 * WIDTH :] = jnp.clip(here, 0.0, float(run))
     count = sib_ref[:, 2 * WIDTH :]
+    count_ref[...] = count
+    inverse = 1.0 / jnp.maximum(count, 1.0)
+    for n in range(2 * KV):
+        cols = slice(n * D, (n + 1) * D)
+        ref = keys_ref if n < KV else values_ref
+        ref[T:, n % KV * D : (n % KV + 1) * D] = (sib_ref[:, cols] * inverse).astype(jnp.bfloat16)
+    for copy in copies:
+        copy.wait()
+    keys_ref[:T, :] = k_ref[...]
+    values_ref[:T, :] = v_ref[...]
+    row_live = lax.broadcasted_iota(jnp.int32, (T, 1), 0) < len_ref[0]
+    g_ref[...] = jnp.where(row_live, g_ref[...], jnp.zeros_like(g_ref))
+
+
+def with_level_5(rows, level, first):
+    return jnp.concatenate([rows[: first + 5 * COARSE], level, rows[first + 6 * COARSE :]], axis=0)
+
+
+def main_kernel(
+    len_ref, q_ref, g_ref, keys_ref, values_ref, count_ref, got5_ref, bias_ref,
+    out_ref, gq_ref, own_ref, coarse_ref, ds_ref,
+):
+    length = len_ref[0]
+    count = with_level_5(count_ref[...], got5_ref[:, 2 * WIDTH :], 0)
     inverse = 1.0 / jnp.maximum(count, 1.0)
     count_t = jnp.concatenate([count[:T].T[:1], count[T:].T[:1]], axis=1)
     token_live = lax.broadcasted_iota(jnp.int32, (1, T), 1) < length
     live = jnp.concatenate([token_live.astype(jnp.float32), count_t], axis=1) > 0.0
     row_live = lax.broadcasted_iota(jnp.int32, (T, 1), 0) < length
-    for copy in copies:
-        copy.wait()
+    inverse_5 = inverse[5 * COARSE : 6 * COARSE]
     for j in range(KV):
         cols = slice(j * D, (j + 1) * D)
         vcols = slice((KV + j) * D, (KV + j + 1) * D)
-        keys = jnp.concatenate([k_ref[:, cols], (sib_ref[:, cols] * inverse).astype(jnp.bfloat16)], axis=0)
-        values = jnp.concatenate([v_ref[:, cols], (sib_ref[:, vcols] * inverse).astype(jnp.bfloat16)], axis=0)
-        heads = range(j * GROUP, (j + 1) * GROUP)
+        keys = with_level_5(keys_ref[:, cols], (got5_ref[:, cols] * inverse_5).astype(jnp.bfloat16), T)
+        values = with_level_5(values_ref[:, cols], (got5_ref[:, vcols] * inverse_5).astype(jnp.bfloat16), T)
         key_grads = jnp.zeros((KEYS, D), jnp.float32)
         value_grads = jnp.zeros((KEYS, D), jnp.float32)
         for first in range(j * GROUP, (j + 1) * GROUP, BATCH):
             heads = range(first, first + BATCH)
             query = jnp.concatenate([q_ref[:, h * D : (h + 1) * D] for h in heads], axis=0)
-            grad = [g_ref[:, h * D : (h + 1) * D] for h in heads]
-            grad = jnp.concatenate([jnp.where(row_live, part, jnp.zeros_like(part)) for part in grad], axis=0)
+            grad = jnp.concatenate([g_ref[:, h * D : (h + 1) * D] for h in heads], axis=0)
             scores = dot(query, keys, NT) * SCALE + bias_ref[first : first + BATCH].reshape(BATCH * T, KEYS)
             scores = jnp.where(live, scores, -jnp.inf)
             weights = jnp.exp(scores - jnp.max(scores, axis=1, keepdims=True))
@@ -237,19 +255,23 @@
     copies = fetch([(out_ref, out_hbm), (gq_ref, gq_hbm)], sems)
     acc_ref[...] = jnp.zeros_like(acc_ref)
 
-    def body(i, carry):
-        rows = pl.ds(pl.multiple_of(i * SUB, SUB), SUB)
+    def operands(rows):
         phase = phase_ref[rows, :]
         parts = [ds_ref[h, rows, :] for h in range(HEADS)]
         parts = jnp.concatenate(parts + [p * phase for p in parts], axis=0)
         high = parts.astype(jnp.bfloat16)
         low = (parts - high.astype(jnp.float32)).astype(jnp.bfloat16)
-        both = jnp.concatenate([high, low], axis=0)
         active = jnp.where(by_units(line_ref, phase) > 0.0, 1.0, 0.0).astype(jnp.bfloat16)
+        return jnp.concatenate([high, low], axis=0), active
+
+    def body(i, carry):
+        first = pl.multiple_of(i * 2 * SUB, 2 * SUB)
+        groups = [operands(pl.ds(first + n * SUB, SUB)) for n in range(2)]
+        both, active = (jnp.concatenate(side, axis=1) for side in zip(*groups))
         acc_ref[...] += dot(both, active, NT)
         return carry
 
-    lax.fori_loop(0, T // SUB, body, 0, unroll=UNROLL)
+    lax.fori_loop(0, T // SUB // 2, body, 0, unroll=UNROLL)
     acc = acc_ref[...]
     rows = 2 * HEADS * SUB
     acc = acc[:rows] + acc[rows:]
@@ -269,25 +291,26 @@
     sizes = [value.shape[0] for value, _ in parts]
     depth = -(-sum(sizes) // 16) * 16
     row = lax.broadcasted_iota(jnp.int32, (rows, 1), 0)
-    col = lax.broadcasted_iota(jnp.int32, (rows, depth), 1)
+    col = twice(rows, depth)
     pick, first = col < 0, 0
     for size, (_, name) in zip(sizes, parts):
         pick = pick | (col == name(row, first))
         first += size
-    pick = jnp.where(pick, 1.0, 0.0).astype(jnp.bfloat16)
     value = [value for value, _ in parts]
     if first < depth:
         value.append(jnp.zeros((depth - first, value[0].shape[1]), jnp.float32))
     return picked(pick, jnp.concatenate(value, axis=0))
 
 
+def twice(rows, depth):
+    col = lax.broadcasted_iota(jnp.int32, (rows, 2 * depth), 1)
+    return jnp.where(col < depth, col, col - depth)
+
+
 def picked(pick, value):
-    total = 0.0
-    for _ in range(3):
-        part = value.astype(jnp.bfloat16)
-        total = total + dot(pick, part)
-        value = value - part.astype(jnp.float32)
-    return total
+    high = value.astype(jnp.bfloat16)
+    low = (value - high.astype(jnp.float32)).astype(jnp.bfloat16)
+    return dot(jnp.where(pick, 1.0, 0.0).astype(jnp.bfloat16), jnp.concatenate([high, low], axis=0))
 
 
 def level_parts(ctx, level, coarse_ref):
@@ -339,22 +362,29 @@
     return sum(ref[n] + ref[n + SIDE // 2] for n in range(SIDE // 2))
 
 
-def return_kernel(place_ref, away_ref, came5_ref, came4_ref, came1_ref, coarse_ref, near_ref, send_ref):
+def base_kernel(place_ref, came5_ref, came1_ref, coarse_ref, base_ref, send_ref):
+    ctx = place_ref[0]
+    parts = level_parts(ctx, 2, coarse_ref) + [(came5_ref[...], half_of(ctx, 4, 3))]
+    base_ref[...] = chosen(SIDE * CHUNK, parts)
+    send_ref[...] = sibling_rows(ctx, 0, coarse_ref, came1_ref)
+
+
+def return_kernel(place_ref, away_ref, came4_ref, base_ref, near_ref):
     ctx = place_ref[0]
     away = summed(away_ref)
-    parts = level_parts(ctx, 2, coarse_ref)
-    parts += [(came5_ref[...], half_of(ctx, 4, 3)), (came4_ref[...], every(2))]
-    parts += [(away[:, : 2 * WIDTH], every(4))]
-    fill(near_ref, FIRST["near"] ^ (((ctx >> 4) & 1) * 8), chosen(SIDE * CHUNK, parts), away[:, 2 * WIDTH :])
-    send_ref[...] = sibling_rows(ctx, 0, coarse_ref, came1_ref)
-
-
-def final_kernel(place_ref, len_ref, near_ref, came1_ref, came0_ref, own_ref, gk_ref, gv_ref):
-    ctx = place_ref[0]
+    rows = base_ref[...] + chosen(SIDE * CHUNK, [(came4_ref[...], every(2)), (away[:, : 2 * WIDTH], every(4))])
+    fill(near_ref, FIRST["near"] ^ (((ctx >> 4) & 1) * 8), rows, away[:, 2 * WIDTH :])
+
+
+def own_kernel(place_ref, own_ref, came1_ref, came0_ref, out_ref):
+    parts = [(came1_ref[...], half_of(place_ref[0], 0, 3)), (came0_ref[...], every(2))]
+    out_ref[...] = own_ref[...] + chosen(T, parts)
+
+
+def final_kernel(len_ref, near_ref, own_ref, gk_ref, gv_ref):
     near = sum(near_ref[n, :, : 2 * WIDTH] for n in range(SIDE))
-    parts = [(came1_ref[...], half_of(ctx, 0, 3)), (came0_ref[...], every(2)), (near, every(4))]
     live = lax.broadcasted_iota(jnp.int32, (T, 1), 0) < len_ref[0]
-    grad = jnp.where(live, own_ref[...] + chosen(T, parts), 0.0)
+    grad = jnp.where(live, own_ref[...] + chosen(T, [(near, every(4))]), 0.0)
     gk_ref[...] = grad[:, :WIDTH].astype(jnp.bfloat16)
     gv_ref[...] = grad[:, WIDTH:].astype(jnp.bfloat16)
 
@@ -369,12 +399,11 @@
 
 
 def merge_kernel(place_ref, own_ref, got_ref, out_ref):
-    shape = (COARSE, 2 * COARSE)
-    row = lax.broadcasted_iota(jnp.int32, shape, 0)
-    col = lax.broadcasted_iota(jnp.int32, shape, 1)
+    row = lax.broadcasted_iota(jnp.int32, (COARSE, 1), 0)
+    col = twice(COARSE, 2 * COARSE)
     upper = (place_ref[0] >> 4) & 1
-    pick = jnp.where((row & 15 == (col & 31) >> 1) & (row >> 4 == (col >> 5) ^ upper), 1.0, 0.0)
-    out_ref[...] = picked(pick.astype(jnp.bfloat16), jnp.concatenate([own_ref[...], got_ref[...]], axis=0))
+    pick = (row & 15 == (col & 31) >> 1) & (row >> 4 == (col >> 5) ^ upper)
+    out_ref[...] = picked(pick, jnp.concatenate([own_ref[...], got_ref[...]], axis=0))
 
 
 def merge(own, got, upper):
@@ -464,6 +493,18 @@
     )(place, own4, got4)
     got5 = exchange(own5, 5)
 
+    both = shape((KEYS, WIDTH), bf16)
+    gathered = pl.pallas_call(
+        gather_kernel,
+        out_shape=(wide_tokens, wide_tokens, both, both, shape((LEVELS * COARSE, D), f32)),
+        in_specs=[SMEM, SMEM] + [HBM] * 4 + [VMEM] * 5 + [ANY],
+        out_specs=(VMEM,) * 5,
+        scratch_shapes=[pltpu.VMEM((T, WIDTH), bf16)] * 2
+        + [pltpu.VMEM((LEVELS * COARSE, 2 * WIDTH + D), f32), dma((4,))],
+        compiler_params=SMALL,
+        cost_estimate=pl.CostEstimate(flops=300_000_000, bytes_accessed=2_000_000, transcendentals=0),
+        name="gather",
+    )(place, lengths, *map(in_hbm, (queries, keys, values, grad_out)), got0, got1, low, got4, high, own5)
     attended, grad_q, own_grad, coarse, dscores = pl.pallas_call(
         main_kernel,
         out_shape=(
@@ -473,13 +514,11 @@
             shape((LEVELS * COARSE, 2 * WIDTH), f32),
             shape((HEADS, T, KEYS), f32),
         ),
-        in_specs=[SMEM, SMEM] + [HBM] * 4 + [VMEM] * 7,
+        in_specs=[SMEM] + [VMEM] * 7,
         out_specs=(VMEM,) * 5,
-        scratch_shapes=[pltpu.VMEM((T, n), bf16) for n in (HEADS * D, WIDTH, WIDTH, HEADS * D)]
-        + [pltpu.VMEM((LEVELS * COARSE, 2 * WIDTH + D), f32), dma((4,))],
         compiler_params=SMALL,
         name="attention",
-    )(place, lengths, *map(in_hbm, (queries, keys, values, grad_out)), got0, got1, low, got4, got5, high, bias)
+    )(lengths, *gathered, got5, bias)
 
     came5 = exchange(coarse[5 * COARSE : 6 * COARSE], 5)
     w_part, attended, grad_q = pl.pallas_call(
@@ -503,27 +542,46 @@
     away = swap_groups(away, high_groups(FIRST["away"]))
     came4 = exchange(send4, 4)
     came1 = exchange(coarse[COARSE : 2 * COARSE], 1)
-    near, send0 = pl.pallas_call(
+    base, send0 = pl.pallas_call(
+        base_kernel,
+        out_shape=(shape((T, 2 * WIDTH), f32), rows),
+        in_specs=[SMEM] + [VMEM] * 3,
+        out_specs=(VMEM, VMEM),
+        compiler_params=SMALL,
+        cost_estimate=pl.CostEstimate(flops=300_000_000, bytes_accessed=1_000_000, transcendentals=0),
+        name="base",
+    )(place, came5, came1, coarse)
+    near = pl.pallas_call(
         return_kernel,
-        out_shape=(payload, rows),
-        in_specs=[SMEM] + [VMEM] * 5,
-        out_specs=(VMEM, VMEM),
+        out_shape=payload,
+        in_specs=[SMEM] + [VMEM] * 3,
+        out_specs=VMEM,
         compiler_params=SMALL,
         name="return",
-    )(place, away, came5, came4, came1, coarse)
+    )(place, away, came4, base)
     near = swap_groups(near, low_groups(FIRST["near"], 8))
     came0 = exchange(send0, 0)
+    own_grad = pl.pallas_call(
+        own_kernel,
+        out_shape=shape((T, 2 * WIDTH), f32),
+        in_specs=[SMEM] + [VMEM] * 3,
+        out_specs=VMEM,
+        compiler_params=SMALL,
+        cost_estimate=pl.CostEstimate(flops=300_000_000, bytes_accessed=1_000_000, transcendentals=0),
+        name="own",
+    )(place, own_grad, came1, came0)
+    near, own_grad = lax.optimization_barrier((near, own_grad))
     w_all = near[:, :, 2 * WIDTH :]
     w_all = (w_all[: SIDE // 2] + w_all[SIDE // 2 :]).sum(0)
     w_other = lax.ppermute(w_all, "mp", [(0, 1), (1, 0)])
     grad_k, grad_v = pl.pallas_call(
         final_kernel,
         out_shape=(tokens, tokens),
-        in_specs=[SMEM, SMEM] + [VMEM] * 4,
+        in_specs=[SMEM] + [VMEM] * 2,
         out_specs=(VMEM, VMEM),
         compiler_params=SMALL,
         name="final",
-    )(place, lengths, near, came1, came0, own_grad)
+    )(lengths, near, own_grad)
     grad_w1, grad_b1, grad_w2 = pl.pallas_call(
         outputs_kernel,
         out_shape=(shape((1, HIDDEN), f32), shape((1, HIDDEN), f32), shape((2 * HEADS, HIDDEN), f32)),

time: 104 us -> 102 us (0.981)
  waiting for transfers between devices: 13.7 us -> 10.3 us
  starting transfers between devices: 67.2 us -> 68.6 us
    all_to_all x4, waiting for transfers between devices: 5.83 us -> 1.49 us  [swap_groups(): return lax.all_to_all(value, 'ctx', 0, 0, axis_index_groups=groups)]
    pallas_call x2 -> x5, Pallas kernels: 3.07 us -> 5.52 us  [the longest x1 1.77 us: shards(): pl.pallas_call(gather_kernel, out_shape=(wide_tokens, wide_tokens, both,...]
    pallas_call x1, Pallas kernels: 4.11 us -> 2.52 us  [shards(): pl.pallas_call(main_kernel, out_shape=(wide_tokens, wide_tokens, shape((T...]
  transfers between devices with their start and end apart: 13 -> 13, of which waited for: 7 -> 7; matrix products, arithmetic and copies ran while one was open for 0% -> 0% of each run, Pallas kernels for 9% -> 12%
where the time goes in v6:
time: 102 us; the launch traced here: 101 us
  starting transfers between devices  68.6 us (67%)
  Pallas kernels  20.4 us (20%)
  waiting for transfers between devices  10.3 us (10%)
  between operations  1.49 us (1%)
    all_to_all x4, starting transfers between devices, swap_groups(): return lax.all_to_all(value, 'ctx', 0, 0, axis_index_groups=groups)  40.2 us
    ppermute x8, starting transfers between devices, shifted(): lax.ppermute(value, 'ctx', [(i, i ^ mask) for i in range(lax.axis_size('c...  20.5 us
    ppermute x8, waiting for transfers between devices, shifted(): lax.ppermute(value, 'ctx', [(i, i ^ mask) for i in range(lax.axis_size('c...  8.83 us
    ppermute x1, starting transfers between devices, shards(): w_other = lax.ppermute(w_all, 'mp', [(0, 1), (1, 0)])  7.85 us
    pallas_call x1, Pallas kernels, shards(): pl.pallas_call(bias_kernel, out_shape=(shape((HEADS, T, KEYS), f32), shap...  4.79 us
    pallas_call x1, Pallas kernels, shards(): pl.pallas_call(main_kernel, out_shape=(wide_tokens, wide_tokens, shape((T...  2.52 us
    pallas_call x1, Pallas kernels, shards(): pl.pallas_call(weight_kernel, out_shape=(shape((HEADS, D), f32), wide_tok...  2.11 us
  transfers between devices with their start and end apart: 13, of which 7 were waited for; matrix products, arithmetic and copies ran while one was open for 0% of the time, Pallas kernels for 12%

profile of v6, /device:TPU:1, one launch (start us, length us, event | category | flops | bytes accessed | tf_op | source)
XLA Modules:
  0.0 101.2 jit_solution(17921035630431485871)
XLA Ops:
  1.3 1.8 %leaf.1 = (f32[32,512]{1,0:T(8,128)S(1)}, f32[16,8,640]{2,1,0:T(8,128)}) custom-call(s32[1]{0:T(128)S(6)} %copy.15.len_ref, bf16[128,256]{1,0:T(8,128)(2,1)} %k_hbm.3, bf16[128,256]{1,0:T(8,128)(2,1)} %v_hbm.3), custom_call_target="tpu_custom_call" | custom-call | tf_op jit(solution)/shard_map/leaf/pallas_call | solution.py:442
  3.0 10.7 %all-to-all-start = ((f32[16,8,640]{2,1,0:T(8,128)}), f32[16,8,640]{2,1,0:T(8,128)S(1)}, u32[]{:S(2)}, u32[]{:S(2)}) async-start(f32[16,8,640]{2,1,0:T(8,128)} %get-tuple-element.42), calls=%async_computation | async-start | bytes 655360 | tf_op jit(solution)/shard_map/all_to_all | solution.py:420
  13.8 2.2 %collective-permute-start = (f32[32,512]{1,0:T(8,128)S(1)}, f32[32,512]{1,0:T(8,128)S(1)}, u32[]{:S(2)}, u32[]{:S(2)}) collective-permute-start(f32[32,512]{1,0:T(8,128)S(1)} %get-tuple-element.39.after_ref), channel_id=1, source_target_pairs={{0,2},{2,0},{4,6},{6,4},{8,10},{10,8},{12,14},{14,12},{16,18},{18,... | collective-permute-start | bytes 196616 | tf_op jit(solution)/shard_map/ppermute | solution.py:43
  16.0 0.1 pad_add_fusion.place_ref
  16.0 4.8 %bias.1 = (f32[8,128,384]{2,1,0:T(8,128)S(1)}, f32[128,384]{1,0:T(8,128)S(1)}, f32[2,256,128]{2,1,0:T(8,128)S(1)}, f32[2,8,128]{2,1,0:T(8,128)S(1)}) custom-call(s32[2]{0:T(128)S(1)} %pad_add_fusion.place_ref, f32[1,32]{1,0:T(1,128)} %bitcast.15, f32[1,32]{1,0:T(1,128)} %bitcast.16, f32[16,32]{1,0:T(8,128)} %bitcast.13, ...), custom_call_target="tpu_custom_call" | custom-call | flops 600000000 | bytes 2000000 | tf_op jit(solution)/shard_map/bias/pallas_call | solution.py:455
  20.8 0.0 collective-permute-done.got0_ref
  20.9 0.1 reshape.37
  21.0 0.2 reduce_sum.18.after_merge_ref
  21.1 0.0 all-to-all-done
  21.1 0.9 middle.1
  22.1 14.8 %all-to-all-start.1 = ((f32[16,8,640]{2,1,0:T(8,128)}), f32[16,8,640]{2,1,0:T(8,128)S(1)}, u32[]{:S(2)}, u32[]{:S(2)}) async-start(f32[16,8,640]{2,1,0:T(8,128)} %get-tuple-element.44), calls=%async_computation.1 | async-start | bytes 655360 | tf_op jit(solution)/shard_map/all_to_all | solution.py:420
  36.9 4.3 %collective-permute-start.2 = (f32[32,640]{1,0:T(8,128)S(1)}, f32[32,640]{1,0:T(8,128)S(1)}, u32[]{:S(2)}, u32[]{:S(2)}) collective-permute-start(f32[32,640]{1,0:T(8,128)S(1)} %get-tuple-element.43.own_ref), channel_id=1, source_target_pairs={{0,48},{2,50},{4,52},{6,54},{8,56},{10,58},{12,60},{14,62},{16,32}... | collective-permute-start | bytes 245768 | tf_op jit(solution)/shard_map/ppermute | solution.py:43
  41.2 2.3 %collective-permute-start.1 = (f32[32,640]{1,0:T(8,128)S(1)}, f32[32,640]{1,0:T(8,128)S(1)}, u32[]{:S(2)}, u32[]{:S(2)}) collective-permute-start(f32[32,640]{1,0:T(8,128)S(1)} %pad.4), channel_id=1, source_target_pairs={{0,4},{2,6},{4,0},{6,2},{8,12},{10,14},{12,8},{14,10},{16,20},{18,... | collective-permute-start | bytes 245768 | tf_op jit(solution)/shard_map/ppermute | solution.py:43
  43.5 0.7 collective-permute-done.2.got_ref.got4_ref
  44.2 0.7 merge.1.after_ref
  44.9 2.4 %collective-permute-start.3 = (f32[32,640]{1,0:T(8,128)S(1)}, f32[32,640]{1,0:T(8,128)S(1)}, u32[]{:S(2)}, u32[]{:S(2)}) collective-permute-start(f32[32,640]{1,0:T(8,128)S(1)} %merge.1.after_ref), channel_id=1, source_target_pairs={{0,64},{2,66},{4,68},{6,70},{8,72},{10,74},{12,76},{14,78},{16,80}... | collective-permute-start | bytes 245768 | tf_op jit(solution)/shard_map/ppermute | solution.py:43
  47.3 1.1 %collective-permute-done.1.got1_ref = f32[32,640]{1,0:T(8,128)S(1)} collective-permute-done((f32[32,640]{1,0:T(8,128)S(1)}, f32[32,640]{1,0:T(8,128)S(1)}, u32[]{:S(2)}, u32[]{:S(2)}) %collective-permute-start.1) | collective-permute-done | bytes 81952 | tf_op jit(solution)/shard_map/ppermute | solution.py:43
  48.5 0.0 all-to-all-done.1
  48.5 1.8 %gather.1 = (bf16[128,1024]{1,0:T(8,128)(2,1)S(1)}, bf16[128,1024]{1,0:T(8,128)(2,1)S(1)}, bf16[384,256]{1,0:T(8,128)(2,1)S(1)}, bf16[384,256]{1,0:T(8,128)(2,1)S(1)}, f32[256,128]{1,0:T(8,128)S(1)}) custom-call(s32[2]{0:T(128)S(1)} %pad_add_fusion.place_ref, s32[1]{0:T(128)S(6)} %copy.15.len_ref, bf16[128,1024]{1,0:T(8,128)(2,1)} %q_hbm.1, ...), custom_call_target="tpu_custom_call" | custom-call | flops 300000000 | bytes 2000000 | tf_op jit(solution)/shard_map/gather/pallas_call | solution.py:497
  50.2 0.0 collective-permute-done.3.got5_ref
  50.2 2.5 %attention.1 = (bf16[128,1024]{1,0:T(8,128)(2,1)S(1)}, bf16[128,1024]{1,0:T(8,128)(2,1)S(1)}, f32[128,512]{1,0:T(8,128)S(1)}, f32[256,512]{1,0:T(8,128)S(1)}, f32[8,128,384]{2,1,0:T(8,128)S(1)}) custom-call(s32[1]{0:T(128)S(6)} %copy.15.len_ref, bf16[128,1024]{1,0:T(8,128)(2,1)S(1)} %get-tuple-element.45.q_ref, ...), custom_call_target="tpu_custom_call" | custom-call | tf_op jit(solution)/shard_map/attention/pallas_call | solution.py:508
  52.8 3.1 %collective-permute-start.4 = (f32[32,512]{1,0:T(8,128)S(1)}, f32[32,512]{1,0:T(8,128)S(1)}, u32[]{:S(2)}, u32[]{:S(2)}) collective-permute-start(f32[32,512]{1,0:T(8,128)S(1)} %get-tuple-element.72), channel_id=1, source_target_pairs={{0,64},{2,66},{4,68},{6,70},{8,72},{10,74},{12,76},{14,78},{16,80}... | collective-permute-start | bytes 196616 | tf_op jit(solution)/shard_map/ppermute | solution.py:43
  55.9 2.1 %weights.1 = (f32[8,128]{1,0:T(8,128)S(1)}, bf16[128,1024]{1,0:T(8,128)(2,1)}, bf16[128,1024]{1,0:T(8,128)(2,1)}) custom-call(f32[2,256,128]{2,1,0:T(8,128)S(1)} %get-tuple-element.40.line_ref, f32[2,8,128]{2,1,0:T(8,128)S(1)} %get-tuple-element.41.after_bias_ref.slot_ref, f32[8,128,384]{2,1,0:T(8,128)S(1)} %get-tuple-element.51.ds_ref, ...), custom_call_target="tpu_custom_call" | custom-call | flops 900000000 | bytes 2000000 | tf_op jit(solution)/shard_map/weights/pallas_call | solution.py:524
  58.0 0.0 collective-permute-done.4.came5_ref
  58.0 1.4 %away.1 = (f32[16,8,640]{2,1,0:T(8,128)}, f32[32,512]{1,0:T(8,128)S(1)}) custom-call(s32[2]{0:T(128)S(1)} %pad_add_fusion.place_ref, f32[8,128]{1,0:T(8,128)S(1)} %get-tuple-element.57.w_ref, f32[256,512]{1,0:T(8,128)S(1)} %get-tuple-element.58.coarse_ref, f32[32,512]{1,0:T(8,128)S(1)} %collective-permute-done.4.came5_ref), custom_call_target="tpu_custom_call" | custom-call | tf_op jit(solution)/shard_map/away/pallas_call | solution.py:534
  59.4 8.6 %all-to-all-start.2 = ((f32[16,8,640]{2,1,0:T(8,128)}), f32[16,8,640]{2,1,0:T(8,128)S(1)}, u32[]{:S(2)}, u32[]{:S(2)}) async-start(f32[16,8,640]{2,1,0:T(8,128)} %get-tuple-element.59), calls=%async_computation.2 | async-start | bytes 655360 | tf_op jit(solution)/shard_map/all_to_all | solution.py:420
  68.1 1.9 %collective-permute-start.6 = (f32[32,512]{1,0:T(8,128)S(1)}, f32[32,512]{1,0:T(8,128)S(1)}, u32[]{:S(2)}, u32[]{:S(2)}) collective-permute-start(f32[32,512]{1,0:T(8,128)S(1)} %get-tuple-element.71), channel_id=1, source_target_pairs={{0,4},{2,6},{4,0},{6,2},{8,12},{10,14},{12,8},{14,10},{16,20},{18,... | collective-permute-start | bytes 196616 | tf_op jit(solution)/shard_map/ppermute | solution.py:43
  70.0 2.2 %collective-permute-start.5 = (f32[32,512]{1,0:T(8,128)S(1)}, f32[32,512]{1,0:T(8,128)S(1)}, u32[]{:S(2)}, u32[]{:S(2)}) collective-permute-start(f32[32,512]{1,0:T(8,128)S(1)} %get-tuple-element.60), channel_id=1, source_target_pairs={{0,48},{2,50},{4,52},{6,54},{8,56},{10,58},{12,60},{14,62},{16,32}... | collective-permute-start | bytes 196616 | tf_op jit(solution)/shard_map/ppermute | solution.py:43
  72.2 2.4 %collective-permute-done.6.came1_ref = f32[32,512]{1,0:T(8,128)S(1)} collective-permute-done((f32[32,512]{1,0:T(8,128)S(1)}, f32[32,512]{1,0:T(8,128)S(1)}, u32[]{:S(2)}, u32[]{:S(2)}) %collective-permute-start.6) | collective-permute-done | bytes 65568 | tf_op jit(solution)/shard_map/ppermute | solution.py:43
  74.6 0.8 base.1
  75.4 1.2 %collective-permute-done.5.came4_ref = f32[32,512]{1,0:T(8,128)S(1)} collective-permute-done((f32[32,512]{1,0:T(8,128)S(1)}, f32[32,512]{1,0:T(8,128)S(1)}, u32[]{:S(2)}, u32[]{:S(2)}) %collective-permute-start.5) | collective-permute-done | bytes 65568 | tf_op jit(solution)/shard_map/ppermute | solution.py:43
  76.6 0.1 all-to-all-done.2.away_ref
  76.7 1.4 %return.1 = f32[16,8,640]{2,1,0:T(8,128)} custom-call(s32[2]{0:T(128)S(1)} %pad_add_fusion.place_ref, f32[16,8,640]{2,1,0:T(8,128)S(1)} %all-to-all-done.2.away_ref, f32[32,512]{1,0:T(8,128)S(1)} %collective-permute-done.5.came4_ref, f32[128,512]{1,0:T(8,128)S(1)} %get-tuple-element.61.base_ref), custom_call_target="tpu_custom_call" | custom-call | tf_op jit(solution)/shard_map/return/pallas_call | solution.py:554
  78.2 6.0 %all-to-all-start.3 = ((f32[16,8,640]{2,1,0:T(8,128)}), f32[16,8,640]{2,1,0:T(8,128)S(1)}, u32[]{:S(2)}, u32[]{:S(2)}) async-start(f32[16,8,640]{2,1,0:T(8,128)} %return.1), calls=%async_computation.3 | async-start | bytes 655360 | tf_op jit(solution)/shard_map/all_to_all | solution.py:420
  84.2 2.2 %collective-permute-start.7 = (f32[32,512]{1,0:T(8,128)S(1)}, f32[32,512]{1,0:T(8,128)S(1)}, u32[]{:S(2)}, u32[]{:S(2)}) collective-permute-start(f32[32,512]{1,0:T(8,128)S(1)} %get-tuple-element.63), channel_id=1, source_target_pairs={{0,2},{2,0},{4,6},{6,4},{8,10},{10,8},{12,14},{14,12},{16,18},{18,... | collective-permute-start | bytes 196616 | tf_op jit(solution)/shard_map/ppermute | solution.py:43
  86.4 3.3 %collective-permute-done.7.came0_ref = f32[32,512]{1,0:T(8,128)S(1)} collective-permute-done((f32[32,512]{1,0:T(8,128)S(1)}, f32[32,512]{1,0:T(8,128)S(1)}, u32[]{:S(2)}, u32[]{:S(2)}) %collective-permute-start.7) | collective-permute-done | bytes 65568 | tf_op jit(solution)/shard_map/ppermute | solution.py:43
  89.7 0.7 own.1.own_ref
  90.4 1.4 %all-to-all-done.3.near_ref = f32[16,8,640]{2,1,0:T(8,128)S(1)} async-done(((f32[16,8,640]{2,1,0:T(8,128)}), f32[16,8,640]{2,1,0:T(8,128)S(1)}, u32[]{:S(2)}, u32[]{:S(2)}) %all-to-all-start.3) | async-done | bytes 327712 | tf_op jit(solution)/shard_map/all_to_all | solution.py:420
  91.8 7.9 %collective-permute-start.8 = (f32[8,128]{1,0:T(8,128)S(1)}, f32[8,128]{1,0:T(8,128)S(1)}, u32[]{:S(2)}, u32[]{:S(2)}) collective-permute-start(f32[8,128]{1,0:T(8,128)S(1)} %add_reduce_fusion.mine_ref), channel_id=1, source_target_pairs={{0,1},{1,0},{2,3},{3,2},{4,5},{5,4},{6,7},{7,6},{8,9},{9,8},{10,11... | collective-permute-start | bytes 12296 | tf_op jit(solution)/shard_map/ppermute | solution.py:576
  99.6 0.8 final.1
  100.5 0.0 collective-permute-done.8.got_ref
  100.5 0.7 outputs.1
  (5 shorter events, 0.1 us)
Async XLA Ops:
  3.0 18.1 %all-to-all-start = ((f32[16,8,640]{2,1,0:T(8,128)}), f32[16,8,640]{2,1,0:T(8,128)S(1)}, u32[]{:S(2)}, u32[]{:S(2)}) async-start(f32[16,8,640]{2,1,0:T(8,128)} %get-tuple-element.42), calls=%async_computation | async-start | bytes 655360 | tf_op jit(solution)/shard_map/all_to_all | solution.py:420
  13.8 7.1 %collective-permute-start = (f32[32,512]{1,0:T(8,128)S(1)}, f32[32,512]{1,0:T(8,128)S(1)}, u32[]{:S(2)}, u32[]{:S(2)}) collective-permute-start(f32[32,512]{1,0:T(8,128)S(1)} %get-tuple-element.39.after_ref), channel_id=1, source_target_pairs={{0,2},{2,0},{4,6},{6,4},{8,10},{10,8},{12,14},{14,12},{16,18},{18,... | collective-permute-start | bytes 196616 | tf_op jit(solution)/shard_map/ppermute | solution.py:43
  22.1 26.4 %all-to-all-start.1 = ((f32[16,8,640]{2,1,0:T(8,128)}), f32[16,8,640]{2,1,0:T(8,128)S(1)}, u32[]{:S(2)}, u32[]{:S(2)}) async-start(f32[16,8,640]{2,1,0:T(8,128)} %get-tuple-element.44), calls=%async_computation.1 | async-start | bytes 655360 | tf_op jit(solution)/shard_map/all_to_all | solution.py:420
  36.9 7.3 %collective-permute-start.2 = (f32[32,640]{1,0:T(8,128)S(1)}, f32[32,640]{1,0:T(8,128)S(1)}, u32[]{:S(2)}, u32[]{:S(2)}) collective-permute-start(f32[32,640]{1,0:T(8,128)S(1)} %get-tuple-element.43.own_ref), channel_id=1, source_target_pairs={{0,48},{2,50},{4,52},{6,54},{8,56},{10,58},{12,60},{14,62},{16,32}... | collective-permute-start | bytes 245768 | tf_op jit(solution)/shard_map/ppermute | solution.py:43
  41.2 7.3 %collective-permute-start.1 = (f32[32,640]{1,0:T(8,128)S(1)}, f32[32,640]{1,0:T(8,128)S(1)}, u32[]{:S(2)}, u32[]{:S(2)}) collective-permute-start(f32[32,640]{1,0:T(8,128)S(1)} %pad.4), channel_id=1, source_target_pairs={{0,4},{2,6},{4,0},{6,2},{8,12},{10,14},{12,8},{14,10},{16,20},{18,... | collective-permute-start | bytes 245768 | tf_op jit(solution)/shard_map/ppermute | solution.py:43
  44.9 5.3 %collective-permute-start.3 = (f32[32,640]{1,0:T(8,128)S(1)}, f32[32,640]{1,0:T(8,128)S(1)}, u32[]{:S(2)}, u32[]{:S(2)}) collective-permute-start(f32[32,640]{1,0:T(8,128)S(1)} %merge.1.after_ref), channel_id=1, source_target_pairs={{0,64},{2,66},{4,68},{6,70},{8,72},{10,74},{12,76},{14,78},{16,80}... | collective-permute-start | bytes 245768 | tf_op jit(solution)/shard_map/ppermute | solution.py:43
  52.8 5.2 %collective-permute-start.4 = (f32[32,512]{1,0:T(8,128)S(1)}, f32[32,512]{1,0:T(8,128)S(1)}, u32[]{:S(2)}, u32[]{:S(2)}) collective-permute-start(f32[32,512]{1,0:T(8,128)S(1)} %get-tuple-element.72), channel_id=1, source_target_pairs={{0,64},{2,66},{4,68},{6,70},{8,72},{10,74},{12,76},{14,78},{16,80}... | collective-permute-start | bytes 196616 | tf_op jit(solution)/shard_map/ppermute | solution.py:43
  59.4 17.3 %all-to-all-start.2 = ((f32[16,8,640]{2,1,0:T(8,128)}), f32[16,8,640]{2,1,0:T(8,128)S(1)}, u32[]{:S(2)}, u32[]{:S(2)}) async-start(f32[16,8,640]{2,1,0:T(8,128)} %get-tuple-element.59), calls=%async_computation.2 | async-start | bytes 655360 | tf_op jit(solution)/shard_map/all_to_all | solution.py:420
  68.1 6.5 %collective-permute-start.6 = (f32[32,512]{1,0:T(8,128)S(1)}, f32[32,512]{1,0:T(8,128)S(1)}, u32[]{:S(2)}, u32[]{:S(2)}) collective-permute-start(f32[32,512]{1,0:T(8,128)S(1)} %get-tuple-element.71), channel_id=1, source_target_pairs={{0,4},{2,6},{4,0},{6,2},{8,12},{10,14},{12,8},{14,10},{16,20},{18,... | collective-permute-start | bytes 196616 | tf_op jit(solution)/shard_map/ppermute | solution.py:43
  70.0 6.6 %collective-permute-start.5 = (f32[32,512]{1,0:T(8,128)S(1)}, f32[32,512]{1,0:T(8,128)S(1)}, u32[]{:S(2)}, u32[]{:S(2)}) collective-permute-start(f32[32,512]{1,0:T(8,128)S(1)} %get-tuple-element.60), channel_id=1, source_target_pairs={{0,48},{2,50},{4,52},{6,54},{8,56},{10,58},{12,60},{14,62},{16,32}... | collective-permute-start | bytes 196616 | tf_op jit(solution)/shard_map/ppermute | solution.py:43
  78.2 13.6 %all-to-all-start.3 = ((f32[16,8,640]{2,1,0:T(8,128)}), f32[16,8,640]{2,1,0:T(8,128)S(1)}, u32[]{:S(2)}, u32[]{:S(2)}) async-start(f32[16,8,640]{2,1,0:T(8,128)} %return.1), calls=%async_computation.3 | async-start | bytes 655360 | tf_op jit(solution)/shard_map/all_to_all | solution.py:420
  84.2 5.5 %collective-permute-start.7 = (f32[32,512]{1,0:T(8,128)S(1)}, f32[32,512]{1,0:T(8,128)S(1)}, u32[]{:S(2)}, u32[]{:S(2)}) collective-permute-start(f32[32,512]{1,0:T(8,128)S(1)} %get-tuple-element.63), channel_id=1, source_target_pairs={{0,2},{2,0},{4,6},{6,4},{8,10},{10,8},{12,14},{14,12},{16,18},{18,... | collective-permute-start | bytes 196616 | tf_op jit(solution)/shard_map/ppermute | solution.py:43
  91.8 8.7 %collective-permute-start.8 = (f32[8,128]{1,0:T(8,128)S(1)}, f32[8,128]{1,0:T(8,128)S(1)}, u32[]{:S(2)}, u32[]{:S(2)}) collective-permute-start(f32[8,128]{1,0:T(8,128)S(1)} %add_reduce_fusion.mine_ref), channel_id=1, source_target_pairs={{0,1},{1,0},{2,3},{3,2},{4,5},{5,4},{6,7},{7,6},{8,9},{9,8},{10,11... | collective-permute-start | bytes 12296 | tf_op jit(solution)/shard_map/ppermute | solution.py:576

commit v7 on v6

--- a/solution.py
+++ b/solution.py
@@ -17,8 +17,7 @@
 KV = 2
 GROUP = HEADS // KV
 SUB = 8
-BATCH = 4
-UNROLL = 2
+UNROLL = 4
 CHUNK = 8
 SIDE = 16
 FIRST = {"low": 12, "high": 14, "away": 3, "near": 2}
@@ -33,6 +32,7 @@
 HBM = pl.BlockSpec(memory_space=pltpu.HBM)
 ANY = pl.BlockSpec(memory_space=pl.ANY)
 SMALL = pltpu.CompilerParams(vmem_limit_bytes=12 * 2**20)
+LARGE = pltpu.CompilerParams(vmem_limit_bytes=24 * 2**20)
 
 
 def dot(a, b, dims=(((1,), (0,)), ((), ()))):
@@ -171,7 +171,8 @@
     for level, ref, first in ((2, low_ref, FIRST["low"]), (6, high_ref, FIRST["high"])):
         quarter = ((ctx >> level) & 3) ^ 1
         half = ((ctx >> level + 1) & 1) ^ 1
-        place = (((col >> 3) ^ first) << 3) + (col & 7)
+        member = col >> 3 if level == 2 else side_member(col >> 3)
+        place = ((member ^ first) << 3) + (col & 7)
         want = jnp.where(row < COARSE, quarter * COARSE + row, (half - 1) * COARSE + row)
         rows = picked(jnp.where(row < COARSE, place, place >> 1) == want, ref[...])
         sib_ref[level * COARSE : (level + 2) * COARSE, :] = rows
@@ -214,35 +215,40 @@
     live = jnp.concatenate([token_live.astype(jnp.float32), count_t], axis=1) > 0.0
     row_live = lax.broadcasted_iota(jnp.int32, (T, 1), 0) < length
     inverse_5 = inverse[5 * COARSE : 6 * COARSE]
-    for j in range(KV):
-        cols = slice(j * D, (j + 1) * D)
-        vcols = slice((KV + j) * D, (KV + j + 1) * D)
-        keys = with_level_5(keys_ref[:, cols], (got5_ref[:, cols] * inverse_5).astype(jnp.bfloat16), T)
-        values = with_level_5(values_ref[:, cols], (got5_ref[:, vcols] * inverse_5).astype(jnp.bfloat16), T)
-        key_grads = jnp.zeros((KEYS, D), jnp.float32)
-        value_grads = jnp.zeros((KEYS, D), jnp.float32)
-        for first in range(j * GROUP, (j + 1) * GROUP, BATCH):
-            heads = range(first, first + BATCH)
-            query = jnp.concatenate([q_ref[:, h * D : (h + 1) * D] for h in heads], axis=0)
-            grad = jnp.concatenate([g_ref[:, h * D : (h + 1) * D] for h in heads], axis=0)
-            scores = dot(query, keys, NT) * SCALE + bias_ref[first : first + BATCH].reshape(BATCH * T, KEYS)
-            scores = jnp.where(live, scores, -jnp.inf)
-            weights = jnp.exp(scores - jnp.max(scores, axis=1, keepdims=True))
-            probs = weights * (1.0 / jnp.sum(weights, axis=1, keepdims=True))
-            probs_b = probs.astype(jnp.bfloat16)
-            attended = dot(probs_b, values)
-            dprobs = dot(grad, values, NT)
-            dscores = probs * (dprobs - jnp.sum(probs * dprobs, axis=1, keepdims=True))
-            ds_ref[first : first + BATCH] = dscores.reshape(BATCH, T, KEYS)
-            dscores_b = dscores.astype(jnp.bfloat16)
-            grad_query = dot(dscores_b, keys) * SCALE
-            for n, h in enumerate(heads):
-                rows = slice(n * T, (n + 1) * T)
-                out_ref[:, h * D : (h + 1) * D] = jnp.where(row_live, attended[rows], 0.0).astype(jnp.bfloat16)
-                gq_ref[:, h * D : (h + 1) * D] = grad_query[rows].astype(jnp.bfloat16)
-            key_grads = key_grads + dot(dscores_b, query, TN)
-            value_grads = value_grads + dot(probs_b, grad, TN)
-        key_grads = key_grads * SCALE
+    def stacked(ref):
+        return jnp.concatenate([ref[:, h * D : (h + 1) * D] for h in range(HEADS)], axis=0)
+
+    def per_group(*pairs, dims=(((1,), (0,)), ((), ()))):
+        return jnp.concatenate([dot(a, b, dims) for a, b in pairs], axis=0)
+
+    span = GROUP * T
+    lanes = [slice(j * D, (j + 1) * D) for j in range(KV)]
+    value_lanes = [slice((KV + j) * D, (KV + j + 1) * D) for j in range(KV)]
+    keys = [with_level_5(keys_ref[:, at], (got5_ref[:, at] * inverse_5).astype(jnp.bfloat16), T) for at in lanes]
+    values = [
+        with_level_5(values_ref[:, at], (got5_ref[:, wide] * inverse_5).astype(jnp.bfloat16), T)
+        for at, wide in zip(lanes, value_lanes)
+    ]
+    query, grad = stacked(q_ref), stacked(g_ref)
+    groups = [slice(j * span, (j + 1) * span) for j in range(KV)]
+    scores = per_group(*[(query[at], k) for at, k in zip(groups, keys)], dims=NT) * SCALE
+    scores = jnp.where(live, scores + bias_ref[...].reshape(HEADS * T, KEYS), -jnp.inf)
+    weights = jnp.exp(scores - jnp.max(scores, axis=1, keepdims=True))
+    probs = weights * (1.0 / jnp.sum(weights, axis=1, keepdims=True))
+    probs_b = probs.astype(jnp.bfloat16)
+    attended = per_group(*[(probs_b[at], v) for at, v in zip(groups, values)])
+    dprobs = per_group(*[(grad[at], v) for at, v in zip(groups, values)], dims=NT)
+    dscores = probs * (dprobs - jnp.sum(probs * dprobs, axis=1, keepdims=True))
+    ds_ref[...] = dscores.reshape(HEADS, T, KEYS)
+    dscores_b = dscores.astype(jnp.bfloat16)
+    grad_query = per_group(*[(dscores_b[at], k) for at, k in zip(groups, keys)]) * SCALE
+    for h in range(HEADS):
+        rows = slice(h * T, (h + 1) * T)
+        out_ref[:, h * D : (h + 1) * D] = jnp.where(row_live, attended[rows], 0.0).astype(jnp.bfloat16)
+        gq_ref[:, h * D : (h + 1) * D] = grad_query[rows].astype(jnp.bfloat16)
+    for at, cols, vcols in zip(groups, lanes, value_lanes):
+        key_grads = dot(dscores_b[at], query[at], TN) * SCALE
+        value_grads = dot(probs_b[at], grad[at], TN)
         own_ref[:, cols] = key_grads[:T]
         own_ref[:, vcols] = value_grads[:T]
         coarse_ref[:, cols] = key_grads[T:] * inverse
@@ -250,7 +256,8 @@
 
 
 def weight_kernel(
-    line_ref, slot_ref, ds_ref, phase_ref, out_ref, gq_ref, w_ref, out_hbm, gq_hbm, acc_ref, sems
+    place_ref, line_ref, slot_ref, ds_ref, phase_ref, out_ref, gq_ref, coarse_ref,
+    w_ref, rows_ref, out_hbm, gq_hbm, acc_ref, sems,
 ):
     copies = fetch([(out_ref, out_hbm), (gq_ref, gq_hbm)], sems)
     acc_ref[...] = jnp.zeros_like(acc_ref)
@@ -282,6 +289,7 @@
     unit = lax.broadcasted_iota(jnp.int32, (HIDDEN * SUB, D), 0) // SUB
     lane = lax.broadcasted_iota(jnp.int32, (HIDDEN * SUB, D), 1) % HIDDEN
     sums = exact_dot(acc, jnp.where(unit == lane, 1.0, 0.0))
+    rows_ref[...] = chosen(SIDE * CHUNK, level_parts(place_ref[0], 6, coarse_ref))
     w_ref[...] = slot_ref[1] * sums[:HEADS] + slot_ref[0] * sums[HEADS:]
     for copy in copies:
         copy.wait()
@@ -346,15 +354,23 @@
     )
 
 
-def fill(payload_ref, first, rows, weights):
+def side_place(member):
+    return (member >> 1) | ((member & 1) << 3)
+
+
+def side_member(place):
+    return ((place & 7) << 1) | (place >> 3)
+
+
+def fill(payload_ref, place_of, rows, weights):
     for n in range(SIDE):
-        payload_ref[n ^ first, :, : 2 * WIDTH] = rows[n * CHUNK : (n + 1) * CHUNK]
-        payload_ref[n ^ first, :, 2 * WIDTH :] = weights
-
-
-def away_kernel(place_ref, w_ref, coarse_ref, came5_ref, away_ref, send_ref):
+        payload_ref[place_of(n), :, : 2 * WIDTH] = rows[n * CHUNK : (n + 1) * CHUNK]
+        payload_ref[place_of(n), :, 2 * WIDTH :] = weights
+
+
+def away_kernel(place_ref, w_ref, rows_ref, coarse_ref, came5_ref, away_ref, send_ref):
     ctx = place_ref[0]
-    fill(away_ref, FIRST["away"], chosen(SIDE * CHUNK, level_parts(ctx, 6, coarse_ref)), w_ref[...])
+    fill(away_ref, lambda n: side_place(n ^ FIRST["away"]), rows_ref[...], w_ref[...])
     send_ref[...] = sibling_rows(ctx, 4, coarse_ref, came5_ref)
 
 
@@ -373,7 +389,7 @@
     ctx = place_ref[0]
     away = summed(away_ref)
     rows = base_ref[...] + chosen(SIDE * CHUNK, [(came4_ref[...], every(2)), (away[:, : 2 * WIDTH], every(4))])
-    fill(near_ref, FIRST["near"] ^ (((ctx >> 4) & 1) * 8), rows, away[:, 2 * WIDTH :])
+    fill(near_ref, lambda n: n ^ FIRST["near"] ^ (((ctx >> 4) & 1) * 8), rows, away[:, 2 * WIDTH :])
 
 
 def own_kernel(place_ref, own_ref, came1_ref, came0_ref, out_ref):
@@ -432,7 +448,7 @@
         return [[high * SIDE + (low ^ first ^ (odd * (high % 2))) for low in blocks] for high in blocks]
 
     def high_groups(first):
-        order = [high ^ first for high in blocks]
+        order = [side_member(place) ^ first for place in blocks]
         return [[high * SIDE + (low ^ (8 * (high % 2))) for high in order] for low in blocks]
 
     payload = shape((SIDE, CHUNK, 2 * WIDTH + D), f32)
@@ -516,29 +532,29 @@
         ),
         in_specs=[SMEM] + [VMEM] * 7,
         out_specs=(VMEM,) * 5,
-        compiler_params=SMALL,
+        compiler_params=LARGE,
         name="attention",
     )(lengths, *gathered, got5, bias)
 
     came5 = exchange(coarse[5 * COARSE : 6 * COARSE], 5)
-    w_part, attended, grad_q = pl.pallas_call(
+    w_part, away_rows, attended, grad_q = pl.pallas_call(
         weight_kernel,
-        out_shape=(shape((HEADS, D), f32), wide_tokens, wide_tokens),
-        in_specs=[VMEM] * 6,
-        out_specs=(VMEM, HBM, HBM),
+        out_shape=(shape((HEADS, D), f32), shape((T, 2 * WIDTH), f32), wide_tokens, wide_tokens),
+        in_specs=[SMEM] + [VMEM] * 7,
+        out_specs=(VMEM, VMEM, HBM, HBM),
         scratch_shapes=[pltpu.VMEM((4 * HEADS * SUB, HIDDEN * SUB), f32), dma((2,))],
         compiler_params=SMALL,
         cost_estimate=pl.CostEstimate(flops=900_000_000, bytes_accessed=2_000_000, transcendentals=0),
         name="weights",
-    )(line, slot, dscores, phase, attended, grad_q)
+    )(place, line, slot, dscores, phase, attended, grad_q, coarse)
     away, send4 = pl.pallas_call(
         away_kernel,
         out_shape=(payload, rows),
-        in_specs=[SMEM] + [VMEM] * 3,
+        in_specs=[SMEM] + [VMEM] * 4,
         out_specs=(VMEM, VMEM),
         compiler_params=SMALL,
         name="away",
-    )(place, w_part, coarse, came5)
+    )(place, w_part, away_rows, coarse, came5)
     away = swap_groups(away, high_groups(FIRST["away"]))
     came4 = exchange(send4, 4)
     came1 = exchange(coarse[COARSE : 2 * COARSE], 1)

time: 102 us -> 101 us (level)
    all_to_all x4, starting transfers between devices: 40.2 us -> 38.5 us  [swap_groups(): return lax.all_to_all(value, 'ctx', 0, 0, axis_index_groups=groups)]
  transfers between devices with their start and end apart: 13 -> 13, of which waited for: 7 -> 8; matrix products, arithmetic and copies ran while one was open for 0% -> 0% of each run, Pallas kernels for 12% -> 11%
where the time goes in v7:
time: 101 us; the launch traced here: 99.9 us
  starting transfers between devices  67.7 us (67%)
  Pallas kernels  19.4 us (19%)
  waiting for transfers between devices  11 us (11%)
  between operations  1.48 us (1%)
    all_to_all x4, starting transfers between devices, swap_groups(): return lax.all_to_all(value, 'ctx', 0, 0, axis_index_groups=groups)  38.5 us
    ppermute x8, starting transfers between devices, shifted(): lax.ppermute(value, 'ctx', [(i, i ^ mask) for i in range(lax.axis_size('c...  20.5 us
    ppermute x8, waiting for transfers between devices, shifted(): lax.ppermute(value, 'ctx', [(i, i ^ mask) for i in range(lax.axis_size('c...  9.58 us
    ppermute x1, starting transfers between devices, shards(): w_other = lax.ppermute(w_all, 'mp', [(0, 1), (1, 0)])  8.69 us
    pallas_call x1, Pallas kernels, shards(): pl.pallas_call(bias_kernel, out_shape=(shape((HEADS, T, KEYS), f32), shap...  4.38 us
    pallas_call x1, Pallas kernels, shards(): pl.pallas_call(weight_kernel, out_shape=(shape((HEADS, D), f32), shape((T...  2.3 us
  transfers between devices with their start and end apart: 13, of which 8 were waited for; matrix products, arithmetic and copies ran while one was open for 0% of the time, Pallas kernels for 11%

profile of v7, /device:TPU:1, one launch (start us, length us, event | category | flops | bytes accessed | tf_op | source)
XLA Modules:
  0.0 99.9 jit_solution(14215282005056057316)
XLA Ops:
  1.3 1.8 %leaf.1 = (f32[32,512]{1,0:T(8,128)S(1)}, f32[16,8,640]{2,1,0:T(8,128)}) custom-call(s32[1]{0:T(128)S(6)} %copy.15.len_ref, bf16[128,256]{1,0:T(8,128)(2,1)} %k_hbm.3, bf16[128,256]{1,0:T(8,128)(2,1)} %v_hbm.3), custom_call_target="tpu_custom_call" | custom-call | tf_op jit(solution)/shard_map/leaf/pallas_call | solution.py:458
  3.0 10.7 %all-to-all-start = ((f32[16,8,640]{2,1,0:T(8,128)}), f32[16,8,640]{2,1,0:T(8,128)S(1)}, u32[]{:S(2)}, u32[]{:S(2)}) async-start(f32[16,8,640]{2,1,0:T(8,128)} %get-tuple-element.43), calls=%async_computation | async-start | bytes 655360 | tf_op jit(solution)/shard_map/all_to_all | solution.py:436
  13.8 2.2 %collective-permute-start = (f32[32,512]{1,0:T(8,128)S(1)}, f32[32,512]{1,0:T(8,128)S(1)}, u32[]{:S(2)}, u32[]{:S(2)}) collective-permute-start(f32[32,512]{1,0:T(8,128)S(1)} %get-tuple-element.40.after_ref), channel_id=1, source_target_pairs={{0,2},{2,0},{4,6},{6,4},{8,10},{10,8},{12,14},{14,12},{16,18},{18,... | collective-permute-start | bytes 196616 | tf_op jit(solution)/shard_map/ppermute | solution.py:43
  16.0 0.1 pad_add_fusion.place_ref
  16.0 4.4 %bias.1 = (f32[8,128,384]{2,1,0:T(8,128)S(1)}, f32[128,384]{1,0:T(8,128)S(1)}, f32[2,256,128]{2,1,0:T(8,128)S(1)}, f32[2,8,128]{2,1,0:T(8,128)S(1)}) custom-call(s32[2]{0:T(128)S(1)} %pad_add_fusion.place_ref, f32[1,32]{1,0:T(1,128)} %bitcast.15, f32[1,32]{1,0:T(1,128)} %bitcast.16, f32[16,32]{1,0:T(8,128)} %bitcast.13, ...), custom_call_target="tpu_custom_call" | custom-call | flops 600000000 | bytes 2000000 | tf_op jit(solution)/shard_map/bias/pallas_call | solution.py:471
  20.4 0.0 collective-permute-done.got0_ref
  20.5 0.1 reshape.37
  20.6 0.2 reduce_sum.18.after_merge_ref
  20.7 0.0 all-to-all-done
  20.7 0.9 middle.1
  21.6 15.2 %all-to-all-start.1 = ((f32[16,8,640]{2,1,0:T(8,128)}), f32[16,8,640]{2,1,0:T(8,128)S(1)}, u32[]{:S(2)}, u32[]{:S(2)}) async-start(f32[16,8,640]{2,1,0:T(8,128)} %get-tuple-element.45), calls=%async_computation.1 | async-start | bytes 655360 | tf_op jit(solution)/shard_map/all_to_all | solution.py:436
  36.8 4.3 %collective-permute-start.2 = (f32[32,640]{1,0:T(8,128)S(1)}, f32[32,640]{1,0:T(8,128)S(1)}, u32[]{:S(2)}, u32[]{:S(2)}) collective-permute-start(f32[32,640]{1,0:T(8,128)S(1)} %get-tuple-element.44.own_ref), channel_id=1, source_target_pairs={{0,48},{2,50},{4,52},{6,54},{8,56},{10,58},{12,60},{14,62},{16,32}... | collective-permute-start | bytes 245768 | tf_op jit(solution)/shard_map/ppermute | solution.py:43
  41.2 2.3 %collective-permute-start.1 = (f32[32,640]{1,0:T(8,128)S(1)}, f32[32,640]{1,0:T(8,128)S(1)}, u32[]{:S(2)}, u32[]{:S(2)}) collective-permute-start(f32[32,640]{1,0:T(8,128)S(1)} %pad.4), channel_id=1, source_target_pairs={{0,4},{2,6},{4,0},{6,2},{8,12},{10,14},{12,8},{14,10},{16,20},{18,... | collective-permute-start | bytes 245768 | tf_op jit(solution)/shard_map/ppermute | solution.py:43
  43.5 1.4 %collective-permute-done.2.got_ref.got4_ref = f32[32,640]{1,0:T(8,128)S(1)} collective-permute-done((f32[32,640]{1,0:T(8,128)S(1)}, f32[32,640]{1,0:T(8,128)S(1)}, u32[]{:S(2)}, u32[]{:S(2)}) %collective-permute-start.2) | collective-permute-done | bytes 81952 | tf_op jit(solution)/shard_map/ppermute | solution.py:43
  44.9 0.7 merge.1.after_ref
  45.6 2.5 %collective-permute-start.3 = (f32[32,640]{1,0:T(8,128)S(1)}, f32[32,640]{1,0:T(8,128)S(1)}, u32[]{:S(2)}, u32[]{:S(2)}) collective-permute-start(f32[32,640]{1,0:T(8,128)S(1)} %merge.1.after_ref), channel_id=1, source_target_pairs={{0,64},{2,66},{4,68},{6,70},{8,72},{10,74},{12,76},{14,78},{16,80}... | collective-permute-start | bytes 245768 | tf_op jit(solution)/shard_map/ppermute | solution.py:43
  48.1 0.2 collective-permute-done.1.got1_ref
  48.3 0.0 all-to-all-done.1
  48.3 1.8 %gather.1 = (bf16[128,1024]{1,0:T(8,128)(2,1)S(1)}, bf16[128,1024]{1,0:T(8,128)(2,1)S(1)}, bf16[384,256]{1,0:T(8,128)(2,1)S(1)}, bf16[384,256]{1,0:T(8,128)(2,1)S(1)}, f32[256,128]{1,0:T(8,128)S(1)}) custom-call(s32[2]{0:T(128)S(1)} %pad_add_fusion.place_ref, s32[1]{0:T(128)S(6)} %copy.15.len_ref, bf16[128,1024]{1,0:T(8,128)(2,1)} %q_hbm.1, ...), custom_call_target="tpu_custom_call" | custom-call | flops 300000000 | bytes 2000000 | tf_op jit(solution)/shard_map/gather/pallas_call | solution.py:513
  50.1 0.7 collective-permute-done.3.got5_ref
  50.8 1.9 %attention.1 = (bf16[128,1024]{1,0:T(8,128)(2,1)S(1)}, bf16[128,1024]{1,0:T(8,128)(2,1)S(1)}, f32[128,512]{1,0:T(8,128)S(1)}, f32[256,512]{1,0:T(8,128)S(1)}, f32[8,128,384]{2,1,0:T(8,128)S(1)}) custom-call(s32[1]{0:T(128)S(6)} %copy.15.len_ref, bf16[128,1024]{1,0:T(8,128)(2,1)S(1)} %get-tuple-element.46.q_ref, ...), custom_call_target="tpu_custom_call" | custom-call | tf_op jit(solution)/shard_map/attention/pallas_call | solution.py:524
  52.7 2.5 %collective-permute-start.4 = (f32[32,512]{1,0:T(8,128)S(1)}, f32[32,512]{1,0:T(8,128)S(1)}, u32[]{:S(2)}, u32[]{:S(2)}) collective-permute-start(f32[32,512]{1,0:T(8,128)S(1)} %get-tuple-element.74), channel_id=1, source_target_pairs={{0,64},{2,66},{4,68},{6,70},{8,72},{10,74},{12,76},{14,78},{16,80}... | collective-permute-start | bytes 196616 | tf_op jit(solution)/shard_map/ppermute | solution.py:43
  55.2 2.3 %weights.1 = (f32[8,128]{1,0:T(8,128)S(1)}, f32[128,512]{1,0:T(8,128)S(1)}, bf16[128,1024]{1,0:T(8,128)(2,1)}, bf16[128,1024]{1,0:T(8,128)(2,1)}) custom-call(s32[2]{0:T(128)S(1)} %pad_add_fusion.place_ref, f32[2,256,128]{2,1,0:T(8,128)S(1)} %get-tuple-element.41.line_ref, f32[2,8,128]{2,1,0:T(8,128)S(1)} %get-tuple-element.42.after_bias_ref.slot_ref, ...), custom_call_target="tpu_custom_call" | custom-call | flops 900000000 | bytes 2000000 | tf_op jit(solution)/shard_map/weights/pallas_call | solution.py:540
  57.5 0.2 collective-permute-done.4.came5_ref
  57.7 1.3 %away.1 = (f32[16,8,640]{2,1,0:T(8,128)}, f32[32,512]{1,0:T(8,128)S(1)}) custom-call(s32[2]{0:T(128)S(1)} %pad_add_fusion.place_ref, f32[8,128]{1,0:T(8,128)S(1)} %get-tuple-element.59.w_ref, f32[128,512]{1,0:T(8,128)S(1)} %get-tuple-element.60.rows_ref, f32[256,512]{1,0:T(8,128)S(1)} %get-tuple-element.56.coarse_ref, ...), custom_call_target="tpu_custom_call" | custom-call | tf_op jit(solution)/shard_map/away/pallas_call | solution.py:550
  59.0 7.2 %all-to-all-start.2 = ((f32[16,8,640]{2,1,0:T(8,128)}), f32[16,8,640]{2,1,0:T(8,128)S(1)}, u32[]{:S(2)}, u32[]{:S(2)}) async-start(f32[16,8,640]{2,1,0:T(8,128)} %get-tuple-element.61), calls=%async_computation.2 | async-start | bytes 655360 | tf_op jit(solution)/shard_map/all_to_all | solution.py:436
  66.2 2.3 %collective-permute-start.6 = (f32[32,512]{1,0:T(8,128)S(1)}, f32[32,512]{1,0:T(8,128)S(1)}, u32[]{:S(2)}, u32[]{:S(2)}) collective-permute-start(f32[32,512]{1,0:T(8,128)S(1)} %get-tuple-element.73), channel_id=1, source_target_pairs={{0,4},{2,6},{4,0},{6,2},{8,12},{10,14},{12,8},{14,10},{16,20},{18,... | collective-permute-start | bytes 196616 | tf_op jit(solution)/shard_map/ppermute | solution.py:43
  68.5 2.2 %collective-permute-start.5 = (f32[32,512]{1,0:T(8,128)S(1)}, f32[32,512]{1,0:T(8,128)S(1)}, u32[]{:S(2)}, u32[]{:S(2)}) collective-permute-start(f32[32,512]{1,0:T(8,128)S(1)} %get-tuple-element.62), channel_id=1, source_target_pairs={{0,48},{2,50},{4,52},{6,54},{8,56},{10,58},{12,60},{14,62},{16,32}... | collective-permute-start | bytes 196616 | tf_op jit(solution)/shard_map/ppermute | solution.py:43
  70.7 2.4 %collective-permute-done.6.came1_ref = f32[32,512]{1,0:T(8,128)S(1)} collective-permute-done((f32[32,512]{1,0:T(8,128)S(1)}, f32[32,512]{1,0:T(8,128)S(1)}, u32[]{:S(2)}, u32[]{:S(2)}) %collective-permute-start.6) | collective-permute-done | bytes 65568 | tf_op jit(solution)/shard_map/ppermute | solution.py:43
  73.1 0.8 base.1
  73.9 1.3 %collective-permute-done.5.came4_ref = f32[32,512]{1,0:T(8,128)S(1)} collective-permute-done((f32[32,512]{1,0:T(8,128)S(1)}, f32[32,512]{1,0:T(8,128)S(1)}, u32[]{:S(2)}, u32[]{:S(2)}) %collective-permute-start.5) | collective-permute-done | bytes 65568 | tf_op jit(solution)/shard_map/ppermute | solution.py:43
  75.2 0.0 all-to-all-done.2.away_ref
  75.2 1.4 %return.1 = f32[16,8,640]{2,1,0:T(8,128)} custom-call(s32[2]{0:T(128)S(1)} %pad_add_fusion.place_ref, f32[16,8,640]{2,1,0:T(8,128)S(1)} %all-to-all-done.2.away_ref, f32[32,512]{1,0:T(8,128)S(1)} %collective-permute-done.5.came4_ref, f32[128,512]{1,0:T(8,128)S(1)} %get-tuple-element.63.base_ref), custom_call_target="tpu_custom_call" | custom-call | tf_op jit(solution)/shard_map/return/pallas_call | solution.py:570
  76.7 5.3 %all-to-all-start.3 = ((f32[16,8,640]{2,1,0:T(8,128)}), f32[16,8,640]{2,1,0:T(8,128)S(1)}, u32[]{:S(2)}, u32[]{:S(2)}) async-start(f32[16,8,640]{2,1,0:T(8,128)} %return.1), calls=%async_computation.3 | async-start | bytes 655360 | tf_op jit(solution)/shard_map/all_to_all | solution.py:436
  82.0 2.2 %collective-permute-start.7 = (f32[32,512]{1,0:T(8,128)S(1)}, f32[32,512]{1,0:T(8,128)S(1)}, u32[]{:S(2)}, u32[]{:S(2)}) collective-permute-start(f32[32,512]{1,0:T(8,128)S(1)} %get-tuple-element.65), channel_id=1, source_target_pairs={{0,2},{2,0},{4,6},{6,4},{8,10},{10,8},{12,14},{14,12},{16,18},{18,... | collective-permute-start | bytes 196616 | tf_op jit(solution)/shard_map/ppermute | solution.py:43
  84.2 3.3 %collective-permute-done.7.came0_ref = f32[32,512]{1,0:T(8,128)S(1)} collective-permute-done((f32[32,512]{1,0:T(8,128)S(1)}, f32[32,512]{1,0:T(8,128)S(1)}, u32[]{:S(2)}, u32[]{:S(2)}) %collective-permute-start.7) | collective-permute-done | bytes 65568 | tf_op jit(solution)/shard_map/ppermute | solution.py:43
  87.5 0.7 own.1.own_ref
  88.2 1.4 %all-to-all-done.3.near_ref = f32[16,8,640]{2,1,0:T(8,128)S(1)} async-done(((f32[16,8,640]{2,1,0:T(8,128)}), f32[16,8,640]{2,1,0:T(8,128)S(1)}, u32[]{:S(2)}, u32[]{:S(2)}) %all-to-all-start.3) | async-done | bytes 327712 | tf_op jit(solution)/shard_map/all_to_all | solution.py:436
  89.6 8.7 %collective-permute-start.8 = (f32[8,128]{1,0:T(8,128)S(1)}, f32[8,128]{1,0:T(8,128)S(1)}, u32[]{:S(2)}, u32[]{:S(2)}) collective-permute-start(f32[8,128]{1,0:T(8,128)S(1)} %add_reduce_fusion.mine_ref), channel_id=1, source_target_pairs={{0,1},{1,0},{2,3},{3,2},{4,5},{5,4},{6,7},{7,6},{8,9},{9,8},{10,11... | collective-permute-start | bytes 12296 | tf_op jit(solution)/shard_map/ppermute | solution.py:592
  98.3 0.8 final.1
  99.2 0.0 collective-permute-done.8.got_ref
  99.2 0.7 outputs.1
  (5 shorter events, 0.1 us)
Async XLA Ops:
  3.0 17.7 %all-to-all-start = ((f32[16,8,640]{2,1,0:T(8,128)}), f32[16,8,640]{2,1,0:T(8,128)S(1)}, u32[]{:S(2)}, u32[]{:S(2)}) async-start(f32[16,8,640]{2,1,0:T(8,128)} %get-tuple-element.43), calls=%async_computation | async-start | bytes 655360 | tf_op jit(solution)/shard_map/all_to_all | solution.py:436
  13.8 6.7 %collective-permute-start = (f32[32,512]{1,0:T(8,128)S(1)}, f32[32,512]{1,0:T(8,128)S(1)}, u32[]{:S(2)}, u32[]{:S(2)}) collective-permute-start(f32[32,512]{1,0:T(8,128)S(1)} %get-tuple-element.40.after_ref), channel_id=1, source_target_pairs={{0,2},{2,0},{4,6},{6,4},{8,10},{10,8},{12,14},{14,12},{16,18},{18,... | collective-permute-start | bytes 196616 | tf_op jit(solution)/shard_map/ppermute | solution.py:43
  21.6 26.6 %all-to-all-start.1 = ((f32[16,8,640]{2,1,0:T(8,128)}), f32[16,8,640]{2,1,0:T(8,128)S(1)}, u32[]{:S(2)}, u32[]{:S(2)}) async-start(f32[16,8,640]{2,1,0:T(8,128)} %get-tuple-element.45), calls=%async_computation.1 | async-start | bytes 655360 | tf_op jit(solution)/shard_map/all_to_all | solution.py:436
  36.8 8.1 %collective-permute-start.2 = (f32[32,640]{1,0:T(8,128)S(1)}, f32[32,640]{1,0:T(8,128)S(1)}, u32[]{:S(2)}, u32[]{:S(2)}) collective-permute-start(f32[32,640]{1,0:T(8,128)S(1)} %get-tuple-element.44.own_ref), channel_id=1, source_target_pairs={{0,48},{2,50},{4,52},{6,54},{8,56},{10,58},{12,60},{14,62},{16,32}... | collective-permute-start | bytes 245768 | tf_op jit(solution)/shard_map/ppermute | solution.py:43
  41.2 7.1 %collective-permute-start.1 = (f32[32,640]{1,0:T(8,128)S(1)}, f32[32,640]{1,0:T(8,128)S(1)}, u32[]{:S(2)}, u32[]{:S(2)}) collective-permute-start(f32[32,640]{1,0:T(8,128)S(1)} %pad.4), channel_id=1, source_target_pairs={{0,4},{2,6},{4,0},{6,2},{8,12},{10,14},{12,8},{14,10},{16,20},{18,... | collective-permute-start | bytes 245768 | tf_op jit(solution)/shard_map/ppermute | solution.py:43
  45.6 5.2 %collective-permute-start.3 = (f32[32,640]{1,0:T(8,128)S(1)}, f32[32,640]{1,0:T(8,128)S(1)}, u32[]{:S(2)}, u32[]{:S(2)}) collective-permute-start(f32[32,640]{1,0:T(8,128)S(1)} %merge.1.after_ref), channel_id=1, source_target_pairs={{0,64},{2,66},{4,68},{6,70},{8,72},{10,74},{12,76},{14,78},{16,80}... | collective-permute-start | bytes 245768 | tf_op jit(solution)/shard_map/ppermute | solution.py:43
  52.7 5.0 %collective-permute-start.4 = (f32[32,512]{1,0:T(8,128)S(1)}, f32[32,512]{1,0:T(8,128)S(1)}, u32[]{:S(2)}, u32[]{:S(2)}) collective-permute-start(f32[32,512]{1,0:T(8,128)S(1)} %get-tuple-element.74), channel_id=1, source_target_pairs={{0,64},{2,66},{4,68},{6,70},{8,72},{10,74},{12,76},{14,78},{16,80}... | collective-permute-start | bytes 196616 | tf_op jit(solution)/shard_map/ppermute | solution.py:43
  59.0 16.2 %all-to-all-start.2 = ((f32[16,8,640]{2,1,0:T(8,128)}), f32[16,8,640]{2,1,0:T(8,128)S(1)}, u32[]{:S(2)}, u32[]{:S(2)}) async-start(f32[16,8,640]{2,1,0:T(8,128)} %get-tuple-element.61), calls=%async_computation.2 | async-start | bytes 655360 | tf_op jit(solution)/shard_map/all_to_all | solution.py:436
  66.2 6.9 %collective-permute-start.6 = (f32[32,512]{1,0:T(8,128)S(1)}, f32[32,512]{1,0:T(8,128)S(1)}, u32[]{:S(2)}, u32[]{:S(2)}) collective-permute-start(f32[32,512]{1,0:T(8,128)S(1)} %get-tuple-element.73), channel_id=1, source_target_pairs={{0,4},{2,6},{4,0},{6,2},{8,12},{10,14},{12,8},{14,10},{16,20},{18,... | collective-permute-start | bytes 196616 | tf_op jit(solution)/shard_map/ppermute | solution.py:43
  68.5 6.7 %collective-permute-start.5 = (f32[32,512]{1,0:T(8,128)S(1)}, f32[32,512]{1,0:T(8,128)S(1)}, u32[]{:S(2)}, u32[]{:S(2)}) collective-permute-start(f32[32,512]{1,0:T(8,128)S(1)} %get-tuple-element.62), channel_id=1, source_target_pairs={{0,48},{2,50},{4,52},{6,54},{8,56},{10,58},{12,60},{14,62},{16,32}... | collective-permute-start | bytes 196616 | tf_op jit(solution)/shard_map/ppermute | solution.py:43
  76.7 12.9 %all-to-all-start.3 = ((f32[16,8,640]{2,1,0:T(8,128)}), f32[16,8,640]{2,1,0:T(8,128)S(1)}, u32[]{:S(2)}, u32[]{:S(2)}) async-start(f32[16,8,640]{2,1,0:T(8,128)} %return.1), calls=%async_computation.3 | async-start | bytes 655360 | tf_op jit(solution)/shard_map/all_to_all | solution.py:436
  82.0 5.5 %collective-permute-start.7 = (f32[32,512]{1,0:T(8,128)S(1)}, f32[32,512]{1,0:T(8,128)S(1)}, u32[]{:S(2)}, u32[]{:S(2)}) collective-permute-start(f32[32,512]{1,0:T(8,128)S(1)} %get-tuple-element.65), channel_id=1, source_target_pairs={{0,2},{2,0},{4,6},{6,4},{8,10},{10,8},{12,14},{14,12},{16,18},{18,... | collective-permute-start | bytes 196616 | tf_op jit(solution)/shard_map/ppermute | solution.py:43
  89.6 9.5 %collective-permute-start.8 = (f32[8,128]{1,0:T(8,128)S(1)}, f32[8,128]{1,0:T(8,128)S(1)}, u32[]{:S(2)}, u32[]{:S(2)}) collective-permute-start(f32[8,128]{1,0:T(8,128)S(1)} %add_reduce_fusion.mine_ref), channel_id=1, source_target_pairs={{0,1},{1,0},{2,3},{3,2},{4,5},{5,4},{6,7},{7,6},{8,9},{9,8},{10,11... | collective-permute-start | bytes 12296 | tf_op jit(solution)/shard_map/ppermute | solution.py:592

commit v8 on v7

--- a/solution.py
+++ b/solution.py
@@ -20,7 +20,7 @@
 UNROLL = 4
 CHUNK = 8
 SIDE = 16
-FIRST = {"low": 12, "high": 14, "away": 3, "near": 2}
+FIRST = {"low": 12, "high": 14, "away": 3, "near": 3}
 WIDTH = KV * D
 LEVEL_TOKENS = float(T * 2**LEVELS)
 SCALE = D ** (-0.5)
@@ -378,18 +378,19 @@
     return sum(ref[n] + ref[n + SIDE // 2] for n in range(SIDE // 2))
 
 
-def base_kernel(place_ref, came5_ref, came1_ref, coarse_ref, base_ref, send_ref):
-    ctx = place_ref[0]
-    parts = level_parts(ctx, 2, coarse_ref) + [(came5_ref[...], half_of(ctx, 4, 3))]
-    base_ref[...] = chosen(SIDE * CHUNK, parts)
-    send_ref[...] = sibling_rows(ctx, 0, coarse_ref, came1_ref)
-
-
-def return_kernel(place_ref, away_ref, came4_ref, base_ref, near_ref):
+def base_kernel(place_ref, away_ref, came5_ref, came1_ref, coarse_ref, base_ref, w_ref, send_ref):
     ctx = place_ref[0]
     away = summed(away_ref)
-    rows = base_ref[...] + chosen(SIDE * CHUNK, [(came4_ref[...], every(2)), (away[:, : 2 * WIDTH], every(4))])
-    fill(near_ref, lambda n: n ^ FIRST["near"] ^ (((ctx >> 4) & 1) * 8), rows, away[:, 2 * WIDTH :])
+    parts = level_parts(ctx, 2, coarse_ref) + [(came5_ref[...], half_of(ctx, 4, 3))]
+    base_ref[...] = chosen(SIDE * CHUNK, parts + [(away[:, : 2 * WIDTH], every(4))])
+    w_ref[...] = away[:, 2 * WIDTH :]
+    send_ref[...] = sibling_rows(ctx, 0, coarse_ref, came1_ref)
+
+
+def return_kernel(place_ref, w_ref, came4_ref, base_ref, near_ref):
+    ctx = place_ref[0]
+    rows = base_ref[...] + chosen(SIDE * CHUNK, [(came4_ref[...], every(2))])
+    fill(near_ref, lambda n: n ^ FIRST["near"] ^ (((ctx >> 4) & 1) * 8), rows, w_ref[...])
 
 
 def own_kernel(place_ref, own_ref, came1_ref, came0_ref, out_ref):
@@ -558,15 +559,15 @@
     away = swap_groups(away, high_groups(FIRST["away"]))
     came4 = exchange(send4, 4)
     came1 = exchange(coarse[COARSE : 2 * COARSE], 1)
-    base, send0 = pl.pallas_call(
+    base, w_away, send0 = pl.pallas_call(
         base_kernel,
-        out_shape=(shape((T, 2 * WIDTH), f32), rows),
-        in_specs=[SMEM] + [VMEM] * 3,
-        out_specs=(VMEM, VMEM),
+        out_shape=(shape((T, 2 * WIDTH), f32), shape((HEADS, D), f32), rows),
+        in_specs=[SMEM] + [VMEM] * 4,
+        out_specs=(VMEM,) * 3,
         compiler_params=SMALL,
         cost_estimate=pl.CostEstimate(flops=300_000_000, bytes_accessed=1_000_000, transcendentals=0),
         name="base",
-    )(place, came5, came1, coarse)
+    )(place, away, came5, came1, coarse)
     near = pl.pallas_call(
         return_kernel,
         out_shape=payload,
@@ -574,7 +575,7 @@
         out_specs=VMEM,
         compiler_params=SMALL,
         name="return",
-    )(place, away, came4, base)
+    )(place, w_away, came4, base)
     near = swap_groups(near, low_groups(FIRST["near"], 8))
     came0 = exchange(send0, 0)
     own_grad = pl.pallas_call(

time: 101 us -> 101 us (level)
    all_to_all x4, waiting for transfers between devices: 1.4 us -> 2.82 us  [swap_groups(): return lax.all_to_all(value, 'ctx', 0, 0, axis_index_groups=groups)]
    ppermute x8, waiting for transfers between devices: 9.58 us -> 8.22 us  [shifted(): lax.ppermute(value, 'ctx', [(i, i ^ mask) for i in range(lax.axis_size('c...]
where the time goes in v8:
time: 101 us; the launch traced here: 99.7 us
  starting transfers between devices  67.4 us (67%)
  Pallas kernels  19.4 us (19%)
  waiting for transfers between devices  11 us (11%)
  between operations  1.48 us (1%)
    all_to_all x4, starting transfers between devices, swap_groups(): return lax.all_to_all(value, 'ctx', 0, 0, axis_index_groups=groups)  38 us
    ppermute x8, starting transfers between devices, shifted(): lax.ppermute(value, 'ctx', [(i, i ^ mask) for i in range(lax.axis_size('c...  20.5 us
    ppermute x1, starting transfers between devices, shards(): w_other = lax.ppermute(w_all, 'mp', [(0, 1), (1, 0)])  8.93 us
    ppermute x8, waiting for transfers between devices, shifted(): lax.ppermute(value, 'ctx', [(i, i ^ mask) for i in range(lax.axis_size('c...  8.22 us
    pallas_call x1, Pallas kernels, shards(): pl.pallas_call(bias_kernel, out_shape=(shape((HEADS, T, KEYS), f32), shap...  4.38 us
    all_to_all x4, waiting for transfers between devices, swap_groups(): return lax.all_to_all(value, 'ctx', 0, 0, axis_index_groups=groups)  2.82 us
    pallas_call x1, Pallas kernels, shards(): pl.pallas_call(weight_kernel, out_shape=(shape((HEADS, D), f32), shape((T...  2.3 us
  transfers between devices with their start and end apart: 13, of which 8 were waited for; matrix products, arithmetic and copies ran while one was open for 0% of the time, Pallas kernels for 11%

profile of v8, /device:TPU:1, one launch (start us, length us, event | category | flops | bytes accessed | tf_op | source)
XLA Modules:
  0.0 99.7 jit_solution(9733132289362616939)
XLA Ops:
  1.3 1.8 %leaf.1 = (f32[32,512]{1,0:T(8,128)S(1)}, f32[16,8,640]{2,1,0:T(8,128)}) custom-call(s32[1]{0:T(128)S(6)} %copy.15.len_ref, bf16[128,256]{1,0:T(8,128)(2,1)} %k_hbm.3, bf16[128,256]{1,0:T(8,128)(2,1)} %v_hbm.3), custom_call_target="tpu_custom_call" | custom-call | tf_op jit(solution)/shard_map/leaf/pallas_call | solution.py:459
  3.0 10.7 %all-to-all-start = ((f32[16,8,640]{2,1,0:T(8,128)}), f32[16,8,640]{2,1,0:T(8,128)S(1)}, u32[]{:S(2)}, u32[]{:S(2)}) async-start(f32[16,8,640]{2,1,0:T(8,128)} %get-tuple-element.44), calls=%async_computation | async-start | bytes 655360 | tf_op jit(solution)/shard_map/all_to_all | solution.py:437
  13.8 2.2 %collective-permute-start = (f32[32,512]{1,0:T(8,128)S(1)}, f32[32,512]{1,0:T(8,128)S(1)}, u32[]{:S(2)}, u32[]{:S(2)}) collective-permute-start(f32[32,512]{1,0:T(8,128)S(1)} %get-tuple-element.41.after_ref), channel_id=1, source_target_pairs={{0,2},{2,0},{4,6},{6,4},{8,10},{10,8},{12,14},{14,12},{16,18},{18,... | collective-permute-start | bytes 196616 | tf_op jit(solution)/shard_map/ppermute | solution.py:43
  16.0 0.1 pad_add_fusion.place_ref
  16.0 4.4 %bias.1 = (f32[8,128,384]{2,1,0:T(8,128)S(1)}, f32[128,384]{1,0:T(8,128)S(1)}, f32[2,256,128]{2,1,0:T(8,128)S(1)}, f32[2,8,128]{2,1,0:T(8,128)S(1)}) custom-call(s32[2]{0:T(128)S(1)} %pad_add_fusion.place_ref, f32[1,32]{1,0:T(1,128)} %bitcast.15, f32[1,32]{1,0:T(1,128)} %bitcast.16, f32[16,32]{1,0:T(8,128)} %bitcast.13, ...), custom_call_target="tpu_custom_call" | custom-call | flops 600000000 | bytes 2000000 | tf_op jit(solution)/shard_map/bias/pallas_call | solution.py:472
  20.4 0.0 collective-permute-done.got0_ref
  20.5 0.1 reshape.37
  20.6 0.2 reduce_sum.18.after_merge_ref
  20.7 0.0 all-to-all-done
  20.7 0.9 middle.1
  21.6 15.2 %all-to-all-start.1 = ((f32[16,8,640]{2,1,0:T(8,128)}), f32[16,8,640]{2,1,0:T(8,128)S(1)}, u32[]{:S(2)}, u32[]{:S(2)}) async-start(f32[16,8,640]{2,1,0:T(8,128)} %get-tuple-element.46), calls=%async_computation.1 | async-start | bytes 655360 | tf_op jit(solution)/shard_map/all_to_all | solution.py:437
  36.8 4.3 %collective-permute-start.2 = (f32[32,640]{1,0:T(8,128)S(1)}, f32[32,640]{1,0:T(8,128)S(1)}, u32[]{:S(2)}, u32[]{:S(2)}) collective-permute-start(f32[32,640]{1,0:T(8,128)S(1)} %get-tuple-element.45.own_ref), channel_id=1, source_target_pairs={{0,48},{2,50},{4,52},{6,54},{8,56},{10,58},{12,60},{14,62},{16,32}... | collective-permute-start | bytes 245768 | tf_op jit(solution)/shard_map/ppermute | solution.py:43
  41.2 2.3 %collective-permute-start.1 = (f32[32,640]{1,0:T(8,128)S(1)}, f32[32,640]{1,0:T(8,128)S(1)}, u32[]{:S(2)}, u32[]{:S(2)}) collective-permute-start(f32[32,640]{1,0:T(8,128)S(1)} %pad.4), channel_id=1, source_target_pairs={{0,4},{2,6},{4,0},{6,2},{8,12},{10,14},{12,8},{14,10},{16,20},{18,... | collective-permute-start | bytes 245768 | tf_op jit(solution)/shard_map/ppermute | solution.py:43
  43.5 1.4 %collective-permute-done.2.got_ref.got4_ref = f32[32,640]{1,0:T(8,128)S(1)} collective-permute-done((f32[32,640]{1,0:T(8,128)S(1)}, f32[32,640]{1,0:T(8,128)S(1)}, u32[]{:S(2)}, u32[]{:S(2)}) %collective-permute-start.2) | collective-permute-done | bytes 81952 | tf_op jit(solution)/shard_map/ppermute | solution.py:43
  44.9 0.7 merge.1.after_ref
  45.6 2.5 %collective-permute-start.3 = (f32[32,640]{1,0:T(8,128)S(1)}, f32[32,640]{1,0:T(8,128)S(1)}, u32[]{:S(2)}, u32[]{:S(2)}) collective-permute-start(f32[32,640]{1,0:T(8,128)S(1)} %merge.1.after_ref), channel_id=1, source_target_pairs={{0,64},{2,66},{4,68},{6,70},{8,72},{10,74},{12,76},{14,78},{16,80}... | collective-permute-start | bytes 245768 | tf_op jit(solution)/shard_map/ppermute | solution.py:43
  48.1 0.2 collective-permute-done.1.got1_ref
  48.3 0.0 all-to-all-done.1
  48.3 1.8 %gather.1 = (bf16[128,1024]{1,0:T(8,128)(2,1)S(1)}, bf16[128,1024]{1,0:T(8,128)(2,1)S(1)}, bf16[384,256]{1,0:T(8,128)(2,1)S(1)}, bf16[384,256]{1,0:T(8,128)(2,1)S(1)}, f32[256,128]{1,0:T(8,128)S(1)}) custom-call(s32[2]{0:T(128)S(1)} %pad_add_fusion.place_ref, s32[1]{0:T(128)S(6)} %copy.15.len_ref, bf16[128,1024]{1,0:T(8,128)(2,1)} %q_hbm.1, ...), custom_call_target="tpu_custom_call" | custom-call | flops 300000000 | bytes 2000000 | tf_op jit(solution)/shard_map/gather/pallas_call | solution.py:514
  50.1 0.7 collective-permute-done.3.got5_ref
  50.8 1.9 %attention.1 = (bf16[128,1024]{1,0:T(8,128)(2,1)S(1)}, bf16[128,1024]{1,0:T(8,128)(2,1)S(1)}, f32[128,512]{1,0:T(8,128)S(1)}, f32[256,512]{1,0:T(8,128)S(1)}, f32[8,128,384]{2,1,0:T(8,128)S(1)}) custom-call(s32[1]{0:T(128)S(6)} %copy.15.len_ref, bf16[128,1024]{1,0:T(8,128)(2,1)S(1)} %get-tuple-element.47.q_ref, ...), custom_call_target="tpu_custom_call" | custom-call | tf_op jit(solution)/shard_map/attention/pallas_call | solution.py:525
  52.7 2.5 %collective-permute-start.4 = (f32[32,512]{1,0:T(8,128)S(1)}, f32[32,512]{1,0:T(8,128)S(1)}, u32[]{:S(2)}, u32[]{:S(2)}) collective-permute-start(f32[32,512]{1,0:T(8,128)S(1)} %get-tuple-element.76), channel_id=1, source_target_pairs={{0,64},{2,66},{4,68},{6,70},{8,72},{10,74},{12,76},{14,78},{16,80}... | collective-permute-start | bytes 196616 | tf_op jit(solution)/shard_map/ppermute | solution.py:43
  55.2 2.3 %weights.1 = (f32[8,128]{1,0:T(8,128)S(1)}, f32[128,512]{1,0:T(8,128)S(1)}, bf16[128,1024]{1,0:T(8,128)(2,1)}, bf16[128,1024]{1,0:T(8,128)(2,1)}) custom-call(s32[2]{0:T(128)S(1)} %pad_add_fusion.place_ref, f32[2,256,128]{2,1,0:T(8,128)S(1)} %get-tuple-element.42.line_ref, f32[2,8,128]{2,1,0:T(8,128)S(1)} %get-tuple-element.43.after_bias_ref.slot_ref, ...), custom_call_target="tpu_custom_call" | custom-call | flops 900000000 | bytes 2000000 | tf_op jit(solution)/shard_map/weights/pallas_call | solution.py:541
  57.5 0.2 collective-permute-done.4.came5_ref
  57.7 1.3 %away.1 = (f32[16,8,640]{2,1,0:T(8,128)}, f32[32,512]{1,0:T(8,128)S(1)}) custom-call(s32[2]{0:T(128)S(1)} %pad_add_fusion.place_ref, f32[8,128]{1,0:T(8,128)S(1)} %get-tuple-element.60.w_ref, f32[128,512]{1,0:T(8,128)S(1)} %get-tuple-element.61.rows_ref, f32[256,512]{1,0:T(8,128)S(1)} %get-tuple-element.57.coarse_ref, ...), custom_call_target="tpu_custom_call" | custom-call | tf_op jit(solution)/shard_map/away/pallas_call | solution.py:551
  59.0 7.2 %all-to-all-start.2 = ((f32[16,8,640]{2,1,0:T(8,128)}), f32[16,8,640]{2,1,0:T(8,128)S(1)}, u32[]{:S(2)}, u32[]{:S(2)}) async-start(f32[16,8,640]{2,1,0:T(8,128)} %get-tuple-element.62), calls=%async_computation.2 | async-start | bytes 655360 | tf_op jit(solution)/shard_map/all_to_all | solution.py:437
  66.2 2.3 %collective-permute-start.5 = (f32[32,512]{1,0:T(8,128)S(1)}, f32[32,512]{1,0:T(8,128)S(1)}, u32[]{:S(2)}, u32[]{:S(2)}) collective-permute-start(f32[32,512]{1,0:T(8,128)S(1)} %get-tuple-element.75), channel_id=1, source_target_pairs={{0,4},{2,6},{4,0},{6,2},{8,12},{10,14},{12,8},{14,10},{16,20},{18,... | collective-permute-start | bytes 196616 | tf_op jit(solution)/shard_map/ppermute | solution.py:43
  68.5 2.2 %collective-permute-start.6 = (f32[32,512]{1,0:T(8,128)S(1)}, f32[32,512]{1,0:T(8,128)S(1)}, u32[]{:S(2)}, u32[]{:S(2)}) collective-permute-start(f32[32,512]{1,0:T(8,128)S(1)} %get-tuple-element.64), channel_id=1, source_target_pairs={{0,48},{2,50},{4,52},{6,54},{8,56},{10,58},{12,60},{14,62},{16,32}... | collective-permute-start | bytes 196616 | tf_op jit(solution)/shard_map/ppermute | solution.py:43
  70.7 2.4 %collective-permute-done.5.came1_ref = f32[32,512]{1,0:T(8,128)S(1)} collective-permute-done((f32[32,512]{1,0:T(8,128)S(1)}, f32[32,512]{1,0:T(8,128)S(1)}, u32[]{:S(2)}, u32[]{:S(2)}) %collective-permute-start.5) | collective-permute-done | bytes 65568 | tf_op jit(solution)/shard_map/ppermute | solution.py:43
  73.1 1.8 %all-to-all-done.2.away_ref = f32[16,8,640]{2,1,0:T(8,128)S(1)} async-done(((f32[16,8,640]{2,1,0:T(8,128)}), f32[16,8,640]{2,1,0:T(8,128)S(1)}, u32[]{:S(2)}, u32[]{:S(2)}) %all-to-all-start.2) | async-done | bytes 327712 | tf_op jit(solution)/shard_map/all_to_all | solution.py:437
  75.0 0.8 base.1
  75.7 0.0 collective-permute-done.6.came4_ref
  75.7 1.4 %return.1 = f32[16,8,640]{2,1,0:T(8,128)} custom-call(s32[2]{0:T(128)S(1)} %pad_add_fusion.place_ref, f32[8,128]{1,0:T(8,128)S(1)} %get-tuple-element.63.w_ref, f32[32,512]{1,0:T(8,128)S(1)} %collective-permute-done.6.came4_ref, f32[128,512]{1,0:T(8,128)S(1)} %get-tuple-element.65.base_ref), custom_call_target="tpu_custom_call" | custom-call | tf_op jit(solution)/shard_map/return/pallas_call | solution.py:571
  77.2 4.9 %all-to-all-start.3 = ((f32[16,8,640]{2,1,0:T(8,128)}), f32[16,8,640]{2,1,0:T(8,128)S(1)}, u32[]{:S(2)}, u32[]{:S(2)}) async-start(f32[16,8,640]{2,1,0:T(8,128)} %return.1), calls=%async_computation.3 | async-start | bytes 655360 | tf_op jit(solution)/shard_map/all_to_all | solution.py:437
  82.1 2.2 %collective-permute-start.7 = (f32[32,512]{1,0:T(8,128)S(1)}, f32[32,512]{1,0:T(8,128)S(1)}, u32[]{:S(2)}, u32[]{:S(2)}) collective-permute-start(f32[32,512]{1,0:T(8,128)S(1)} %get-tuple-element.67), channel_id=1, source_target_pairs={{0,2},{2,0},{4,6},{6,4},{8,10},{10,8},{12,14},{14,12},{16,18},{18,... | collective-permute-start | bytes 196616 | tf_op jit(solution)/shard_map/ppermute | solution.py:43
  84.2 3.3 %collective-permute-done.7.came0_ref = f32[32,512]{1,0:T(8,128)S(1)} collective-permute-done((f32[32,512]{1,0:T(8,128)S(1)}, f32[32,512]{1,0:T(8,128)S(1)}, u32[]{:S(2)}, u32[]{:S(2)}) %collective-permute-start.7) | collective-permute-done | bytes 65568 | tf_op jit(solution)/shard_map/ppermute | solution.py:43
  87.5 0.7 own.1.own_ref
  88.2 1.0 all-to-all-done.3.near_ref
  89.2 8.9 %collective-permute-start.8 = (f32[8,128]{1,0:T(8,128)S(1)}, f32[8,128]{1,0:T(8,128)S(1)}, u32[]{:S(2)}, u32[]{:S(2)}) collective-permute-start(f32[8,128]{1,0:T(8,128)S(1)} %add_reduce_fusion.mine_ref), channel_id=1, source_target_pairs={{0,1},{1,0},{2,3},{3,2},{4,5},{5,4},{6,7},{7,6},{8,9},{9,8},{10,11... | collective-permute-start | bytes 12296 | tf_op jit(solution)/shard_map/ppermute | solution.py:593
  98.2 0.8 final.1
  99.0 0.0 collective-permute-done.8.got_ref
  99.0 0.7 outputs.1
  (5 shorter events, 0.1 us)
Async XLA Ops:
  3.0 17.7 %all-to-all-start = ((f32[16,8,640]{2,1,0:T(8,128)}), f32[16,8,640]{2,1,0:T(8,128)S(1)}, u32[]{:S(2)}, u32[]{:S(2)}) async-start(f32[16,8,640]{2,1,0:T(8,128)} %get-tuple-element.44), calls=%async_computation | async-start | bytes 655360 | tf_op jit(solution)/shard_map/all_to_all | solution.py:437
  13.8 6.7 %collective-permute-start = (f32[32,512]{1,0:T(8,128)S(1)}, f32[32,512]{1,0:T(8,128)S(1)}, u32[]{:S(2)}, u32[]{:S(2)}) collective-permute-start(f32[32,512]{1,0:T(8,128)S(1)} %get-tuple-element.41.after_ref), channel_id=1, source_target_pairs={{0,2},{2,0},{4,6},{6,4},{8,10},{10,8},{12,14},{14,12},{16,18},{18,... | collective-permute-start | bytes 196616 | tf_op jit(solution)/shard_map/ppermute | solution.py:43
  21.6 26.6 %all-to-all-start.1 = ((f32[16,8,640]{2,1,0:T(8,128)}), f32[16,8,640]{2,1,0:T(8,128)S(1)}, u32[]{:S(2)}, u32[]{:S(2)}) async-start(f32[16,8,640]{2,1,0:T(8,128)} %get-tuple-element.46), calls=%async_computation.1 | async-start | bytes 655360 | tf_op jit(solution)/shard_map/all_to_all | solution.py:437
  36.8 8.1 %collective-permute-start.2 = (f32[32,640]{1,0:T(8,128)S(1)}, f32[32,640]{1,0:T(8,128)S(1)}, u32[]{:S(2)}, u32[]{:S(2)}) collective-permute-start(f32[32,640]{1,0:T(8,128)S(1)} %get-tuple-element.45.own_ref), channel_id=1, source_target_pairs={{0,48},{2,50},{4,52},{6,54},{8,56},{10,58},{12,60},{14,62},{16,32}... | collective-permute-start | bytes 245768 | tf_op jit(solution)/shard_map/ppermute | solution.py:43
  41.2 7.1 %collective-permute-start.1 = (f32[32,640]{1,0:T(8,128)S(1)}, f32[32,640]{1,0:T(8,128)S(1)}, u32[]{:S(2)}, u32[]{:S(2)}) collective-permute-start(f32[32,640]{1,0:T(8,128)S(1)} %pad.4), channel_id=1, source_target_pairs={{0,4},{2,6},{4,0},{6,2},{8,12},{10,14},{12,8},{14,10},{16,20},{18,... | collective-permute-start | bytes 245768 | tf_op jit(solution)/shard_map/ppermute | solution.py:43
  45.6 5.2 %collective-permute-start.3 = (f32[32,640]{1,0:T(8,128)S(1)}, f32[32,640]{1,0:T(8,128)S(1)}, u32[]{:S(2)}, u32[]{:S(2)}) collective-permute-start(f32[32,640]{1,0:T(8,128)S(1)} %merge.1.after_ref), channel_id=1, source_target_pairs={{0,64},{2,66},{4,68},{6,70},{8,72},{10,74},{12,76},{14,78},{16,80}... | collective-permute-start | bytes 245768 | tf_op jit(solution)/shard_map/ppermute | solution.py:43
  52.7 5.0 %collective-permute-start.4 = (f32[32,512]{1,0:T(8,128)S(1)}, f32[32,512]{1,0:T(8,128)S(1)}, u32[]{:S(2)}, u32[]{:S(2)}) collective-permute-start(f32[32,512]{1,0:T(8,128)S(1)} %get-tuple-element.76), channel_id=1, source_target_pairs={{0,64},{2,66},{4,68},{6,70},{8,72},{10,74},{12,76},{14,78},{16,80}... | collective-permute-start | bytes 196616 | tf_op jit(solution)/shard_map/ppermute | solution.py:43
  59.0 16.0 %all-to-all-start.2 = ((f32[16,8,640]{2,1,0:T(8,128)}), f32[16,8,640]{2,1,0:T(8,128)S(1)}, u32[]{:S(2)}, u32[]{:S(2)}) async-start(f32[16,8,640]{2,1,0:T(8,128)} %get-tuple-element.62), calls=%async_computation.2 | async-start | bytes 655360 | tf_op jit(solution)/shard_map/all_to_all | solution.py:437
  66.2 6.9 %collective-permute-start.5 = (f32[32,512]{1,0:T(8,128)S(1)}, f32[32,512]{1,0:T(8,128)S(1)}, u32[]{:S(2)}, u32[]{:S(2)}) collective-permute-start(f32[32,512]{1,0:T(8,128)S(1)} %get-tuple-element.75), channel_id=1, source_target_pairs={{0,4},{2,6},{4,0},{6,2},{8,12},{10,14},{12,8},{14,10},{16,20},{18,... | collective-permute-start | bytes 196616 | tf_op jit(solution)/shard_map/ppermute | solution.py:43
  68.5 7.2 %collective-permute-start.6 = (f32[32,512]{1,0:T(8,128)S(1)}, f32[32,512]{1,0:T(8,128)S(1)}, u32[]{:S(2)}, u32[]{:S(2)}) collective-permute-start(f32[32,512]{1,0:T(8,128)S(1)} %get-tuple-element.64), channel_id=1, source_target_pairs={{0,48},{2,50},{4,52},{6,54},{8,56},{10,58},{12,60},{14,62},{16,32}... | collective-permute-start | bytes 196616 | tf_op jit(solution)/shard_map/ppermute | solution.py:43
  77.2 12.0 %all-to-all-start.3 = ((f32[16,8,640]{2,1,0:T(8,128)}), f32[16,8,640]{2,1,0:T(8,128)S(1)}, u32[]{:S(2)}, u32[]{:S(2)}) async-start(f32[16,8,640]{2,1,0:T(8,128)} %return.1), calls=%async_computation.3 | async-start | bytes 655360 | tf_op jit(solution)/shard_map/all_to_all | solution.py:437
  82.1 5.5 %collective-permute-start.7 = (f32[32,512]{1,0:T(8,128)S(1)}, f32[32,512]{1,0:T(8,128)S(1)}, u32[]{:S(2)}, u32[]{:S(2)}) collective-permute-start(f32[32,512]{1,0:T(8,128)S(1)} %get-tuple-element.67), channel_id=1, source_target_pairs={{0,2},{2,0},{4,6},{6,4},{8,10},{10,8},{12,14},{14,12},{16,18},{18,... | collective-permute-start | bytes 196616 | tf_op jit(solution)/shard_map/ppermute | solution.py:43
  89.2 9.8 %collective-permute-start.8 = (f32[8,128]{1,0:T(8,128)S(1)}, f32[8,128]{1,0:T(8,128)S(1)}, u32[]{:S(2)}, u32[]{:S(2)}) collective-permute-start(f32[8,128]{1,0:T(8,128)S(1)} %add_reduce_fusion.mine_ref), channel_id=1, source_target_pairs={{0,1},{1,0},{2,3},{3,2},{4,5},{5,4},{6,7},{7,6},{8,9},{9,8},{10,11... | collective-permute-start | bytes 12296 | tf_op jit(solution)/shard_map/ppermute | solution.py:593
